TPU v7x, 32 devices: a whole 2x2x4 slice. The times are simulated.
32 devices in a mesh: seg: 16 (over z, x, core), mlp: 2 (over y).
Axes of the slice: x: 2, y: 2, z: 4, core: 2. Of those that a mesh axis runs over, the one named last changes fastest.
Arguments:
- tokens: bfloat16 [32, 1024, 1024], P(('seg', 'mlp')), may hold values from -6 to 6
- initial_state: bfloat16 [32, 512, 1024], P(('seg', 'mlp')), may hold values from -6 to 6
- valid: int32 [32], P(('seg', 'mlp')), may hold values from 513 to 1024, as said below
- token_query_weight: bfloat16 [1024, 1024], P('seg'), may hold values from -0.1875 to 0.1875
- token_key_weight: bfloat16 [1024, 1024], P('seg'), may hold values from -0.1875 to 0.1875
- token_value_weight: bfloat16 [1024, 1024], P('seg'), may hold values from -0.1875 to 0.1875
- token_output_weight: bfloat16 [1024, 1024], P('seg'), may hold values from -3.5 to 3.5
- state_query_weight: bfloat16 [1024, 1024], P('seg'), may hold values from -0.1875 to 0.1875
- state_key_weight: bfloat16 [1024, 1024], P('seg'), may hold values from -0.1875 to 0.1875
- state_value_weight: bfloat16 [1024, 1024], P('seg'), may hold values from -0.1875 to 0.1875
- state_update_weight: bfloat16 [1024, 1024], P('seg'), may hold values from -2.5 to 2.5
- up_projection_weight: bfloat16 [1024, 4096], P('seg', 'mlp'), may hold values from -0.1875 to 0.1875
- down_projection_weight: bfloat16 [1024, 4096], P('seg', 'mlp'), may hold values from -0.09375 to 0.09375
- token_norm_gain: bfloat16 [1024], P('seg'), may hold values from 0.099609375 to 1.8984375
- state_norm_gain: bfloat16 [1024], P('seg'), may hold values from 0.099609375 to 1.8984375
- feedforward_norm_gain: bfloat16 [1024], P('seg'), may hold values from 0.099609375 to 1.8984375
- state_gate_bias: bfloat16 [1024], P('seg'), may hold values from -3 to 3
- output_cotangent: bfloat16 [32, 1024, 1024], P(('seg', 'mlp')), may hold values from -6 to 6
- final_state_cotangent: bfloat16 [32, 512, 1024], P(('seg', 'mlp')), may hold values from -6 to 6
Outputs:
- out: bfloat16 [32, 1024, 1024], P(('seg', 'mlp'))
- final_state: bfloat16 [32, 512, 1024], P(('seg', 'mlp'))
- grad_tokens: float32 [32, 1024, 1024], P(('seg', 'mlp'))
- grad_state: float32 [32, 512, 1024], P(('seg', 'mlp'))
- grad_w_query: float32 [1024, 1024], P('seg')
- grad_w_key: float32 [1024, 1024], P('seg')
- grad_w_value: float32 [1024, 1024], P('seg')
- grad_w_out: float32 [1024, 1024], P('seg')
- grad_w_squery: float32 [1024, 1024], P('seg')
- grad_w_skey: float32 [1024, 1024], P('seg')
- grad_w_svalue: float32 [1024, 1024], P('seg')
- grad_w_sout: float32 [1024, 1024], P('seg')
- grad_w_up: float32 [1024, 4096], P('seg', 'mlp')
- grad_w_down: float32 [1024, 4096], P('seg', 'mlp')
- grad_gain_attn: float32 [1024], P('seg')
- grad_gain_state: float32 [1024], P('seg')
- grad_gain_mlp: float32 [1024], P('seg')
- grad_gate_bias: float32 [1024], P('seg')
Inputs may be any that keep to these rules, and one draw needn't show every extreme that they name: More than 512 valid tokens in each segment, so only its last block has masked positions; in every draw some segment has all 1024 tokens valid.
All inputs are finite; a program needn't handle non-finite values.
Results may differ from a plain program's by a relative error of at most 0.022.
Values may be sent and summed in bfloat16 or wider, within the bound.
A program may use at most 448 MiB of HBM per device.

v0:
```python
import jax
import jax.numpy as jnp
from jax import lax
from jax.sharding import PartitionSpec as P

HEADS = 8
HEAD = 128
BLOCK = 512


EPS = 1e-06
NEGATIVE = -1e30
GELU_C = 0.7978845608
GELU_K = 0.044715


def rms_norm(values, gain):
    return values * lax.rsqrt(jnp.mean(values * values, axis=-1, keepdims=True) + EPS) * gain


def gelu_tanh(values):
    return 0.5 * values * (1.0 + jnp.tanh(GELU_C * (values + GELU_K * values * values * values)))


def matmul(left, right):
    return jnp.dot(left, right, preferred_element_type=jnp.float32)


def matmul_tn(left, right):
    return lax.dot_general(
        left, right, (((0,), (0,)), ((), ())), preferred_element_type=jnp.float32
    )


def matmul_nt(left, right):
    return lax.dot_general(
        left, right, (((1,), (1,)), ((), ())), preferred_element_type=jnp.float32
    )


def split_heads(values):
    return values.reshape(values.shape[0], HEADS, HEAD)


def score_block(query_rows, key_rows, allowed):
    scores = jnp.einsum(
        "qhd,khd->hqk",
        split_heads(query_rows),
        split_heads(key_rows),
        preferred_element_type=jnp.float32,
    ) * HEAD ** (-0.5)
    return jnp.where(allowed[None], scores, NEGATIVE)


def attend_forward(query_rows, key_rows, value_rows, allowed):
    scores = score_block(query_rows, key_rows, allowed)
    row_max = jnp.max(scores, axis=-1, keepdims=True)
    weights = jnp.exp(scores - row_max)
    row_total = jnp.sum(weights, axis=-1, keepdims=True)
    probs = (weights / row_total).astype(jnp.bfloat16)
    mixed_out = jnp.einsum(
        "hqk,khd->qhd", probs, split_heads(value_rows), preferred_element_type=jnp.float32
    )
    log_total = (row_max + jnp.log(row_total))[..., 0]
    return (mixed_out.reshape(query_rows.shape[0], -1).astype(jnp.bfloat16), log_total)


def attend_backward(query_rows, key_rows, value_rows, allowed, log_total, grad_mixed):
    score_scale = HEAD ** (-0.5)
    scores = score_block(query_rows, key_rows, allowed)
    probs = jnp.exp(scores - log_total[..., None])
    grad_heads = split_heads(grad_mixed)
    grad_values = jnp.einsum(
        "hqk,qhd->khd", probs.astype(jnp.bfloat16), grad_heads, preferred_element_type=jnp.float32
    )
    grad_probs = jnp.einsum(
        "qhd,khd->hqk", grad_heads, split_heads(value_rows), preferred_element_type=jnp.float32
    )
    grad_scores = (
        probs * (grad_probs - jnp.sum(grad_probs * probs, axis=-1, keepdims=True))
    ).astype(jnp.bfloat16)
    grad_query = (
        jnp.einsum(
            "hqk,khd->qhd", grad_scores, split_heads(key_rows), preferred_element_type=jnp.float32
        )
        * score_scale
    )
    grad_keys = (
        jnp.einsum(
            "hqk,qhd->khd", grad_scores, split_heads(query_rows), preferred_element_type=jnp.float32
        )
        * score_scale
    )
    query_count = query_rows.shape[0]
    key_count = key_rows.shape[0]
    return (
        grad_query.reshape(query_count, -1),
        grad_keys.reshape(key_count, -1),
        grad_values.reshape(key_count, -1),
    )


def shards(
    tokens,
    initial_state,
    valid,
    token_query_weight,
    token_key_weight,
    token_value_weight,
    token_output_weight,
    state_query_weight,
    state_key_weight,
    state_value_weight,
    state_update_weight,
    up_projection_weight,
    down_projection_weight,
    token_norm_gain,
    state_norm_gain,
    feedforward_norm_gain,
    state_gate_bias,
    output_cotangent,
    final_state_cotangent,
):
    (
        query_full,
        key_full,
        value_full,
        out_full,
        state_query_matrix,
        state_key_matrix,
        state_value_matrix,
        sout_full,
        up_part,
        down_part,
        attn_gain_b,
        state_gain_b,
        mlp_gain_b,
        bias_full,
    ) = (
        lax.all_gather(token_query_weight, "seg", axis=0, tiled=True),
        lax.all_gather(token_key_weight, "seg", axis=0, tiled=True),
        lax.all_gather(token_value_weight, "seg", axis=0, tiled=True),
        lax.all_gather(token_output_weight, "seg", axis=0, tiled=True),
        lax.all_gather(state_query_weight, "seg", axis=0, tiled=True),
        lax.all_gather(state_key_weight, "seg", axis=0, tiled=True),
        lax.all_gather(state_value_weight, "seg", axis=0, tiled=True),
        lax.all_gather(state_update_weight, "seg", axis=0, tiled=True),
        lax.all_gather(up_projection_weight, "seg", axis=0, tiled=True),
        lax.all_gather(down_projection_weight, "seg", axis=0, tiled=True),
        lax.all_gather(token_norm_gain, "seg", axis=0, tiled=True),
        lax.all_gather(state_norm_gain, "seg", axis=0, tiled=True),
        lax.all_gather(feedforward_norm_gain, "seg", axis=0, tiled=True),
        lax.all_gather(state_gate_bias, "seg", axis=0, tiled=True),
    )
    attn_gain = attn_gain_b.astype(jnp.float32)
    state_gain = state_gain_b.astype(jnp.float32)
    mlp_gain = mlp_gain_b.astype(jnp.float32)
    gate_open = 1.0 / (1.0 + jnp.exp(-bias_full.astype(jnp.float32)))
    token_proj = jnp.concatenate([query_full, key_full, value_full], axis=1)
    state_projection = jnp.concatenate(
        [state_query_matrix, state_key_matrix, state_value_matrix], axis=1
    )
    seg_tokens = tokens[0].astype(jnp.float32)
    seq_len = seg_tokens.shape[0]
    feature_width = seg_tokens.shape[1]
    block_count = seq_len // BLOCK
    state_rows = initial_state.shape[1]
    valid_count = valid[0]
    block_ids = jnp.arange(block_count, dtype=jnp.int32)
    zero_block = jnp.zeros((BLOCK, feature_width), jnp.bfloat16)

    def masks_for(block_index):
        row_ids = block_index * BLOCK + jnp.arange(BLOCK, dtype=jnp.int32)
        col_ids = jnp.concatenate([row_ids - BLOCK, row_ids])
        near_ok = (
            (col_ids[None, :] <= row_ids[:, None])
            & (col_ids[None, :] > row_ids[:, None] - BLOCK)
            & (col_ids[None, :] >= 0)
            & (col_ids[None, :] < valid_count)
        )
        allowed = jnp.concatenate([near_ok, jnp.ones((BLOCK, state_rows), dtype=jnp.bool_)], axis=1)
        seen = jnp.broadcast_to((row_ids < valid_count)[None, :], (state_rows, BLOCK))
        return (allowed, seen)

    def forward_step(state_carry, inputs):
        state_now, key_prev, value_prev = state_carry
        block_x, block_index = inputs
        allowed, seen = masks_for(block_index)
        normed = rms_norm(block_x, attn_gain).astype(jnp.bfloat16)
        token_qkv = matmul(normed, token_proj).astype(jnp.bfloat16)
        query_tok = token_qkv[:, :feature_width]
        key_tok = token_qkv[:, feature_width : 2 * feature_width]
        value_tok = token_qkv[:, 2 * feature_width :]
        normalized_state = rms_norm(state_now, state_gain).astype(jnp.bfloat16)
        state_qkv = matmul(normalized_state, state_projection).astype(jnp.bfloat16)
        key_all = jnp.concatenate(
            [key_prev, key_tok, state_qkv[:, feature_width : 2 * feature_width]], axis=0
        )
        value_all = jnp.concatenate(
            [value_prev, value_tok, state_qkv[:, 2 * feature_width :]], axis=0
        )
        mixed_out, log_total = attend_forward(query_tok, key_all, value_all, allowed)
        resid = block_x + matmul(mixed_out, out_full)
        state_read, state_log = attend_forward(
            state_qkv[:, :feature_width], key_tok, value_tok, seen
        )
        update = matmul(state_read, sout_full)
        next_state = gate_open * state_now + (1.0 - gate_open) * update
        kept_block = (
            normed,
            token_qkv,
            normalized_state,
            state_qkv,
            mixed_out,
            log_total,
            state_read,
            state_log,
            update,
            resid,
            state_now,
        )
        return ((next_state, key_tok, value_tok), kept_block)

    state_start = initial_state[0].astype(jnp.float32)
    (last_state, key_last, value_last), kept_all = lax.scan(
        forward_step,
        (state_start, zero_block, zero_block),
        (seg_tokens.reshape(block_count, BLOCK, feature_width), block_ids),
    )
    (
        normed_all,
        token_qkv_all,
        state_normed_all,
        state_qkv_all,
        mixed_all,
        log_all,
        read_all,
        read_log_all,
        update_all,
        resid_all,
        states_all,
    ) = kept_all
    resid_rows = resid_all.reshape(seq_len, feature_width)
    ynorm = rms_norm(resid_rows, mlp_gain).astype(jnp.bfloat16)
    rows_all = lax.all_gather(ynorm, "mlp", axis=0, tiled=True)
    up_act = matmul(rows_all, up_part)
    hidden = gelu_tanh(up_act).astype(jnp.bfloat16)
    branch_out = lax.psum_scatter(
        matmul_nt(hidden, down_part).astype(jnp.bfloat16), "mlp", scatter_dimension=0, tiled=True
    ).astype(jnp.float32)
    out_rows = resid_rows + branch_out
    keep_rows = (jnp.arange(seq_len, dtype=jnp.int32) < valid_count).astype(jnp.float32)[:, None]
    grad_out = output_cotangent[0].astype(jnp.float32) * keep_rows
    grad_branch = grad_out.astype(jnp.bfloat16)
    branch_all = lax.all_gather(grad_branch, "mlp", axis=0, tiled=True)
    grad_hidden = matmul(branch_all, down_part)
    grad_up = jax.vjp(gelu_tanh, up_act)[1](grad_hidden)[0].astype(jnp.bfloat16)
    down_grad_part = matmul_tn(branch_all, hidden)
    up_grad_part = matmul_tn(rows_all, grad_up)
    grad_ynorm = lax.psum_scatter(
        matmul_nt(grad_up, up_part).astype(jnp.bfloat16), "mlp", scatter_dimension=0, tiled=True
    ).astype(jnp.float32)
    grad_resid_norm, mlp_gain_grad = jax.vjp(rms_norm, resid_rows, mlp_gain)[1](grad_ynorm)
    grad_resid = grad_out + grad_resid_norm

    def backward_step(grad_carry, inputs):
        grad_state_next, grad_key_next, grad_value_next = grad_carry
        (
            block_index,
            prev_qkv,
            token_qkv,
            state_qkv,
            mixed_out,
            log_total,
            state_read,
            state_log,
            update,
            state_now,
            grad_block,
        ) = inputs
        allowed, seen = masks_for(block_index)
        query_tok = token_qkv[:, :feature_width]
        key_tok = token_qkv[:, feature_width : 2 * feature_width]
        value_tok = token_qkv[:, 2 * feature_width :]
        key_all = jnp.concatenate(
            [
                prev_qkv[:, feature_width : 2 * feature_width],
                key_tok,
                state_qkv[:, feature_width : 2 * feature_width],
            ],
            axis=0,
        )
        value_all = jnp.concatenate(
            [prev_qkv[:, 2 * feature_width :], value_tok, state_qkv[:, 2 * feature_width :]], axis=0
        )
        grad_update = (grad_state_next * (1.0 - gate_open)).astype(jnp.bfloat16)
        bias_term = (
            jnp.sum(grad_state_next * (state_now - update), axis=0) * gate_open * (1.0 - gate_open)
        )
        grad_read = matmul_nt(grad_update, sout_full).astype(jnp.bfloat16)
        grad_squery, grad_key_read, grad_value_read = attend_backward(
            state_qkv[:, :feature_width], key_tok, value_tok, seen, state_log, grad_read
        )
        grad_mix_in = grad_block.astype(jnp.bfloat16)
        grad_mixed = matmul_nt(grad_mix_in, out_full).astype(jnp.bfloat16)
        grad_query, grad_keys, grad_values = attend_backward(
            query_tok, key_all, value_all, allowed, log_total, grad_mixed
        )
        grad_key_tok = (grad_keys[BLOCK : 2 * BLOCK] + grad_key_read + grad_key_next).astype(
            jnp.bfloat16
        )
        grad_value_tok = (
            grad_values[BLOCK : 2 * BLOCK] + grad_value_read + grad_value_next
        ).astype(jnp.bfloat16)
        grad_token_qkv = jnp.concatenate(
            [grad_query.astype(jnp.bfloat16), grad_key_tok, grad_value_tok], axis=1
        )
        grad_state_qkv = jnp.concatenate(
            [grad_squery, grad_keys[2 * BLOCK :], grad_values[2 * BLOCK :]], axis=1
        ).astype(jnp.bfloat16)
        grad_state_normed = matmul_nt(grad_state_qkv, state_projection)
        grad_state_norm, state_gain_term = jax.vjp(rms_norm, state_now, state_gain)[1](
            grad_state_normed
        )
        grad_state_now = grad_state_next * gate_open + grad_state_norm
        carry_out = (grad_state_now, grad_keys[:BLOCK], grad_values[:BLOCK])
        return (
            carry_out,
            (grad_token_qkv, grad_state_qkv, grad_mix_in, grad_update, bias_term, state_gain_term),
        )

    prev_qkv_all = jnp.concatenate(
        [jnp.zeros((1, BLOCK, 3 * feature_width), jnp.bfloat16), token_qkv_all[:-1]], axis=0
    )
    zero_grad = jnp.zeros((BLOCK, feature_width), jnp.float32)
    (grad_state_start, unused_key, unused_value), grads_block = lax.scan(
        backward_step,
        (final_state_cotangent[0].astype(jnp.float32), zero_grad, zero_grad),
        (
            block_ids,
            prev_qkv_all,
            token_qkv_all,
            state_qkv_all,
            mixed_all,
            log_all,
            read_all,
            read_log_all,
            update_all,
            states_all,
            grad_resid.reshape(block_count, BLOCK, feature_width),
        ),
        reverse=True,
    )
    (
        grad_token_qkv_all,
        grad_state_qkv_all,
        grad_mix_all,
        grad_update_all,
        bias_terms,
        state_gain_terms,
    ) = grads_block
    grad_qkv_rows = grad_token_qkv_all.reshape(seq_len, 3 * feature_width)
    token_proj_grad = matmul_tn(normed_all.reshape(seq_len, feature_width), grad_qkv_rows)
    grad_normed = matmul_nt(grad_qkv_rows, token_proj)
    grad_tok_norm, attn_gain_grad = jax.vjp(rms_norm, seg_tokens, attn_gain)[1](grad_normed)
    grad_tokens = grad_resid + grad_tok_norm
    out_grad = matmul_tn(
        mixed_all.reshape(seq_len, feature_width), grad_mix_all.reshape(seq_len, feature_width)
    )
    state_total = block_count * state_rows
    state_projection_gradient = matmul_tn(
        state_normed_all.reshape(state_total, feature_width),
        grad_state_qkv_all.reshape(state_total, 3 * feature_width),
    )
    sout_grad = matmul_tn(
        read_all.reshape(state_total, feature_width),
        grad_update_all.reshape(state_total, feature_width),
    )
    bias_grad = jnp.sum(bias_terms, axis=0)
    state_gain_grad = jnp.sum(state_gain_terms, axis=0)
    query_grad = token_proj_grad[:, :feature_width]
    key_grad = token_proj_grad[:, feature_width : 2 * feature_width]
    value_grad = token_proj_grad[:, 2 * feature_width :]
    squery_grad = state_projection_gradient[:, :feature_width]
    state_key_gradient = state_projection_gradient[:, feature_width : 2 * feature_width]
    svalue_grad = state_projection_gradient[:, 2 * feature_width :]
    (
        query_grad,
        key_grad,
        value_grad,
        out_grad,
        squery_grad,
        state_key_gradient,
        svalue_grad,
        sout_grad,
        attn_gain_grad,
        state_gain_grad,
        mlp_gain_grad,
        bias_grad,
        up_grad_part,
        down_grad_part,
    ) = (
        lax.psum_scatter(
            query_grad.astype(jnp.bfloat16), "seg", scatter_dimension=0, tiled=True
        ).astype(jnp.float32),
        lax.psum_scatter(
            key_grad.astype(jnp.bfloat16), "seg", scatter_dimension=0, tiled=True
        ).astype(jnp.float32),
        lax.psum_scatter(
            value_grad.astype(jnp.bfloat16), "seg", scatter_dimension=0, tiled=True
        ).astype(jnp.float32),
        lax.psum_scatter(
            out_grad.astype(jnp.bfloat16), "seg", scatter_dimension=0, tiled=True
        ).astype(jnp.float32),
        lax.psum_scatter(
            squery_grad.astype(jnp.bfloat16), "seg", scatter_dimension=0, tiled=True
        ).astype(jnp.float32),
        lax.psum_scatter(
            state_key_gradient.astype(jnp.bfloat16), "seg", scatter_dimension=0, tiled=True
        ).astype(jnp.float32),
        lax.psum_scatter(
            svalue_grad.astype(jnp.bfloat16), "seg", scatter_dimension=0, tiled=True
        ).astype(jnp.float32),
        lax.psum_scatter(
            sout_grad.astype(jnp.bfloat16), "seg", scatter_dimension=0, tiled=True
        ).astype(jnp.float32),
        lax.psum_scatter(
            attn_gain_grad.astype(jnp.bfloat16), "seg", scatter_dimension=0, tiled=True
        ).astype(jnp.float32),
        lax.psum_scatter(
            state_gain_grad.astype(jnp.bfloat16), "seg", scatter_dimension=0, tiled=True
        ).astype(jnp.float32),
        lax.psum_scatter(
            mlp_gain_grad.astype(jnp.bfloat16), "seg", scatter_dimension=0, tiled=True
        ).astype(jnp.float32),
        lax.psum_scatter(
            bias_grad.astype(jnp.bfloat16), "seg", scatter_dimension=0, tiled=True
        ).astype(jnp.float32),
        lax.psum_scatter(
            up_grad_part.astype(jnp.bfloat16), "seg", scatter_dimension=0, tiled=True
        ).astype(jnp.float32),
        lax.psum_scatter(
            down_grad_part.astype(jnp.bfloat16), "seg", scatter_dimension=0, tiled=True
        ).astype(jnp.float32),
    )
    (
        query_grad,
        key_grad,
        value_grad,
        out_grad,
        squery_grad,
        state_key_gradient,
        svalue_grad,
        sout_grad,
        attn_gain_grad,
        state_gain_grad,
        mlp_gain_grad,
        bias_grad,
    ) = (
        lax.psum(query_grad.astype(jnp.bfloat16), "mlp").astype(jnp.float32),
        lax.psum(key_grad.astype(jnp.bfloat16), "mlp").astype(jnp.float32),
        lax.psum(value_grad.astype(jnp.bfloat16), "mlp").astype(jnp.float32),
        lax.psum(out_grad.astype(jnp.bfloat16), "mlp").astype(jnp.float32),
        lax.psum(squery_grad.astype(jnp.bfloat16), "mlp").astype(jnp.float32),
        lax.psum(state_key_gradient.astype(jnp.bfloat16), "mlp").astype(jnp.float32),
        lax.psum(svalue_grad.astype(jnp.bfloat16), "mlp").astype(jnp.float32),
        lax.psum(sout_grad.astype(jnp.bfloat16), "mlp").astype(jnp.float32),
        lax.psum(attn_gain_grad.astype(jnp.bfloat16), "mlp").astype(jnp.float32),
        lax.psum(state_gain_grad.astype(jnp.bfloat16), "mlp").astype(jnp.float32),
        lax.psum(mlp_gain_grad.astype(jnp.bfloat16), "mlp").astype(jnp.float32),
        lax.psum(bias_grad.astype(jnp.bfloat16), "mlp").astype(jnp.float32),
    )
    return (
        out_rows.astype(jnp.bfloat16)[None],
        last_state.astype(jnp.bfloat16)[None],
        grad_tokens[None],
        grad_state_start[None],
        query_grad,
        key_grad,
        value_grad,
        out_grad,
        squery_grad,
        state_key_gradient,
        svalue_grad,
        sout_grad,
        up_grad_part,
        down_grad_part,
        attn_gain_grad,
        state_gain_grad,
        mlp_gain_grad,
        bias_grad,
    )


def solution(mesh):
    return jax.shard_map(
        shards,
        mesh=mesh,
        in_specs=(
            P(("seg", "mlp"), None, None),
            P(("seg", "mlp"), None, None),
            P(("seg", "mlp")),
            P("seg", None),
            P("seg", None),
            P("seg", None),
            P("seg", None),
            P("seg", None),
            P("seg", None),
            P("seg", None),
            P("seg", None),
            P("seg", "mlp"),
            P("seg", "mlp"),
            P("seg"),
            P("seg"),
            P("seg"),
            P("seg"),
            P(("seg", "mlp"), None, None),
            P(("seg", "mlp"), None, None),
        ),
        out_specs=(
            P(("seg", "mlp"), None, None),
            P(("seg", "mlp"), None, None),
            P(("seg", "mlp"), None, None),
            P(("seg", "mlp"), None, None),
            P("seg", None),
            P("seg", None),
            P("seg", None),
            P("seg", None),
            P("seg", None),
            P("seg", None),
            P("seg", None),
            P("seg", None),
            P("seg", "mlp"),
            P("seg", "mlp"),
            P("seg"),
            P("seg"),
            P("seg"),
            P("seg"),
        ),
        check_vma=False,
    )
```

profile of v0, /device:TPU:0, one launch (start us, length us, event | category | flops | bytes accessed | tf_op | source)
XLA Modules:
  0.0 1753.6 jit_solution(10910735289349010931)
XLA Ops:
  21.5 35.8 %all-reduce.12 = (bf16[1024]{0:T(1024)(128)(2,1)S(1)}, bf16[1024]{0:T(1024)(128)(2,1)S(1)}, bf16[1024]{0:T(1024)(128)(2,1)S(1)}, bf16[1024]{0:T(1024)(128)(2,1)S(1)}) all-reduce(bf16[1024]{0:T(1024)(128)(2,1)S(1)} %dynamic-update-slice, bf16[1024]{0:T(1024)(128)(2,1)S(1)} %dynamic-update-slice.1, ...), channel_id=1, replica_groups=mesh['seg'=16,'mlp'=2] {'seg'}, use_global_device_ids=true, to_apply=%add.3 | all-reduce | flops 4096 | bytes 16384
  65.4 31.6 %all-gather.13.cloned.1.call-done = bf16[1024,1024]{1,0:T(8,128)(2,1)} async-done(((bf16[64,1024]{1,0:T(8,128)(2,1)}), bf16[1024,1024]{1,0:T(8,128)(2,1)}) %all-gather.13.cloned.1.call-update) | async-done | bytes 2097168 | tf_op jit(solution)/shard_map/all_gather | solution.py:140
  100.2 39.2 %all-gather.21.cloned.1.call-done = bf16[1024,1024]{1,0:T(8,128)(2,1)} async-done(((bf16[64,1024]{1,0:T(8,128)(2,1)}), bf16[1024,1024]{1,0:T(8,128)(2,1)}) %all-gather.21.cloned.1.call-update) | async-done | bytes 2097168 | tf_op jit(solution)/shard_map/all_gather | solution.py:145
  142.7 39.0 %all-gather.23.cloned.1.call-done = bf16[1024,1024]{1,0:T(8,128)(2,1)} async-done(((bf16[64,1024]{1,0:T(8,128)(2,1)}), bf16[1024,1024]{1,0:T(8,128)(2,1)}) %all-gather.23.cloned.1.call-update) | async-done | bytes 2097168 | tf_op jit(solution)/shard_map/all_gather | solution.py:146
  184.7 39.1 %all-gather.15.cloned.1.call-done = bf16[1024,1024]{1,0:T(8,128)(2,1)} async-done(((bf16[64,1024]{1,0:T(8,128)(2,1)}), bf16[1024,1024]{1,0:T(8,128)(2,1)}) %all-gather.15.cloned.1.call-update) | async-done | bytes 2097168 | tf_op jit(solution)/shard_map/all_gather | solution.py:141
  227.0 39.1 %all-gather.17.cloned.1.call-done = bf16[1024,1024]{1,0:T(8,128)(2,1)} async-done(((bf16[64,1024]{1,0:T(8,128)(2,1)}), bf16[1024,1024]{1,0:T(8,128)(2,1)}) %all-gather.17.cloned.1.call-update) | async-done | bytes 2097168 | tf_op jit(solution)/shard_map/all_gather | solution.py:142
  269.2 39.2 %all-gather.27.cloned.1.call-done = bf16[1024,1024]{1,0:T(8,128)(2,1)} async-done(((bf16[64,1024]{1,0:T(8,128)(2,1)}), bf16[1024,1024]{1,0:T(8,128)(2,1)}) %all-gather.27.cloned.1.call-update) | async-done | bytes 2097168 | tf_op jit(solution)/shard_map/all_gather | solution.py:143
  308.4 42.4 %all-gather.25.cloned.1.call-done = bf16[1024,1024]{1,0:T(8,128)(2,1)} async-done(((bf16[64,1024]{1,0:T(8,128)(2,1)}), bf16[1024,1024]{1,0:T(8,128)(2,1)}) %all-gather.25.cloned.1.call-update) | async-done | bytes 2097168 | tf_op jit(solution)/shard_map/all_gather | solution.py:147
  359.6 239.3 %while.70 = (s32[]{:T(128)}, f32[512,1024]{1,0:T(8,128)S(1)}, bf16[512,1024]{1,0:T(8,128)(2,1)}, bf16[512,1024]{1,0:T(8,128)(2,1)}, bf16[2,512,1024]{2,1,0:T(8,1...) while((s32[]{:T(128)}, f32[512,1024]{1,0:T(8,128)S(1)}, ...), condition=%wide.region_7.8_spmd, body=%wide.region_0.7_spmd.sunk | while | flops 13021742080 | bytes 366299872 | solution.py:225
  439.3 13.9 fusion.228
  454.2 12.0 fusion.229
  466.2 13.8 fusion.230
  493.5 8.7 convolution_convert_fusion.11
  550.8 13.9 fusion.228
  565.7 11.8 fusion.229
  577.5 13.6 fusion.230
  605.1 15.2 fusion.100
  620.2 40.5 %all-gather.29.cloned.1.call-done = bf16[2048,1024]{1,0:T(8,128)(2,1)} async-done(((bf16[1024,1024]{1,0:T(8,128)(2,1)}), bf16[2048,1024]{1,0:T(8,128)(2,1)}) %all-gather.29.cloned.1.call-update) | async-done | bytes 4194320 | tf_op jit(solution)/shard_map/all_gather | solution.py:245
  660.7 29.2 %fusion.74 = (bf16[2048,2048]{1,0:T(8,128)(2,1)S(1)}, f32[2048,2048]{1,0:T(8,128)}) fusion(f32[2048,2048]{1,0:T(8,128)} %fusion.100, bf16[2048,1024]{1,0:T(8,128)(2,1)} %all-gather.29.cloned.1.call-done, bf16[1024,2048]{1,0:T(8,128)(2,1)} %all-gather.31.cloned.1.call-done), kind=kOutput, calls=%fused_computation.153 | convolution fusion | flops 8690597888 | bytes 50331648 | tf_op jit(solution)/shard_map/dot_general | solution.py:26
  693.2 11.0 convolution_convert_fusion.6
  704.3 16.5 convolution_convert_fusion.7
  720.9 14.3 convolution_convert_fusion.5
  743.0 14.6 convolution_convert_fusion.4
  763.4 51.9 %reduce-scatter.13.cloned.1.call-done = bf16[1024,1024]{1,0:T(8,128)(2,1)} async-done(((bf16[2048,1024]{1,0:T(8,128)(2,1)}), bf16[1024,1024]{1,0:T(8,128)(2,1)}) %reduce-scatter.13.cloned.1.call-update) | async-done | bytes 2097168 | tf_op jit(solution)/shard_map/reduce_scatter | solution.py:248
  836.1 321.9 %while.71 = (s32[]{:T(128)}, f32[512,1024]{1,0:T(8,128)S(1)}, f32[512,1024]{0,1:T(8,128)}, f32[512,1024]{0,1:T(8,128)}, bf16[2,512,3072]{1,2,0:T(8,128)(2,1)}, /...) while((s32[]{:T(128)}, f32[512,1024]{1,0:T(8,128)S(1)}, ...), condition=%wide.region_19.20_spmd, body=%wide.region_12.19_spmd.sunk | while | flops 16263942144 | bytes 724355968 | solution.py:336
  884.8 12.1 subtract_exponential_fusion.5
  896.9 13.8 fusion.261
  919.2 18.8 %multiply_reduce_fusion.9 = (f32[8,512]{1,0:T(8,128)S(1)}, f32[8,512,1536]{2,1,0:T(8,128)}) fusion(f32[8,512,1536]{2,1,0:T(8,128)} %subtract_exponential_fusion.5, bf16[512,8,128]{0,2,1:T(8,128)(2,1)} %bitcast.452, bf16[1536,8,128]{0,2,1:T(8,128)(2,1)S(1)} %bitcast.448), kind=kOutput, calls=%fused_computation.69.clone.1 | convolution fusion | flops 1623191552 | bytes 54542336 | tf_op jit(solution)/shard_map/while/body/eval_jaxpr/qhd,khd->hqk/dot_general | solution.py:76
  937.9 22.1 %multiply_convert_fusion.19 = bf16[8,512,1536]{2,1,0:T(8,128)(2,1)} fusion(f32[8,512,1536]{2,1,0:T(8,128)} %subtract_exponential_fusion.5, f32[8,512,1536]{2,1,0:T(8,128)} %get-tuple-element.1783, f32[8,512]{1,0:T(8,128)S(1)} %get-tuple-element.1784), kind=kLoop, calls=%fused_computation.68.clone.1 | loop fusion | flops 18874368 | bytes 62930944 | tf_op jit(solution)/shard_map/while/body/eval_jaxpr/convert_element_type | solution.py:81
  960.0 10.0 multiply_convert_fusion.22
  1042.4 12.1 subtract_exponential_fusion.5
  1054.5 12.9 fusion.261
  1075.9 16.8 multiply_reduce_fusion.9
  1092.7 21.6 %multiply_convert_fusion.19 = bf16[8,512,1536]{2,1,0:T(8,128)(2,1)} fusion(f32[8,512,1536]{2,1,0:T(8,128)} %subtract_exponential_fusion.5, f32[8,512,1536]{2,1,0:T(8,128)} %get-tuple-element.1783, f32[8,512]{1,0:T(8,128)S(1)} %get-tuple-element.1784), kind=kLoop, calls=%fused_computation.68.clone.1 | loop fusion | flops 18874368 | bytes 62930944 | tf_op jit(solution)/shard_map/while/body/eval_jaxpr/convert_element_type | solution.py:81
  1114.3 9.8 multiply_convert_fusion.22
  1170.8 10.0 bitcast_convert_fusion
  1185.3 9.8 bitcast_convert_fusion.1
  1207.0 8.8 copy.122
  1215.8 10.3 reduce-scatter.31.cloned.1.call-done
  1226.1 64.7 %reduce-scatter.23.cloned.1.call-done = bf16[64,1024]{1,0:T(8,128)(2,1)} async-done(((bf16[1024,1024]{1,0:T(8,128)(2,1)}), bf16[64,1024]{1,0:T(8,128)(2,1)}) %reduce-scatter.23.cloned.1.call-update) | async-done | bytes 131088 | tf_op jit(solution)/shard_map/reduce_scatter | solution.py:412
  1290.8 64.4 %reduce-scatter.29.cloned.1.call-done = bf16[64,1024]{1,0:T(8,128)(2,1)} async-done(((bf16[1024,1024]{1,0:T(8,128)(2,1)}), bf16[64,1024]{1,0:T(8,128)(2,1)}) %reduce-scatter.29.cloned.1.call-update) | async-done | bytes 131088 | tf_op jit(solution)/shard_map/reduce_scatter | solution.py:421
  1355.2 64.7 %reduce-scatter.27.cloned.1.call-done = bf16[64,1024]{1,0:T(8,128)(2,1)} async-done(((bf16[1024,1024]{1,0:T(8,128)(2,1)}), bf16[64,1024]{1,0:T(8,128)(2,1)}) %reduce-scatter.27.cloned.1.call-update) | async-done | bytes 131088 | tf_op jit(solution)/shard_map/reduce_scatter | solution.py:418
  1419.8 64.4 %reduce-scatter.25.cloned.1.call-done = bf16[64,1024]{1,0:T(8,128)(2,1)} async-done(((bf16[1024,1024]{1,0:T(8,128)(2,1)}), bf16[64,1024]{1,0:T(8,128)(2,1)}) %reduce-scatter.25.cloned.1.call-update) | async-done | bytes 131088 | tf_op jit(solution)/shard_map/reduce_scatter | solution.py:415
  1484.2 65.3 %reduce-scatter.21.cloned.1.call-done = bf16[64,1024]{1,0:T(8,128)(2,1)} async-done(((bf16[1024,1024]{1,0:T(8,128)(2,1)}), bf16[64,1024]{1,0:T(8,128)(2,1)}) %reduce-scatter.21.cloned.1.call-update) | async-done | bytes 131088 | tf_op jit(solution)/shard_map/reduce_scatter | solution.py:409
  1549.6 64.3 %reduce-scatter.19.cloned.1.call-done = bf16[64,1024]{1,0:T(8,128)(2,1)} async-done(((bf16[1024,1024]{1,0:T(8,128)(2,1)}), bf16[64,1024]{1,0:T(8,128)(2,1)}) %reduce-scatter.19.cloned.1.call-update) | async-done | bytes 131088 | tf_op jit(solution)/shard_map/reduce_scatter | solution.py:406
  1613.9 64.7 %reduce-scatter.17.cloned.1.call-done = bf16[64,1024]{1,0:T(8,128)(2,1)} async-done(((bf16[1024,1024]{1,0:T(8,128)(2,1)}), bf16[64,1024]{1,0:T(8,128)(2,1)}) %reduce-scatter.17.cloned.1.call-update) | async-done | bytes 131088 | tf_op jit(solution)/shard_map/reduce_scatter | solution.py:403
  1678.6 12.5 fusion.88
  1691.1 30.0 %all-reduce.11 = (bf16[1024]{0:T(1024)(128)(2,1)S(1)}, bf16[1024]{0:T(1024)(128)(2,1)S(1)}, bf16[1024]{0:T(1024)(128)(2,1)S(1)}, bf16[1024]{0:T(1024)(128)(2,1)S(1)}) all-reduce(bf16[1024]{0:T(1024)(128)(2,1)S(1)} %get-tuple-element.1213, bf16[1024]{0:T(1024)(128)(2,1)S(1)} %reduce_sum.253, ...), channel_id=14, replica_groups=mesh['seg'=16,'mlp'=2] {'seg'}, use_global_device_ids=true, to_apply=%region_41.42.clone | all-reduce | flops 4096 | bytes 16384
  (574 shorter events, 437.0 us)
Async XLA Ops:
  7.2 11.5 copy-start.44
  7.2 55.0 %all-gather.19.cloned.1.call-start = ((), (), s32[]{:S(2)}) async-start(), calls=%async_computation.15 | async-start | bytes 2228224 | tf_op jit(solution)/shard_map/all_gather | solution.py:144
  7.9 89.1 %all-gather.13.cloned.1.call-start = ((), (), s32[]{:S(2)}) async-start(), calls=%async_computation.12 | async-start | bytes 2228224 | tf_op jit(solution)/shard_map/all_gather | solution.py:140
  8.7 130.7 %all-gather.21.cloned.1.call-start = ((), (), s32[]{:S(2)}) async-start(), calls=%async_computation.16 | async-start | bytes 2228224 | tf_op jit(solution)/shard_map/all_gather | solution.py:145
  9.4 172.2 %all-gather.23.cloned.1.call-start = ((), (), s32[]{:S(2)}) async-start(), calls=%async_computation.17 | async-start | bytes 2228224 | tf_op jit(solution)/shard_map/all_gather | solution.py:146
  10.0 213.9 %all-gather.15.cloned.1.call-start = ((), (), s32[]{:S(2)}) async-start(), calls=%async_computation.13 | async-start | bytes 2228224 | tf_op jit(solution)/shard_map/all_gather | solution.py:141
  10.6 255.5 %all-gather.17.cloned.1.call-start = ((), (), s32[]{:S(2)}) async-start(), calls=%async_computation.14 | async-start | bytes 2228224 | tf_op jit(solution)/shard_map/all_gather | solution.py:142
  11.2 297.3 %all-gather.27.cloned.1.call-start = ((), (), s32[]{:S(2)}) async-start(), calls=%async_computation.19 | async-start | bytes 2228224 | tf_op jit(solution)/shard_map/all_gather | solution.py:143
  11.9 338.9 %all-gather.25.cloned.1.call-start = ((), (), s32[]{:S(2)}) async-start(), calls=%async_computation.18 | async-start | bytes 2228224 | tf_op jit(solution)/shard_map/all_gather | solution.py:147
  12.7 592.4 %all-gather.35.cloned.1.call-start = ((), (), s32[]{:S(2)}) async-start(), calls=%async_computation.24 | async-start | bytes 6291456 | tf_op jit(solution)/shard_map/all_gather | solution.py:255
  17.3 587.7 %all-gather.33.cloned.1.call-start = ((), (), s32[]{:S(2)}) async-start(), calls=%async_computation.22 | async-start | bytes 4456448 | tf_op jit(solution)/shard_map/all_gather | solution.py:149
  17.9 602.3 %all-gather.31.cloned.1.call-start = ((), (), s32[]{:S(2)}) async-start(), calls=%async_computation.21 | async-start | bytes 4456448 | tf_op jit(solution)/shard_map/all_gather | solution.py:148
  18.6 642.0 %all-gather.29.cloned.1.call-start = ((), (), s32[]{:S(2)}) async-start(), calls=%async_computation.20 | async-start | bytes 6291456 | tf_op jit(solution)/shard_map/all_gather | solution.py:245
  454.2 12.0 copy-start.31
  565.7 11.9 copy-start.31
  605.0 153.7 %reduce-scatter.15.cloned.1.call-start = ((), (), s32[]{:S(2)}) async-start(), calls=%async_computation.25 | async-start | bytes 6291456 | tf_op jit(solution)/shard_map/reduce_scatter | solution.py:260
  660.7 32.5 %copy-start.71 = (bf16[1024,2048]{1,0:T(8,128)(2,1)S(1)}, bf16[1024,2048]{1,0:T(8,128)(2,1)}, u32[]{:S(2)}) copy-start(bf16[1024,2048]{1,0:T(8,128)(2,1)} %all-gather.31.cloned.1.call-done) | copy-start | bytes 12582916
  704.3 111.0 %reduce-scatter.13.cloned.1.call-start = ((), (), s32[]{:S(2)}) async-start(), calls=%async_computation.23 | async-start | bytes 6291456 | tf_op jit(solution)/shard_map/reduce_scatter | solution.py:248
  720.8 482.6 %reduce-scatter.33.cloned.1.call-start = ((), (), s32[]{:S(2)}) async-start(), calls=%async_computation.34 | async-start | bytes 4456448 | tf_op jit(solution)/shard_map/reduce_scatter | solution.py:439
  735.2 470.1 %reduce-scatter.35.cloned.1.call-start = ((), (), s32[]{:S(2)}) async-start(), calls=%async_computation.35 | async-start | bytes 4456448 | tf_op jit(solution)/shard_map/reduce_scatter | solution.py:442
  757.7 57.6 %copy-start.65 = (f32[1024]{0:T(1024)S(1)}, f32[1024]{0:T(1024)}, u32[]{:S(2)}) copy-start(f32[1024]{0:T(1024)} %copy-done.64) | copy-start | bytes 12292
  757.7 468.4 %reduce-scatter.31.cloned.1.call-start = ((), (), s32[]{:S(2)}) async-start(), calls=%async_computation.33 | async-start | bytes 2228224 | tf_op jit(solution)/shard_map/reduce_scatter | solution.py:424
  861.5 12.1 copy-start.14
  864.3 20.5 %copy-start.25 = (bf16[512,1024]{0,1:T(8,128)(2,1)}, bf16[512,1024]{0,1:T(8,128)(2,1)S(1)}, u32[]{:S(2)}) copy-start(bf16[512,1024]{0,1:T(8,128)(2,1)S(1)} %get-tuple-element.1774) | copy-start | bytes 3145732 | tf_op jit(solution)/shard_map/while
  865.8 19.0 %copy-start.5 = (bf16[1536,1024]{0,1:T(8,128)(2,1)}, bf16[1536,1024]{0,1:T(8,128)(2,1)S(1)}, u32[]{:S(2)}) copy-start(bf16[1536,1024]{0,1:T(8,128)(2,1)S(1)} %pad_maximum_fusion.7) | copy-start | bytes 9437188 | tf_op jit(solution)/shard_map/while
  884.8 12.1 copy-start.13
  937.9 22.1 %copy-start.6 = (bf16[1536,1024]{0,1:T(8,128)(2,1)S(1)}, bf16[1536,1024]{0,1:T(8,128)(2,1)}, u32[]{:S(2)}) copy-start(bf16[1536,1024]{0,1:T(8,128)(2,1)} %copy-done.5) | copy-start | bytes 9437188 | tf_op jit(solution)/shard_map/while
  960.0 10.0 copy-start.26
  970.0 11.3 slice-start.2
  979.8 9.6 copy-start.23
  1019.2 12.0 copy-start.14
  1022.0 20.4 %copy-start.25 = (bf16[512,1024]{0,1:T(8,128)(2,1)}, bf16[512,1024]{0,1:T(8,128)(2,1)S(1)}, u32[]{:S(2)}) copy-start(bf16[512,1024]{0,1:T(8,128)(2,1)S(1)} %get-tuple-element.1774) | copy-start | bytes 3145732 | tf_op jit(solution)/shard_map/while
  1023.4 19.0 %copy-start.5 = (bf16[1536,1024]{0,1:T(8,128)(2,1)}, bf16[1536,1024]{0,1:T(8,128)(2,1)S(1)}, u32[]{:S(2)}) copy-start(bf16[1536,1024]{0,1:T(8,128)(2,1)S(1)} %pad_maximum_fusion.7) | copy-start | bytes 9437188 | tf_op jit(solution)/shard_map/while
  1042.4 12.1 copy-start.13
  1092.7 21.6 %copy-start.6 = (bf16[1536,1024]{0,1:T(8,128)(2,1)S(1)}, bf16[1536,1024]{0,1:T(8,128)(2,1)}, u32[]{:S(2)}) copy-start(bf16[1536,1024]{0,1:T(8,128)(2,1)} %copy-done.5) | copy-start | bytes 9437188 | tf_op jit(solution)/shard_map/while
  1114.3 9.8 copy-start.26
  1124.1 11.3 slice-start.2
  1164.6 126.2 %reduce-scatter.23.cloned.1.call-start = ((), (), s32[]{:S(2)}) async-start(), calls=%async_computation.29 | async-start | bytes 2228224 | tf_op jit(solution)/shard_map/reduce_scatter | solution.py:412
  1170.8 184.4 %reduce-scatter.29.cloned.1.call-start = ((), (), s32[]{:S(2)}) async-start(), calls=%async_computation.32 | async-start | bytes 2228224 | tf_op jit(solution)/shard_map/reduce_scatter | solution.py:421
  1183.8 236.1 %reduce-scatter.27.cloned.1.call-start = ((), (), s32[]{:S(2)}) async-start(), calls=%async_computation.31 | async-start | bytes 2228224 | tf_op jit(solution)/shard_map/reduce_scatter | solution.py:418
  1184.4 299.9 %reduce-scatter.25.cloned.1.call-start = ((), (), s32[]{:S(2)}) async-start(), calls=%async_computation.30 | async-start | bytes 2228224 | tf_op jit(solution)/shard_map/reduce_scatter | solution.py:415
  1185.1 364.5 %reduce-scatter.21.cloned.1.call-start = ((), (), s32[]{:S(2)}) async-start(), calls=%async_computation.28 | async-start | bytes 2228224 | tf_op jit(solution)/shard_map/reduce_scatter | solution.py:409
  1198.0 415.9 %reduce-scatter.19.cloned.1.call-start = ((), (), s32[]{:S(2)}) async-start(), calls=%async_computation.27 | async-start | bytes 2228224 | tf_op jit(solution)/shard_map/reduce_scatter | solution.py:406
  1198.7 479.8 %reduce-scatter.17.cloned.1.call-start = ((), (), s32[]{:S(2)}) async-start(), calls=%async_computation.26 | async-start | bytes 2228224 | tf_op jit(solution)/shard_map/reduce_scatter | solution.py:403
  1199.3 534.5 %all-reduce.17.cloned.1.call-start = ((), (), s32[]{:S(2)}) async-start(), calls=%async_computation.36 | async-start | bytes 2097152 | tf_op jit(solution)/shard_map/psum | solution.py:460
  1207.0 471.5 %copy-start.43 = (bf16[1,1024,1024]{2,1,0:T(8,128)(2,1)S(1)}, bf16[1,1024,1024]{2,1,0:T(8,128)(2,1)}, u32[]{:S(2)}) copy-start(bf16[1,1024,1024]{2,1,0:T(8,128)(2,1)} %param.23) | copy-start | bytes 6291460
  1207.0 471.5 %copy-start.62 = (f32[1024]{0:T(1024)S(1)}, f32[1024]{0:T(1024)}, u32[]{:S(2)}) copy-start(f32[1024]{0:T(1024)} %copy-done.61) | copy-start | bytes 12292
  1678.6 12.5 copy-start.68
  (109 other events, 404.4 us)
Sparse Core Ops, SparseCore 0:
  10.2 44.3 all-gather.18
  56.7 40.2 all-gather.12
  99.2 40.1 all-gather.20
  141.4 40.1 all-gather.22
  183.6 40.1 all-gather.14
  225.9 40.1 all-gather.16
  268.2 40.1 all-gather.26
  310.6 40.1 all-gather.24
  352.9 55.5 all-gather.34
  410.5 50.7 all-gather.32
  463.4 49.0 all-gather.30
  605.1 55.5 all-gather.28
  704.4 54.2 reduce-scatter.14
  761.0 54.2 reduce-scatter.12
  819.0 72.4 reduce-scatter.32
  895.7 71.3 reduce-scatter.34
  1164.8 61.3 reduce-scatter.30
  1230.2 60.6 reduce-scatter.22
  1294.6 60.5 reduce-scatter.28
  1359.2 60.5 reduce-scatter.26
  1423.6 60.5 reduce-scatter.24
  1489.0 60.5 reduce-scatter.20
  1553.3 60.5 reduce-scatter.18
  1617.9 60.5 reduce-scatter.16
  1681.2 40.3 all-reduce.16
where the time goes:
time: 1760 us; the launch traced here: 1750 us
  waiting for transfers between devices  834 us (47%)
  matrix products  423 us (24%)
  local copies, waits for them, and re-layouts  199 us (11%)
  other arithmetic  178 us (10%)
  blocking collectives  70.8 us (4%)
  loops' own time  30 us (2%)
    dot_general x10, matrix products, matmul(): return jnp.dot(left, right, preferred_element_type=jnp.float32)  89.2 us
    unnamed x2, blocking collectives  65.9 us
    reduce_scatter x1, waiting for transfers between devices, shards(): lax.psum_scatter(value_grad.astype(jnp.bfloat16), 'seg', scatter_dimensio...  65.3 us
    reduce_scatter x1, waiting for transfers between devices, shards(): lax.psum_scatter(out_grad.astype(jnp.bfloat16), 'seg', scatter_dimension=...  64.7 us
    reduce_scatter x1, waiting for transfers between devices, shards(): lax.psum_scatter(state_key_gradient.astype(jnp.bfloat16), 'seg', scatter_...  64.7 us
    reduce_scatter x1, waiting for transfers between devices, shards(): lax.psum_scatter(query_grad.astype(jnp.bfloat16), 'seg', scatter_dimensio...  64.7 us
    reduce_scatter x1, waiting for transfers between devices, shards(): lax.psum_scatter(squery_grad.astype(jnp.bfloat16), 'seg', scatter_dimensi...  64.4 us
    reduce_scatter x1, waiting for transfers between devices, shards(): lax.psum_scatter(svalue_grad.astype(jnp.bfloat16), 'seg', scatter_dimensi...  64.4 us
  transfers between devices with their start and end apart: 25, of which 18 were waited for; matrix products, arithmetic and copies ran while one was open for 40% of the time, Pallas kernels for 0%

commit v1 on v0

--- a/solution.py
+++ b/solution.py
@@ -1,7 +1,368 @@
+import functools
 import jax
 import jax.numpy as jnp
 from jax import lax
+from jax.experimental import pallas as pl
+from jax.experimental.pallas import tpu as pltpu
 from jax.sharding import PartitionSpec as P
+
+MESH = pl.DeviceIdType.MESH
+
+
+class Place:
+    def __init__(self, seg_size, mlp_size):
+        seg = lax.axis_index("seg")
+        self.sizes = {"z": seg_size // 4, "x": 2, "c": 2, "m": mlp_size}
+        self.at = {
+            "z": lax.div(seg, 4),
+            "x": lax.rem(lax.div(seg, 2), 2),
+            "c": lax.rem(seg, 2),
+            "m": lax.axis_index("mlp"),
+        }
+
+    def device(self, **moved):
+        at = {**self.at, **moved}
+        return (at["z"] * 4 + at["x"] * 2 + at["c"], at["m"])
+
+    def ahead(self, axis, step):
+        return lax.rem(self.at[axis] + step, self.sizes[axis])
+
+    def behind(self, axis, step):
+        return lax.rem(self.at[axis] + self.sizes[axis] - step, self.sizes[axis])
+
+    def greet(self):
+        barrier = pltpu.get_barrier_semaphore()
+
+        def signal(**moved):
+            pl.semaphore_signal(
+                barrier, inc=1, device_id=self.device(**moved), device_id_type=MESH
+            )
+
+        z, last = self.at["z"], self.sizes["z"] - 1
+        count = 0
+        for axis in "xcm":
+            for step in range(1, self.sizes[axis]):
+                signal(**{axis: self.ahead(axis, step)})
+                count += 1
+
+        @pl.when(z > 0)
+        def _():
+            signal(z=z - 1)
+
+        @pl.when(z < last)
+        def _():
+            signal(z=z + 1)
+
+        count = count + lax.min(z, 1) + lax.min(last - z, 1)
+        pl.semaphore_wait(barrier, count)
+
+
+class Wires:
+    def __init__(self, place, send, recv):
+        self.place, self.send, self.recv, self.used = place, send, recv, 0
+
+    def copy(self, src, dst, pair, moved):
+        return pltpu.make_async_remote_copy(
+            src_ref=src,
+            dst_ref=dst,
+            send_sem=self.send.at[pair],
+            recv_sem=self.recv.at[pair],
+            device_id=self.place.device(**moved),
+            device_id_type=MESH,
+        )
+
+
+def guarded(condition, action):
+    if condition is None:
+        action()
+    else:
+        pl.when(condition)(action)
+
+
+class Flow:
+    def __init__(self, wires):
+        self.wires, self.arriving, self.sent = wires, [], []
+
+    def move(self, src, dst, moved, landing, goes=None, comes=None):
+        pair = self.wires.used
+        self.wires.used += 1
+        out = lambda: self.wires.copy(src, dst, pair, moved)
+        guarded(goes, lambda: out().start())
+        self.sent.append((goes, lambda: out().wait_send()))
+        self.arriving.append(
+            (comes, lambda: self.wires.copy(landing, landing, pair, moved).wait_recv())
+        )
+
+    def arrive(self):
+        for condition, wait in self.arriving:
+            guarded(condition, wait)
+        self.arriving.clear()
+
+    def finish(self):
+        self.arrive()
+        for condition, wait in self.sent:
+            guarded(condition, wait)
+        self.sent.clear()
+
+
+def gather(wires, source, target, order, local_sem):
+    place, flow = wires.place, Flow(wires)
+    axes = ("m" if len(target.shape) == 6 else "") + "zxc"
+    at, sizes, done = place.at, place.sizes, set()
+
+    def view(**moved):
+        index = [
+            moved[a] if a in moved else pl.ds(0, sizes[a]) if a in done else at[a] for a in axes
+        ]
+        return target.at[tuple(index)]
+
+    own = pltpu.make_async_copy(source, view(), local_sem)
+    own.start()
+    first = True
+    z, last = at["z"], sizes["z"] - 1
+    for axis in order + "c":
+        if axis == "z":
+            for t in range(last):
+                flow.arrive()
+                below, above = lax.max(z - t, 0), lax.min(z + t, last)
+                flow.move(
+                    source if first and t == 0 else view(z=below),
+                    view(z=below),
+                    dict(z=z + 1),
+                    view(z=lax.max(z - 1 - t, 0)),
+                    (z >= t) & (z < last),
+                    z >= t + 1,
+                )
+                flow.move(
+                    source if first and t == 0 else view(z=above),
+                    view(z=above),
+                    dict(z=z - 1),
+                    view(z=lax.min(z + 1 + t, last)),
+                    (z + t <= last) & (z > 0),
+                    z + 1 + t <= last,
+                )
+                yield
+        else:
+            flow.arrive()
+            for step in range(1, sizes[axis]):
+                flow.move(
+                    source if first else view(),
+                    view(),
+                    {axis: place.ahead(axis, step)},
+                    view(**{axis: place.behind(axis, step)}),
+                )
+            yield
+        done.add(axis)
+        if first:
+            own.wait()
+            first = False
+    flow.finish()
+
+
+def add_into(total, term, chunks):
+    def body(i, carry):
+        total[i] = (total[i].astype(jnp.float32) + term[i].astype(jnp.float32)).astype(total.dtype)
+        return carry
+
+    lax.fori_loop(0, chunks, body, 0)
+
+
+def flat_add(total, term):
+    lead = total.shape[:-2]
+    n = 1
+    for d in lead:
+        n *= d
+    def body(i, carry):
+        idx, rest = [], i
+        for d in reversed(lead):
+            idx.append(lax.rem(rest, d)); rest = lax.div(rest, d)
+        idx = tuple(reversed(idx))
+        total[idx] = (total[idx].astype(jnp.float32) + term[idx].astype(jnp.float32)).astype(total.dtype)
+        return carry
+    lax.fori_loop(0, n, body, 0)
+
+
+def scatter(wires, grad, result, own, core_in, m_in, x_in, up_in, down_in, order, local_sem):
+    place, flow = wires.place, Flow(wires)
+    split_m = len(grad.shape) == 6
+    axes = ("m" if split_m else "") + "zx"
+    at, sizes, done = place.at, place.sizes, set()
+    z, last = at["z"], sizes["z"] - 1
+    lead = (slice(None),) * len(axes)
+    full = tuple(pl.ds(0, sizes[a]) for a in axes)
+
+    def view(ref, **moved):
+        index = [
+            moved[a] if a in moved else at[a] if a in done else pl.ds(0, sizes[a]) for a in axes
+        ]
+        return ref.at[tuple(index)]
+
+    load = pltpu.make_async_copy(grad.at[full + (at["c"],)], own, local_sem)
+    load.start()
+    flow.move(grad.at[full + (1 - at["c"],)], core_in, dict(c=1 - at["c"]), core_in)
+    yield
+    load.wait()
+    flow.arrive()
+    flat_add(own, core_in)
+    for axis in order:
+        if axis == "x":
+            flow.move(view(own, x=1 - at["x"]), x_in, dict(x=1 - at["x"]), x_in)
+            yield
+            flow.arrive()
+            done.add("x")
+            flat_add(view(own), x_in)
+        elif axis == "m":
+            for step in range(1, sizes["m"]):
+                flow.move(
+                    view(own, m=place.ahead("m", step)), m_in.at[step - 1],
+                    dict(m=place.ahead("m", step)), m_in.at[step - 1],
+                )
+            yield
+            flow.arrive()
+            done.add("m")
+            for step in range(1, sizes["m"]):
+                flat_add(view(own), m_in.at[step - 1])
+        else:
+            for t in range(last):
+                up, down = lax.min(last - t + z, last), lax.max(z - last + t, 0)
+                flow.move(view(own, z=up), up_in.at[t], dict(z=z + 1), up_in.at[t],
+                          (z <= t) & (z < last), (z >= 1) & (z - 1 <= t))
+                flow.move(view(own, z=down), down_in.at[t], dict(z=z - 1), down_in.at[t],
+                          (last - z <= t) & (z > 0), (z < last) & (last - z - 1 <= t))
+                yield
+                flow.arrive()
+                up, down = lax.min(last - 1 - t + z, last), lax.max(z - last + t + 1, 0)
+                pl.when((z >= 1) & (z - 1 <= t))(lambda: flat_add(view(own, z=up), up_in.at[t]))
+                pl.when((z < last) & (last - z - 1 <= t))(lambda: flat_add(view(own, z=down), down_in.at[t]))
+            done.add("z")
+    if split_m:
+        result[...] = view(own)[...].astype(jnp.float32)
+    else:
+        slot = m_in.at[at["m"]]
+        slot[...] = view(own)[...]
+        for step in range(1, sizes["m"]):
+            flow.move(slot, slot, dict(m=place.ahead("m", step)), m_in.at[place.behind("m", step)])
+        yield
+        flow.arrive()
+        total = m_in[0].astype(jnp.float32)
+        for i in range(1, sizes["m"]):
+            total = total + m_in[i].astype(jnp.float32)
+        result[...] = total
+    flow.finish()
+
+
+def run_rounds(flows):
+    live, waiting = [], list(flows)
+    while live or waiting:
+        if waiting:
+            live.append(waiting.pop(0))
+        live = [f for f in live if next(f, StopIteration) is not StopIteration]
+
+
+def lead_shape(order, split_m, done, sizes):
+    axes = ("m" if split_m else "") + "zx"
+    return tuple(sizes[a] for a in axes if a not in done)
+
+
+def gather_call(sources, orders, seg_size, mlp_size, name, collective_id):
+    count = len(sources)
+    sizes = {"z": seg_size // 4, "x": 2, "c": 2, "m": mlp_size}
+
+    def kernel(*refs):
+        ins, outs = refs[:count], refs[count : 2 * count]
+        send, recv, local = refs[2 * count :]
+        place = Place(seg_size, mlp_size)
+        place.greet()
+        wires = Wires(place, send, recv)
+        run_rounds(
+            [gather(wires, ins[i], outs[i], orders[i], local.at[i]) for i in range(count)]
+        )
+
+    shapes = [
+        jax.ShapeDtypeStruct(
+            ((mlp_size,) if "m" in order else ()) + (sizes["z"], 2, 2) + source.shape, source.dtype
+        )
+        for source, order in zip(sources, orders)
+    ]
+    pairs = sum(2 * (sizes["z"] - 1) + 2 + ("m" in order) * (mlp_size - 1) for order in orders)
+    anywhere = pl.BlockSpec(memory_space=pl.ANY)
+    return pl.pallas_call(
+        kernel,
+        out_shape=shapes,
+        in_specs=[anywhere] * count,
+        out_specs=[anywhere] * count,
+        scratch_shapes=[
+            pltpu.SemaphoreType.DMA((pairs,)),
+            pltpu.SemaphoreType.DMA((pairs,)),
+            pltpu.SemaphoreType.DMA((count,)),
+        ],
+        compiler_params=pltpu.CompilerParams(collective_id=collective_id, has_side_effects=True),
+        name=name,
+    )(*sources)
+
+
+def scatter_buffers(grad, order, sizes):
+    split_m = grad.ndim == 6
+    rows = grad.shape[-2:]
+
+    def left(axis):
+        done = order[: order.index(axis) + 1]
+        return lead_shape(order, split_m, done, sizes) + rows
+
+    return [
+        pltpu.VMEM(shape, grad.dtype)
+        for shape in (
+            lead_shape(order, split_m, "", sizes) + rows,
+            lead_shape(order, split_m, "", sizes) + rows,
+            (sizes["m"] - 1,) + left("m") if split_m else (sizes["m"],) + rows,
+            left("x"),
+            (sizes["z"] - 1,) + left("z"),
+            (sizes["z"] - 1,) + left("z"),
+        )
+    ]
+
+
+def scatter_call(grads, orders, seg_size, mlp_size, name, collective_id):
+    count = len(grads)
+    sizes = {"z": seg_size // 4, "x": 2, "c": 2, "m": mlp_size}
+
+    def kernel(*refs):
+        ins, outs = refs[:count], refs[count : 2 * count]
+        buffers = refs[2 * count : -3]
+        send, recv, local = refs[-3:]
+        place = Place(seg_size, mlp_size)
+        place.greet()
+        wires = Wires(place, send, recv)
+        run_rounds(
+            [
+                scatter(
+                    wires, ins[i], outs[i], *buffers[6 * i : 6 * i + 6], orders[i], local.at[i]
+                )
+                for i in range(count)
+            ]
+        )
+
+    buffers = []
+    for grad, order in zip(grads, orders):
+        buffers += scatter_buffers(grad, order, sizes)
+    pairs = sum(2 * (sizes["z"] - 1) + 2 + (mlp_size - 1) for order in orders)
+    return pl.pallas_call(
+        kernel,
+        out_shape=[jax.ShapeDtypeStruct(grad.shape[-2:], jnp.float32) for grad in grads],
+        in_specs=[pl.BlockSpec(memory_space=pl.ANY)] * count,
+        out_specs=[pl.BlockSpec(memory_space=pltpu.VMEM)] * count,
+        scratch_shapes=buffers
+        + [
+            pltpu.SemaphoreType.DMA((pairs,)),
+            pltpu.SemaphoreType.DMA((pairs,)),
+            pltpu.SemaphoreType.DMA((count,)),
+        ],
+        compiler_params=pltpu.CompilerParams(
+            collective_id=collective_id, has_side_effects=True, vmem_limit_bytes=56 << 20
+        ),
+        name=name,
+    )(*grads)
+
 
 HEADS = 8
 HEAD = 128
@@ -101,6 +462,7 @@
 
 
 def shards(
+    mlp_size,
     tokens,
     initial_state,
     valid,
@@ -121,41 +483,58 @@
     output_cotangent,
     final_state_cotangent,
 ):
+    rows = token_query_weight.shape[0]
+    width = tokens.shape[2]
+    seg_size = width // rows
+    part = up_projection_weight.shape[1]
+    half = part // 2
+    small = jnp.concatenate(
+        [token_norm_gain, state_norm_gain, feedforward_norm_gain, state_gate_bias]
+    ).reshape(-1, 128)
+    small = jnp.pad(small, ((0, 16 - small.shape[0]), (0, 0)))
+    sources = [
+        token_query_weight,
+        token_key_weight,
+        token_value_weight,
+        small,
+        state_query_weight,
+        state_key_weight,
+        state_value_weight,
+        token_output_weight,
+        state_update_weight,
+        up_projection_weight[:, :half],
+        down_projection_weight[:, :half],
+        up_projection_weight[:, half:],
+        down_projection_weight[:, half:],
+    ]
+    gathered = gather_call(
+        sources, ["zx"] * 9 + ["zxm"] * 4, seg_size, mlp_size, "gather_weights", 1
+    )
     (
         query_full,
         key_full,
         value_full,
-        out_full,
+        small_all,
         state_query_matrix,
         state_key_matrix,
         state_value_matrix,
+        out_full,
         sout_full,
-        up_part,
-        down_part,
-        attn_gain_b,
-        state_gain_b,
-        mlp_gain_b,
-        bias_full,
-    ) = (
-        lax.all_gather(token_query_weight, "seg", axis=0, tiled=True),
-        lax.all_gather(token_key_weight, "seg", axis=0, tiled=True),
-        lax.all_gather(token_value_weight, "seg", axis=0, tiled=True),
-        lax.all_gather(token_output_weight, "seg", axis=0, tiled=True),
-        lax.all_gather(state_query_weight, "seg", axis=0, tiled=True),
-        lax.all_gather(state_key_weight, "seg", axis=0, tiled=True),
-        lax.all_gather(state_value_weight, "seg", axis=0, tiled=True),
-        lax.all_gather(state_update_weight, "seg", axis=0, tiled=True),
-        lax.all_gather(up_projection_weight, "seg", axis=0, tiled=True),
-        lax.all_gather(down_projection_weight, "seg", axis=0, tiled=True),
-        lax.all_gather(token_norm_gain, "seg", axis=0, tiled=True),
-        lax.all_gather(state_norm_gain, "seg", axis=0, tiled=True),
-        lax.all_gather(feedforward_norm_gain, "seg", axis=0, tiled=True),
-        lax.all_gather(state_gate_bias, "seg", axis=0, tiled=True),
-    )
-    attn_gain = attn_gain_b.astype(jnp.float32)
-    state_gain = state_gain_b.astype(jnp.float32)
-    mlp_gain = mlp_gain_b.astype(jnp.float32)
-    gate_open = 1.0 / (1.0 + jnp.exp(-bias_full.astype(jnp.float32)))
+    ) = gathered[:9]
+    query_full, key_full, value_full, out_full, sout_full = [
+        w.reshape(width, width) for w in (query_full, key_full, value_full, out_full, sout_full)
+    ]
+    state_query_matrix, state_key_matrix, state_value_matrix = [
+        w.reshape(width, width) for w in (state_query_matrix, state_key_matrix, state_value_matrix)
+    ]
+    ups, downs = [
+        [pair[m].reshape(width, half) for pair in pairs for m in range(mlp_size)]
+        for pairs in ((gathered[9], gathered[11]), (gathered[10], gathered[12]))
+    ]
+    small_rows = small_all.reshape(seg_size, -1)[:, : 4 * rows].reshape(seg_size, 4, rows)
+    small_rows = small_rows.transpose(1, 0, 2).reshape(4, width).astype(jnp.float32)
+    attn_gain, state_gain, mlp_gain, gate_bias = small_rows
+    gate_open = 1.0 / (1.0 + jnp.exp(-gate_bias))
     token_proj = jnp.concatenate([query_full, key_full, value_full], axis=1)
     state_projection = jnp.concatenate(
         [state_query_matrix, state_key_matrix, state_value_matrix], axis=1
@@ -242,24 +621,32 @@
     ) = kept_all
     resid_rows = resid_all.reshape(seq_len, feature_width)
     ynorm = rms_norm(resid_rows, mlp_gain).astype(jnp.bfloat16)
-    rows_all = lax.all_gather(ynorm, "mlp", axis=0, tiled=True)
-    up_act = matmul(rows_all, up_part)
-    hidden = gelu_tanh(up_act).astype(jnp.bfloat16)
-    branch_out = lax.psum_scatter(
-        matmul_nt(hidden, down_part).astype(jnp.bfloat16), "mlp", scatter_dimension=0, tiled=True
-    ).astype(jnp.float32)
-    out_rows = resid_rows + branch_out
     keep_rows = (jnp.arange(seq_len, dtype=jnp.int32) < valid_count).astype(jnp.float32)[:, None]
     grad_out = output_cotangent[0].astype(jnp.float32) * keep_rows
     grad_branch = grad_out.astype(jnp.bfloat16)
-    branch_all = lax.all_gather(grad_branch, "mlp", axis=0, tiled=True)
-    grad_hidden = matmul(branch_all, down_part)
-    grad_up = jax.vjp(gelu_tanh, up_act)[1](grad_hidden)[0].astype(jnp.bfloat16)
-    down_grad_part = matmul_tn(branch_all, hidden)
-    up_grad_part = matmul_tn(rows_all, grad_up)
-    grad_ynorm = lax.psum_scatter(
-        matmul_nt(grad_up, up_part).astype(jnp.bfloat16), "mlp", scatter_dimension=0, tiled=True
-    ).astype(jnp.float32)
+    out_rows = resid_rows
+    grad_ynorm = jnp.zeros_like(resid_rows)
+    up_grads, down_grads = [], []
+    for up_part, down_part in zip(ups, downs):
+        up_act = matmul(ynorm, up_part)
+        hidden = gelu_tanh(up_act).astype(jnp.bfloat16)
+        out_rows = out_rows + matmul_nt(hidden, down_part)
+        grad_hidden = matmul(grad_branch, down_part)
+        grad_up = jax.vjp(gelu_tanh, up_act)[1](grad_hidden)[0].astype(jnp.bfloat16)
+        down_grads.append(matmul_tn(grad_branch, hidden).astype(jnp.bfloat16))
+        up_grads.append(matmul_tn(ynorm, grad_up).astype(jnp.bfloat16))
+        grad_ynorm = grad_ynorm + matmul_nt(grad_up, up_part)
+    depth = seg_size // 4
+    forward_grads = [
+        jnp.stack(grads[start : start + mlp_size]).reshape(mlp_size, depth, 2, 2, rows, half)
+        for start in (0, mlp_size)
+        for grads in (up_grads, down_grads)
+    ]
+    up_left, down_left, up_right, down_right = scatter_call(
+        forward_grads, ["mxz"] * 4, seg_size, mlp_size, "scatter_forward", 2
+    )
+    up_grad_part = jnp.concatenate([up_left, up_right], axis=1)
+    down_grad_part = jnp.concatenate([down_left, down_right], axis=1)
     grad_resid_norm, mlp_gain_grad = jax.vjp(rms_norm, resid_rows, mlp_gain)[1](grad_ynorm)
     grad_resid = grad_out + grad_resid_norm
 
@@ -384,91 +771,45 @@
     squery_grad = state_projection_gradient[:, :feature_width]
     state_key_gradient = state_projection_gradient[:, feature_width : 2 * feature_width]
     svalue_grad = state_projection_gradient[:, 2 * feature_width :]
+    small_grads = jnp.stack([attn_gain_grad, state_gain_grad, mlp_gain_grad, bias_grad])
+    small_grads = small_grads.reshape(4, seg_size, rows).transpose(1, 0, 2)
+    small_grads = small_grads.reshape(seg_size, -1, 128)
+    small_lines = small_grads.shape[1]
+    small_grads = jnp.pad(small_grads, ((0, 0), (0, 8 - small_lines), (0, 0)))
+    summed = scatter_call(
+        [small_grads.reshape(depth, 2, 2, 8, 128)]
+        + [
+            grad.astype(jnp.bfloat16).reshape(depth, 2, 2, rows, width)
+            for grad in (
+                out_grad,
+                sout_grad,
+                squery_grad,
+                state_key_gradient,
+                svalue_grad,
+                query_grad,
+                key_grad,
+                value_grad,
+            )
+        ],
+        ["xz"] * 9,
+        seg_size,
+        mlp_size,
+        "scatter_rest",
+        3,
+    )
     (
+        small_sum,
+        out_grad,
+        sout_grad,
+        squery_grad,
+        state_key_gradient,
+        svalue_grad,
         query_grad,
         key_grad,
         value_grad,
-        out_grad,
-        squery_grad,
-        state_key_gradient,
-        svalue_grad,
-        sout_grad,
-        attn_gain_grad,
-        state_gain_grad,
-        mlp_gain_grad,
-        bias_grad,
-        up_grad_part,
-        down_grad_part,
-    ) = (
-        lax.psum_scatter(
-            query_grad.astype(jnp.bfloat16), "seg", scatter_dimension=0, tiled=True
-        ).astype(jnp.float32),
-        lax.psum_scatter(
-            key_grad.astype(jnp.bfloat16), "seg", scatter_dimension=0, tiled=True
-        ).astype(jnp.float32),
-        lax.psum_scatter(
-            value_grad.astype(jnp.bfloat16), "seg", scatter_dimension=0, tiled=True
-        ).astype(jnp.float32),
-        lax.psum_scatter(
-            out_grad.astype(jnp.bfloat16), "seg", scatter_dimension=0, tiled=True
-        ).astype(jnp.float32),
-        lax.psum_scatter(
-            squery_grad.astype(jnp.bfloat16), "seg", scatter_dimension=0, tiled=True
-        ).astype(jnp.float32),
-        lax.psum_scatter(
-            state_key_gradient.astype(jnp.bfloat16), "seg", scatter_dimension=0, tiled=True
-        ).astype(jnp.float32),
-        lax.psum_scatter(
-            svalue_grad.astype(jnp.bfloat16), "seg", scatter_dimension=0, tiled=True
-        ).astype(jnp.float32),
-        lax.psum_scatter(
-            sout_grad.astype(jnp.bfloat16), "seg", scatter_dimension=0, tiled=True
-        ).astype(jnp.float32),
-        lax.psum_scatter(
-            attn_gain_grad.astype(jnp.bfloat16), "seg", scatter_dimension=0, tiled=True
-        ).astype(jnp.float32),
-        lax.psum_scatter(
-            state_gain_grad.astype(jnp.bfloat16), "seg", scatter_dimension=0, tiled=True
-        ).astype(jnp.float32),
-        lax.psum_scatter(
-            mlp_gain_grad.astype(jnp.bfloat16), "seg", scatter_dimension=0, tiled=True
-        ).astype(jnp.float32),
-        lax.psum_scatter(
-            bias_grad.astype(jnp.bfloat16), "seg", scatter_dimension=0, tiled=True
-        ).astype(jnp.float32),
-        lax.psum_scatter(
-            up_grad_part.astype(jnp.bfloat16), "seg", scatter_dimension=0, tiled=True
-        ).astype(jnp.float32),
-        lax.psum_scatter(
-            down_grad_part.astype(jnp.bfloat16), "seg", scatter_dimension=0, tiled=True
-        ).astype(jnp.float32),
-    )
-    (
-        query_grad,
-        key_grad,
-        value_grad,
-        out_grad,
-        squery_grad,
-        state_key_gradient,
-        svalue_grad,
-        sout_grad,
-        attn_gain_grad,
-        state_gain_grad,
-        mlp_gain_grad,
-        bias_grad,
-    ) = (
-        lax.psum(query_grad.astype(jnp.bfloat16), "mlp").astype(jnp.float32),
-        lax.psum(key_grad.astype(jnp.bfloat16), "mlp").astype(jnp.float32),
-        lax.psum(value_grad.astype(jnp.bfloat16), "mlp").astype(jnp.float32),
-        lax.psum(out_grad.astype(jnp.bfloat16), "mlp").astype(jnp.float32),
-        lax.psum(squery_grad.astype(jnp.bfloat16), "mlp").astype(jnp.float32),
-        lax.psum(state_key_gradient.astype(jnp.bfloat16), "mlp").astype(jnp.float32),
-        lax.psum(svalue_grad.astype(jnp.bfloat16), "mlp").astype(jnp.float32),
-        lax.psum(sout_grad.astype(jnp.bfloat16), "mlp").astype(jnp.float32),
-        lax.psum(attn_gain_grad.astype(jnp.bfloat16), "mlp").astype(jnp.float32),
-        lax.psum(state_gain_grad.astype(jnp.bfloat16), "mlp").astype(jnp.float32),
-        lax.psum(mlp_gain_grad.astype(jnp.bfloat16), "mlp").astype(jnp.float32),
-        lax.psum(bias_grad.astype(jnp.bfloat16), "mlp").astype(jnp.float32),
+    ) = summed
+    attn_gain_grad, state_gain_grad, mlp_gain_grad, bias_grad = small_sum[:small_lines].reshape(
+        4, rows
     )
     return (
         out_rows.astype(jnp.bfloat16)[None],
@@ -494,7 +835,7 @@
 
 def solution(mesh):
     return jax.shard_map(
-        shards,
+        functools.partial(shards, mesh.shape["mlp"]),
         mesh=mesh,
         in_specs=(
             P(("seg", "mlp"), None, None),

time: 1760 us -> 1330 us (0.76)
  waiting for transfers between devices: 834 us -> 0 us
  Pallas kernels: 0 us -> 479 us
  blocking collectives: 70.8 us -> 0 us
  loops' own time: 30 us -> 59.4 us
  matrix products: 423 us -> 404 us
    reduce_scatter x12 -> x0, waiting for transfers between devices: 516 us -> none  [the longest x1 65.3 us: shards(): lax.psum_scatter(value_grad.astype(jnp.bfloat16), 'seg', scatter_dimensio...]
    pallas_call x0 -> x3, Pallas kernels: none -> 479 us  [the longest x2 255 us: scatter_call(): pl.pallas_call(kernel, out_shape=[jax.ShapeDtypeStruct(grad.shape[-2:], j...]
    all_gather x12 -> x0, waiting for transfers between devices: 310 us -> none  [the longest x1 42.4 us: shards(): lax.all_gather(state_update_weight, 'seg', axis=0, tiled=True)]
    unnamed x2 -> x0, blocking collectives: 65.9 us -> none
    convert_element_type x18 -> x1, other arithmetic: 22.5 us -> 0.01 us  [shards(): small_rows.transpose(1, 0, 2).reshape(4, width).astype(jnp.float32)]
    another operation x1, loops' own time: 11.5 us -> 31.4 us  [shards(): lax.scan(backward_step, (final_state_cotangent[0].astype(jnp.float32), ze...]
    dot_general x6 -> x12, matrix products: 61.3 us -> 49.4 us  [matmul_tn(): lax.dot_general(left, right, (((0,), (0,)), ((), ())), preferred_element_...]
    dot_general x10 -> x16, matrix products: 89.2 us -> 81.3 us  [matmul(): return jnp.dot(left, right, preferred_element_type=jnp.float32)]
  transfers between devices with their start and end apart: 25 -> 0, of which waited for: 18 -> 0; matrix products, arithmetic and copies ran while one was open for 40% -> 0% of each run, Pallas kernels for 0% -> 0%
where the time goes in v1:
time: 1330 us; the launch traced here: 1320 us
  Pallas kernels  479 us (36%)
  matrix products  404 us (30%)
  local copies, waits for them, and re-layouts  205 us (15%)
  other arithmetic  173 us (13%)
  loops' own time  59.4 us (4%)
    pallas_call x2, Pallas kernels, scatter_call(): pl.pallas_call(kernel, out_shape=[jax.ShapeDtypeStruct(grad.shape[-2:], j...  255 us
    pallas_call x1, Pallas kernels, gather_call(): pl.pallas_call(kernel, out_shape=shapes, in_specs=[anywhere] * count, out...  224 us
    dot_general x16, matrix products, matmul(): return jnp.dot(left, right, preferred_element_type=jnp.float32)  81.3 us
    dot_general x15, matrix products, matmul_nt(): lax.dot_general(left, right, (((1,), (1,)), ((), ())), preferred_element_...  67.9 us
    dot_general x8, matrix products, score_block(): jnp.einsum('qhd,khd->hqk', split_heads(query_rows), split_heads(key_rows)...  60.2 us
    dot_general x12, matrix products, matmul_tn(): lax.dot_general(left, right, (((0,), (0,)), ((), ())), preferred_element_...  49.4 us
    convert_element_type x4, other arithmetic, attend_backward(): grad_scores = (probs * (grad_probs - jnp.sum(grad_probs * probs, axis=-1,...  49.1 us
    while x204, local copies, waits for them, and re-layouts  45.2 us

profile of v1, /device:TPU:0, one launch (start us, length us, event | category | flops | bytes accessed | tf_op | source)
XLA Modules:
  0.0 1322.3 jit_solution(14579441681735977635)
XLA Ops:
  17.3 224.3 %gather_weights.1 = (bf16[4,2,2,64,1024]{4,3,2,1,0:T(8,128)(2,1)}, bf16[4,2,2,64,1024]{4,3,2,1,0:T(8,128)(2,1)}, bf16[4,2,2,64,1024]{4,3,2,1,0:T(8,128)(2,1)}, b...) custom-call(bf16[64,1024]{1,0:T(8,128)(2,1)} %refs_0_.1, ...), custom_call_target="tpu_custom_call" | custom-call | tf_op jit(solution)/shard_map/gather_weights/pallas_call | solution.py:289
  244.2 10.2 pad_maximum_fusion.3
  262.9 248.0 %while.70 = (s32[]{:T(128)}, f32[512,1024]{1,0:T(8,128)S(1)}, bf16[512,1024]{1,0:T(8,128)(2,1)}, bf16[512,1024]{1,0:T(8,128)(2,1)}, bf16[2,512,1024]{2,1,0:T(8,1...) while((s32[]{:T(128)}, f32[512,1024]{1,0:T(8,128)S(1)}, ...), condition=%wide.region_7.8_spmd, body=%wide.region_0.7_spmd.sunk | while | flops 13021742080 | bytes 366299872 | solution.py:604
  285.4 8.6 convolution_convert_fusion.15
  294.0 4.7 copy.169
  309.1 7.8 bitcast_dynamic-update-slice_fusion.13
  321.5 4.8 copy.170
  342.5 14.0 %fusion.312 = (f32[8,512]{1,0:T(8,128)S(1)}, f32[8,512,1536]{2,1,0:T(8,128)}) fusion(pred[512,1536]{1,0:T(8,128)(4,1)S(1)} %copy-done.29, bf16[64,8,8,128]{3,2,1,0:T(8,128)(2,1)S(1)} %copy-done.38, bf16[512,1024]{1,0:T(8,128)(2,1)S(1)} %copy-done.39, bf16[512,1024]{1,0:T(8,128)(2,1)S(1)} %copy-done.26, bf16[512,1024]{1,0:T(8,128)(2,1)S(1)} %copy-done.65), kind=kOutput, calls=%fused_computation.3.clone.1 | convolution fusion | flops 1638920192 | bytes 30162944 | tf_op jit(solution)/shard_map/while/body/eval_jaxpr/qhd,khd->hqk/dot_general | solution.py:407
  357.5 11.8 fusion.313
  369.4 13.5 %fusion.314 = bf16[8,128,512]{2,1,0:T(8,128)(2,1)} fusion(bf16[1536,8,128]{0,2,1:T(8,128)(2,1)} %bitcast.587, f32[8,512,1536]{2,1,0:T(8,128)} %get-tuple-element.1746, f32[8,512]{1,0:T(8,128)S(1)} %fusion.313, f32[8,512]{1,0:T(8,128)S(1)} %get-tuple-element.1747, pred[512,1536]{1,0:T(8,128)(4,1)S(1)} %copy-done.30), kind=kOutput, calls=%fused_computation.35.clone.1 | convolution fusion | flops 1642594304 | bytes 30179328 | tf_op jit(solution)/shard_map/while/body/eval_jaxpr/hqk,khd->qhd/dot_general | solution.py:422
  396.3 8.6 convolution_convert_fusion.15
  404.8 4.7 copy.169
  420.0 7.7 bitcast_dynamic-update-slice_fusion.13
  432.4 4.8 copy.170
  453.4 14.0 %fusion.312 = (f32[8,512]{1,0:T(8,128)S(1)}, f32[8,512,1536]{2,1,0:T(8,128)}) fusion(pred[512,1536]{1,0:T(8,128)(4,1)S(1)} %copy-done.29, bf16[64,8,8,128]{3,2,1,0:T(8,128)(2,1)S(1)} %copy-done.38, bf16[512,1024]{1,0:T(8,128)(2,1)S(1)} %copy-done.39, bf16[512,1024]{1,0:T(8,128)(2,1)S(1)} %copy-done.26, bf16[512,1024]{1,0:T(8,128)(2,1)S(1)} %copy-done.65), kind=kOutput, calls=%fused_computation.3.clone.1 | convolution fusion | flops 1638920192 | bytes 30162944 | tf_op jit(solution)/shard_map/while/body/eval_jaxpr/qhd,khd->hqk/dot_general | solution.py:407
  468.4 11.8 fusion.313
  480.2 13.5 %fusion.314 = bf16[8,128,512]{2,1,0:T(8,128)(2,1)} fusion(bf16[1536,8,128]{0,2,1:T(8,128)(2,1)} %bitcast.587, f32[8,512,1536]{2,1,0:T(8,128)} %get-tuple-element.1746, f32[8,512]{1,0:T(8,128)S(1)} %fusion.313, f32[8,512]{1,0:T(8,128)S(1)} %get-tuple-element.1747, pred[512,1536]{1,0:T(8,128)(4,1)S(1)} %copy-done.30), kind=kOutput, calls=%fused_computation.35.clone.1 | convolution fusion | flops 1642594304 | bytes 30179328 | tf_op jit(solution)/shard_map/while/body/eval_jaxpr/hqk,khd->qhd/dot_general | solution.py:422
  556.0 6.7 fusion.82
  565.3 6.8 fusion.78
  572.2 4.6 fusion.119
  576.7 6.7 fusion.90
  583.5 6.7 fusion.86
  590.2 4.6 fusion.121
  594.8 6.9 fusion.111
  610.8 5.1 multiply_reduce_fusion.3
  634.2 133.1 %scatter_forward.1 = (f32[64,1024]{1,0:T(8,128)}, f32[64,1024]{1,0:T(8,128)}, f32[64,1024]{1,0:T(8,128)}, f32[64,1024]{1,0:T(8,128)}) custom-call(bf16[2,4,2,2,64,1024]{5,4,3,2,1,0:T(8,128)(2,1)} %pad_maximum_fusion.5.refs_0_, bf16[2,4,2,2,64,1024]{5,4,3,2,1,0:T(8,128)(2,1)} %pad_maximum_fusion.6.refs_1_, ...), custom_call_target="tpu_custom_call" | custom-call | tf_op jit(solution)/shard_map/scatter_forward/pallas_call | solution.py:349
  788.2 337.3 %while.71 = (s32[]{:T(128)}, f32[512,1024]{1,0:T(8,128)S(1)}, f32[512,1024]{0,1:T(8,128)}, f32[512,1024]{0,1:T(8,128)}, bf16[2,512,3072]{1,2,0:T(8,128)(2,1)}, /...) while((s32[]{:T(128)}, f32[512,1024]{1,0:T(8,128)S(1)}, ...), condition=%wide.region_17.18_spmd, body=%wide.region_10.17_spmd.sunk | while | flops 16263942144 | bytes 724355968 | solution.py:723
  856.8 12.1 subtract_exponential_fusion.5
  868.9 12.9 fusion.345
  890.4 16.6 %multiply_reduce_fusion.10 = (f32[8,512]{1,0:T(8,128)S(1)}, f32[8,512,1536]{2,1,0:T(8,128)}) fusion(f32[8,512,1536]{2,1,0:T(8,128)} %subtract_exponential_fusion.5, bf16[512,8,128]{0,2,1:T(8,128)(2,1)} %bitcast.567, bf16[1536,8,128]{0,2,1:T(8,128)(2,1)S(1)} %bitcast.563), kind=kOutput, calls=%fused_computation.69.clone.1 | convolution fusion | flops 1623191552 | bytes 54542336 | tf_op jit(solution)/shard_map/while/body/eval_jaxpr/qhd,khd->hqk/dot_general | solution.py:437
  906.9 21.7 %multiply_convert_fusion.29 = bf16[8,512,1536]{2,1,0:T(8,128)(2,1)} fusion(f32[8,512,1536]{2,1,0:T(8,128)} %subtract_exponential_fusion.5, f32[8,512,1536]{2,1,0:T(8,128)} %get-tuple-element.1790, f32[8,512]{1,0:T(8,128)S(1)} %get-tuple-element.1791), kind=kLoop, calls=%fused_computation.68.clone.1 | loop fusion | flops 18874368 | bytes 62930944 | tf_op jit(solution)/shard_map/while/body/eval_jaxpr/convert_element_type | solution.py:442
  928.6 9.8 multiply_convert_fusion.32
  938.5 6.5 multiply_bitcast_fusion.2
  952.2 5.7 fusion.348
  1010.8 12.1 subtract_exponential_fusion.5
  1022.9 12.9 fusion.345
  1044.3 16.6 %multiply_reduce_fusion.10 = (f32[8,512]{1,0:T(8,128)S(1)}, f32[8,512,1536]{2,1,0:T(8,128)}) fusion(f32[8,512,1536]{2,1,0:T(8,128)} %subtract_exponential_fusion.5, bf16[512,8,128]{0,2,1:T(8,128)(2,1)} %bitcast.567, bf16[1536,8,128]{0,2,1:T(8,128)(2,1)S(1)} %bitcast.563), kind=kOutput, calls=%fused_computation.69.clone.1 | convolution fusion | flops 1623191552 | bytes 54542336 | tf_op jit(solution)/shard_map/while/body/eval_jaxpr/qhd,khd->hqk/dot_general | solution.py:437
  1060.9 21.7 %multiply_convert_fusion.29 = bf16[8,512,1536]{2,1,0:T(8,128)(2,1)} fusion(f32[8,512,1536]{2,1,0:T(8,128)} %subtract_exponential_fusion.5, f32[8,512,1536]{2,1,0:T(8,128)} %get-tuple-element.1790, f32[8,512]{1,0:T(8,128)S(1)} %get-tuple-element.1791), kind=kLoop, calls=%fused_computation.68.clone.1 | loop fusion | flops 18874368 | bytes 62930944 | tf_op jit(solution)/shard_map/while/body/eval_jaxpr/convert_element_type | solution.py:442
  1082.6 9.8 multiply_convert_fusion.32
  1092.4 6.5 multiply_bitcast_fusion.2
  1106.2 5.7 fusion.348
  1113.1 4.7 fusion.352
  1125.5 6.7 bitcast_convert_fusion.3
  1136.1 9.7 bitcast_convert_fusion.1
  1148.7 8.7 bitcast_convert_fusion
  1157.4 8.8 copy.92
  1166.3 11.7 fusion.104
  1186.0 121.4 %scatter_rest.1 = (f32[8,128]{1,0:T(8,128)}, f32[64,1024]{1,0:T(8,128)}, f32[64,1024]{1,0:T(8,128)}, f32[64,1024]{1,0:T(8,128)}, f32[64,1024]{1,0:T(8,128)}, /*i...) custom-call(f32[4,2,2,8,128]{4,3,2,1,0:T(8,128)} %bitcast.655, ...), custom_call_target="tpu_custom_call" | custom-call | tf_op jit(solution)/shard_map/scatter_rest/pallas_call | solution.py:349
  (572 shorter events, 371.9 us)
Async XLA Ops:
  0.7 12.4 copy-start.43
  0.7 10.9 copy-start.64
  7.5 9.8 copy-start.73
  357.5 11.9 copy-start.30
  468.4 11.9 copy-start.30
  517.1 5.7 copy-start.47
  524.3 13.9 %copy-start.57 = (bf16[1,4,2,2,64,1024]{5,4,3,2,1,0:T(8,128)(2,1)}, bf16[1,4,2,2,64,1024]{5,4,3,2,1,0:T(8,128)(2,1)S(1)}, u32[]{:S(2)}) copy-start(bf16[1,4,2,2,64,1024]{5,4,3,2,1,0:T(8,128)(2,1)S(1)} %get-tuple-element.1395) | copy-start | bytes 6291460
  524.3 16.2 %copy-start.59 = (bf16[1,4,2,2,64,1024]{5,4,3,2,1,0:T(8,128)(2,1)}, bf16[1,4,2,2,64,1024]{5,4,3,2,1,0:T(8,128)(2,1)S(1)}, u32[]{:S(2)}) copy-start(bf16[1,4,2,2,64,1024]{5,4,3,2,1,0:T(8,128)(2,1)S(1)} %get-tuple-element.1396) | copy-start | bytes 6291460
  540.6 5.5 copy-start.90
  556.0 6.7 copy-start.92
  576.7 6.7 copy-start.87
  594.8 7.0 copy-start.62
  809.7 9.1 copy-start.8
  833.7 12.0 copy-start.13
  836.4 20.4 %copy-start.24 = (bf16[512,1024]{0,1:T(8,128)(2,1)}, bf16[512,1024]{0,1:T(8,128)(2,1)S(1)}, u32[]{:S(2)}) copy-start(bf16[512,1024]{0,1:T(8,128)(2,1)S(1)} %get-tuple-element.1781) | copy-start | bytes 3145732 | tf_op jit(solution)/shard_map/while
  837.8 19.0 %copy-start.3 = (bf16[1536,1024]{0,1:T(8,128)(2,1)}, bf16[1536,1024]{0,1:T(8,128)(2,1)S(1)}, u32[]{:S(2)}) copy-start(bf16[1536,1024]{0,1:T(8,128)(2,1)S(1)} %pad_maximum_fusion.16) | copy-start | bytes 9437188 | tf_op jit(solution)/shard_map/while
  837.9 5.5 copy-start.52
  856.8 12.1 copy-start.12
  881.8 5.8 copy-start.2
  906.9 21.7 %copy-start.4 = (bf16[1536,1024]{0,1:T(8,128)(2,1)S(1)}, bf16[1536,1024]{0,1:T(8,128)(2,1)}, u32[]{:S(2)}) copy-start(bf16[1536,1024]{0,1:T(8,128)(2,1)} %copy-done.3) | copy-start | bytes 9437188 | tf_op jit(solution)/shard_map/while
  928.6 9.8 copy-start.25
  938.4 6.6 copy-start.1
  938.4 6.6 copy-start.14
  938.4 11.4 slice-start.8
  948.3 9.6 copy-start.22
  963.7 9.1 copy-start.8
  987.7 12.0 copy-start.13
  990.4 20.4 %copy-start.24 = (bf16[512,1024]{0,1:T(8,128)(2,1)}, bf16[512,1024]{0,1:T(8,128)(2,1)S(1)}, u32[]{:S(2)}) copy-start(bf16[512,1024]{0,1:T(8,128)(2,1)S(1)} %get-tuple-element.1781) | copy-start | bytes 3145732 | tf_op jit(solution)/shard_map/while
  991.8 19.0 %copy-start.3 = (bf16[1536,1024]{0,1:T(8,128)(2,1)}, bf16[1536,1024]{0,1:T(8,128)(2,1)S(1)}, u32[]{:S(2)}) copy-start(bf16[1536,1024]{0,1:T(8,128)(2,1)S(1)} %pad_maximum_fusion.16) | copy-start | bytes 9437188 | tf_op jit(solution)/shard_map/while
  991.8 5.5 copy-start.52
  1010.8 12.1 copy-start.12
  1035.8 5.8 copy-start.2
  1060.9 21.7 %copy-start.4 = (bf16[1536,1024]{0,1:T(8,128)(2,1)S(1)}, bf16[1536,1024]{0,1:T(8,128)(2,1)}, u32[]{:S(2)}) copy-start(bf16[1536,1024]{0,1:T(8,128)(2,1)} %copy-done.3) | copy-start | bytes 9437188 | tf_op jit(solution)/shard_map/while
  1082.6 9.8 copy-start.25
  1092.4 6.6 copy-start.1
  1092.4 6.6 copy-start.14
  1092.4 11.4 slice-start.8
  1102.3 9.6 copy-start.22
  1125.5 6.7 copy-start.11
  1125.5 6.7 copy-start.54
  1125.5 6.7 copy-start.84
  1132.2 16.4 %slice-start.4 = ((s8[6291456]{0:T(1024)(128)(4,1)}), s8[2097152]{0:T(1024)(128)(4,1)S(1)}, s32[]{:S(2)}) async-start(s8[6291456]{0:T(1024)(128)(4,1)} %bitcast.597), calls=%async_computation.4 | async-start | bytes 4194304
  1136.1 12.6 slice-start.5
  1157.4 8.8 copy-start.42
  1157.4 8.8 copy-start.80
  1157.4 8.8 copy-start.81
  1166.2 11.7 copy-start.74
  1166.2 11.7 copy-start.35
  (109 other events, 345.4 us)

commit v2 on v1

v2 whole, which is shorter than its diff:
```python
import functools
import jax
import jax.numpy as jnp
from jax import lax
from jax.experimental import pallas as pl
from jax.experimental.pallas import tpu as pltpu
from jax.sharding import PartitionSpec as P

MESH = pl.DeviceIdType.MESH


class Place:
    def __init__(self, seg_size, mlp_size):
        seg = lax.axis_index("seg")
        self.sizes = {"z": seg_size // 4, "x": 2, "c": 2, "m": mlp_size}
        self.at = {
            "z": lax.div(seg, 4),
            "x": lax.rem(lax.div(seg, 2), 2),
            "c": lax.rem(seg, 2),
            "m": lax.axis_index("mlp"),
        }

    def device(self, **moved):
        at = {**self.at, **moved}
        return (at["z"] * 4 + at["x"] * 2 + at["c"], at["m"])

    def ahead(self, axis, step):
        return lax.rem(self.at[axis] + step, self.sizes[axis])

    def behind(self, axis, step):
        return lax.rem(self.at[axis] + self.sizes[axis] - step, self.sizes[axis])

    def greet(self):
        barrier = pltpu.get_barrier_semaphore()

        def signal(**moved):
            pl.semaphore_signal(
                barrier, inc=1, device_id=self.device(**moved), device_id_type=MESH
            )

        z, last = self.at["z"], self.sizes["z"] - 1
        count = 0
        for axis in "xcm":
            for step in range(1, self.sizes[axis]):
                signal(**{axis: self.ahead(axis, step)})
                count += 1

        @pl.when(z > 0)
        def _():
            signal(z=z - 1)

        @pl.when(z < last)
        def _():
            signal(z=z + 1)

        count = count + lax.min(z, 1) + lax.min(last - z, 1)
        pl.semaphore_wait(barrier, count)


class Wires:
    def __init__(self, place, send, recv):
        self.place, self.send, self.recv, self.used = place, send, recv, 0

    def copy(self, src, dst, pair, moved):
        return pltpu.make_async_remote_copy(
            src_ref=src,
            dst_ref=dst,
            send_sem=self.send.at[pair],
            recv_sem=self.recv.at[pair],
            device_id=self.place.device(**moved),
            device_id_type=MESH,
        )


def guarded(condition, action):
    if condition is None:
        action()
    else:
        pl.when(condition)(action)


class Flow:
    def __init__(self, wires):
        self.wires, self.arriving, self.sent = wires, [], []

    def move(self, src, dst, moved, landing, goes=None, comes=None):
        pair = self.wires.used
        self.wires.used += 1
        out = lambda: self.wires.copy(src, dst, pair, moved)
        guarded(goes, lambda: out().start())
        self.sent.append((goes, lambda: out().wait_send()))
        self.arriving.append(
            (comes, lambda: self.wires.copy(landing, landing, pair, moved).wait_recv())
        )

    def arrive(self):
        for condition, wait in self.arriving:
            guarded(condition, wait)
        self.arriving.clear()

    def finish(self):
        self.arrive()
        for condition, wait in self.sent:
            guarded(condition, wait)
        self.sent.clear()


def gather(wires, source, target, order, columns, local_sem):
    place, flow = wires.place, Flow(wires)
    axes = ("m" if len(target.shape) == 6 else "") + "zxc"
    at, sizes, done = place.at, place.sizes, set()

    def view(**moved):
        index = [
            moved[a] if a in moved else pl.ds(0, sizes[a]) if a in done else at[a] for a in axes
        ]
        return target.at[tuple(index) + block]

    block = (pl.ds(0, source.shape[0]), pl.ds(*columns))
    source = source.at[block]
    own = pltpu.make_async_copy(source, view(), local_sem)
    own.start()
    first = True
    z, last = at["z"], sizes["z"] - 1
    for axis in order + "c":
        if axis == "z":
            for t in range(last):
                flow.arrive()
                below, above = lax.max(z - t, 0), lax.min(z + t, last)
                flow.move(
                    source if first and t == 0 else view(z=below),
                    view(z=below),
                    dict(z=z + 1),
                    view(z=lax.max(z - 1 - t, 0)),
                    (z >= t) & (z < last),
                    z >= t + 1,
                )
                flow.move(
                    source if first and t == 0 else view(z=above),
                    view(z=above),
                    dict(z=z - 1),
                    view(z=lax.min(z + 1 + t, last)),
                    (z + t <= last) & (z > 0),
                    z + 1 + t <= last,
                )
                yield
        else:
            flow.arrive()
            for step in range(1, sizes[axis]):
                flow.move(
                    source if first else view(),
                    view(),
                    {axis: place.ahead(axis, step)},
                    view(**{axis: place.behind(axis, step)}),
                )
            yield
        done.add(axis)
        if first:
            own.wait()
            first = False
    flow.finish()


def add_into(total, term):
    lead = total.shape[:-2]

    def body(i, carry):
        index, rest = [], i
        for size in reversed(lead):
            index.append(lax.rem(rest, size))
            rest = lax.div(rest, size)
        there = tuple(reversed(index))
        summed = total[there].astype(jnp.float32) + term[there].astype(jnp.float32)
        total[there] = summed.astype(total.dtype)
        return carry

    lax.fori_loop(0, functools.reduce(lambda a, b: a * b, lead, 1), body, 0)


def scatter(wires, grad, result, own, core_in, m_in, x_in, up_in, down_in, order, columns, local_sem):
    place, flow = wires.place, Flow(wires)
    split_m = len(grad.shape) == 6
    axes = ("m" if split_m else "") + "zx"
    at, sizes, done = place.at, place.sizes, set()
    z, last = at["z"], sizes["z"] - 1
    full = tuple(pl.ds(0, sizes[a]) for a in axes)
    block = (pl.ds(0, grad.shape[-2]), pl.ds(*columns))

    def view(ref, **moved):
        index = [
            moved[a] if a in moved else at[a] if a in done else pl.ds(0, sizes[a]) for a in axes
        ]
        return ref.at[tuple(index)]

    load = pltpu.make_async_copy(grad.at[full + (at["c"],) + block], own, local_sem)
    load.start()
    flow.move(grad.at[full + (1 - at["c"],) + block], core_in, dict(c=1 - at["c"]), core_in)
    yield
    load.wait()
    flow.arrive()
    add_into(own, core_in)
    for axis in order:
        if axis == "x":
            flow.move(view(own, x=1 - at["x"]), x_in, dict(x=1 - at["x"]), x_in)
            yield
            flow.arrive()
            done.add("x")
            add_into(view(own), x_in)
        elif axis == "m":
            for step in range(1, sizes["m"]):
                flow.move(
                    view(own, m=place.ahead("m", step)), m_in.at[step - 1],
                    dict(m=place.ahead("m", step)), m_in.at[step - 1],
                )
            yield
            flow.arrive()
            done.add("m")
            for step in range(1, sizes["m"]):
                add_into(view(own), m_in.at[step - 1])
        else:
            for t in range(last):
                up, down = lax.min(last - t + z, last), lax.max(z - last + t, 0)
                flow.move(view(own, z=up), up_in.at[t], dict(z=z + 1), up_in.at[t],
                          (z <= t) & (z < last), (z >= 1) & (z - 1 <= t))
                flow.move(view(own, z=down), down_in.at[t], dict(z=z - 1), down_in.at[t],
                          (last - z <= t) & (z > 0), (z < last) & (last - z - 1 <= t))
                yield
                flow.arrive()
                up, down = lax.min(last - 1 - t + z, last), lax.max(z - last + t + 1, 0)
                pl.when((z >= 1) & (z - 1 <= t))(lambda: add_into(view(own, z=up), up_in.at[t]))
                pl.when((z < last) & (last - z - 1 <= t))(lambda: add_into(view(own, z=down), down_in.at[t]))
            done.add("z")
    if split_m:
        result[block] = view(own)[...].astype(jnp.float32)
    else:
        slot = m_in.at[at["m"]]
        slot[...] = view(own)[...]
        for step in range(1, sizes["m"]):
            flow.move(slot, slot, dict(m=place.ahead("m", step)), m_in.at[place.behind("m", step)])
        yield
        flow.arrive()
        total = m_in[0].astype(jnp.float32)
        for i in range(1, sizes["m"]):
            total = total + m_in[i].astype(jnp.float32)
        result[block] = total
    flow.finish()


def run_rounds(flows):
    live, waiting = [], list(flows)
    while live or waiting:
        if waiting:
            live.append(waiting.pop(0))
        live = [f for f in live if next(f, StopIteration) is not StopIteration]


def lead_shape(order, split_m, done, sizes):
    axes = ("m" if split_m else "") + "zx"
    return tuple(sizes[a] for a in axes if a not in done)


def gather_call(sources, units, seg_size, mlp_size, name, collective_id):
    count = len(sources)
    sizes = {"z": seg_size // 4, "x": 2, "c": 2, "m": mlp_size}

    def kernel(*refs):
        ins, outs = refs[:count], refs[count : 2 * count]
        send, recv, local = refs[2 * count :]
        place = Place(seg_size, mlp_size)
        place.greet()
        wires = Wires(place, send, recv)
        run_rounds(
            [
                gather(wires, ins[i], outs[i], order, columns, local.at[unit])
                for unit, (i, order, columns) in enumerate(units)
            ]
        )

    kinds = {i: order for i, order, _ in units}
    shapes = [
        jax.ShapeDtypeStruct(
            ((mlp_size,) if "m" in kinds[i] else ()) + (sizes["z"], 2, 2) + source.shape,
            source.dtype,
        )
        for i, source in enumerate(sources)
    ]
    pairs = sum(2 * (sizes["z"] - 1) + 2 + ("m" in order) * (mlp_size - 1) for _, order, _ in units)
    anywhere = pl.BlockSpec(memory_space=pl.ANY)
    return pl.pallas_call(
        kernel,
        out_shape=shapes,
        in_specs=[anywhere] * count,
        out_specs=[anywhere] * count,
        scratch_shapes=[
            pltpu.SemaphoreType.DMA((pairs,)),
            pltpu.SemaphoreType.DMA((pairs,)),
            pltpu.SemaphoreType.DMA((len(units),)),
        ],
        compiler_params=pltpu.CompilerParams(collective_id=collective_id, has_side_effects=True),
        name=name,
    )(*sources)


def scatter_buffers(grad, order, columns, sizes):
    split_m = grad.ndim == 6
    rows = (grad.shape[-2], columns[1])

    def left(axis):
        done = order[: order.index(axis) + 1]
        return lead_shape(order, split_m, done, sizes) + rows

    return [
        pltpu.VMEM(shape, grad.dtype)
        for shape in (
            lead_shape(order, split_m, "", sizes) + rows,
            lead_shape(order, split_m, "", sizes) + rows,
            (sizes["m"] - 1,) + left("m") if split_m else (sizes["m"],) + rows,
            left("x"),
            (sizes["z"] - 1,) + left("z"),
            (sizes["z"] - 1,) + left("z"),
        )
    ]


def scatter_call(grads, units, seg_size, mlp_size, name, collective_id):
    count = len(grads)
    sizes = {"z": seg_size // 4, "x": 2, "c": 2, "m": mlp_size}

    def kernel(*refs):
        ins, outs = refs[:count], refs[count : 2 * count]
        buffers = refs[2 * count : -3]
        send, recv, local = refs[-3:]
        place = Place(seg_size, mlp_size)
        place.greet()
        wires = Wires(place, send, recv)
        run_rounds(
            [
                scatter(
                    wires, ins[i], outs[i], *buffers[6 * unit : 6 * unit + 6], order, columns,
                    local.at[unit],
                )
                for unit, (i, order, columns) in enumerate(units)
            ]
        )

    buffers = []
    for i, order, columns in units:
        buffers += scatter_buffers(grads[i], order, columns, sizes)
    pairs = sum(2 * (sizes["z"] - 1) + 2 + (mlp_size - 1) for _, order, _ in units)
    return pl.pallas_call(
        kernel,
        out_shape=[jax.ShapeDtypeStruct(grad.shape[-2:], jnp.float32) for grad in grads],
        in_specs=[pl.BlockSpec(memory_space=pl.ANY)] * count,
        out_specs=[pl.BlockSpec(memory_space=pltpu.VMEM)] * count,
        scratch_shapes=buffers
        + [
            pltpu.SemaphoreType.DMA((pairs,)),
            pltpu.SemaphoreType.DMA((pairs,)),
            pltpu.SemaphoreType.DMA((len(units),)),
        ],
        compiler_params=pltpu.CompilerParams(
            collective_id=collective_id, has_side_effects=True, vmem_limit_bytes=56 << 20
        ),
        name=name,
    )(*grads)


HEAD = 128
BLOCK = 512
EPS = 1e-06
NEGATIVE = -1e30
GELU_C = 0.7978845608
GELU_K = 0.044715
SCALE = HEAD**-0.5
LOG2E = 1.4426950408889634
PAIR = 2 * HEAD
TILE = 256
BF16 = jnp.bfloat16
F32 = jnp.float32
VMEM_LIMIT = 60 << 20


def matmul(left, right):
    return jnp.dot(left, right, preferred_element_type=F32)


def matmul_nt(left, right):
    return lax.dot_general(left, right, (((1,), (1,)), ((), ())), preferred_element_type=F32)


def inverse_rms(values):
    return lax.rsqrt(jnp.mean(values * values, axis=-1, keepdims=True) + EPS)


def rms_backward(values, gain, grad):
    inverse = inverse_rms(values)
    unit = values * inverse
    weighted = grad * gain
    inner = jnp.mean(weighted * unit, axis=-1, keepdims=True)
    return inverse * (weighted - unit * inner), grad * unit


def params(**more):
    return pltpu.CompilerParams(vmem_limit_bytes=VMEM_LIMIT, **more)


def whole(shape):
    return pl.BlockSpec(shape, lambda *_: (0,) * len(shape))


def project_kernel(x_ref, gain_ref, wq, wk, wv, normed, q, k, v):
    @pl.when(pl.program_id(0) == 0)
    def _():
        x = x_ref[...].astype(F32)
        normed[...] = (x * inverse_rms(x) * gain_ref[...]).astype(BF16)

    rows = normed[...]
    for weight, out in ((wq, q), (wk, k), (wv, v)):
        out[...] = matmul(rows, weight[...]).astype(BF16)


def project(x, gain, weights):
    rows, width = x.shape
    tile = pl.BlockSpec((width, TILE), lambda j: (0, j))
    out = pl.BlockSpec((rows, TILE), lambda j: (0, j))
    return pl.pallas_call(
        project_kernel,
        grid=(width // TILE,),
        in_specs=[whole((rows, width)), whole((1, width)), tile, tile, tile],
        out_specs=[whole((rows, width)), out, out, out],
        out_shape=[jax.ShapeDtypeStruct((rows, width), BF16)] * 4,
        compiler_params=params(),
        name="project_tokens",
    )(x, gain, *weights)


def attend(query, pieces):
    scores = []
    for keys, _, mask in pieces:
        score = matmul_nt(keys, query) * (SCALE * LOG2E)
        scores.append(score if mask is None else jnp.where(mask, score, NEGATIVE))
    top = functools.reduce(jnp.maximum, [jnp.max(s, axis=0, keepdims=True) for s in scores])
    total, mixed = 0.0, 0.0
    for score, (_, values, _) in zip(scores, pieces):
        weights = jnp.exp2(score - top)
        total = total + jnp.sum(weights, axis=0, keepdims=True)
        mixed = mixed + matmul(values.T, weights.astype(BF16))
    return (mixed / total).T.astype(BF16), top + jnp.log2(total)


def attend_backward(query, log_total, grad, centre, pieces):
    grad_query = 0.0
    for keys, values, mask, add_keys, add_values in pieces:
        score = matmul_nt(keys, query) * (SCALE * LOG2E)
        if mask is not None:
            score = jnp.where(mask, score, NEGATIVE)
        probs = jnp.exp2(score - log_total)
        add_values(matmul(probs.astype(BF16), grad))
        grad_probs = matmul_nt(values, grad)
        grad_scores = (probs * (grad_probs - centre)).astype(BF16)
        add_keys(matmul(grad_scores, query) * SCALE)
        grad_query = grad_query + matmul(keys.T, grad_scores)
    return (grad_query * SCALE).T


def centre_of(grad, mixed):
    return jnp.sum((grad.astype(F32) * mixed.astype(F32)).T, axis=0, keepdims=True)


def position(shape, axis):
    return lax.broadcasted_iota(jnp.int32, shape, axis)


def token_pieces(block, half, valid):
    key = position((TILE, TILE), 0)
    query = position((TILE, TILE), 1)
    causal, recent = key <= query, key > query
    pieces = []
    if block:
        start = (block - 1) * BLOCK
        pieces.append(("near", start + half * TILE, TILE, recent))
        if half == 0:
            pieces.append(("near", start + TILE, TILE, None))
    start = block * BLOCK
    for piece in range(half + 1):
        first = start + piece * TILE
        seen = first + key < valid
        mask = causal if piece == half else None
        if block:
            mask = seen if mask is None else mask & seen
        pieces.append(("near", first, TILE, mask))
    pieces.append(("state", block * BLOCK, BLOCK, None))
    return pieces


def state_forward_kernel(
    valid, s0, gain, gate_bias, wq, wk, wv, wu, k, v,
    normed_out, sq, sk, sv, read, log_out, update_out, states, last,
    state, normed, total,
):
    block, pair = pl.program_id(0), pl.program_id(1)

    @pl.when((block == 0) & (pair == 0))
    def _():
        state[...] = s0[...].astype(F32)

    @pl.when(pair == 0)
    def _():
        now = state[...]
        rows = (now * inverse_rms(now) * gain[...]).astype(BF16)
        normed[...] = rows
        normed_out[...] = rows
        states[...] = now
        total[...] = jnp.zeros_like(total)

    rows = normed[...]
    for weight, out in ((wq, sq), (wk, sk), (wv, sv)):
        out[...] = matmul(rows, weight[...]).astype(BF16)
    seen = block * BLOCK + position((BLOCK, BLOCK), 0) < valid[0]
    for head in range(2):
        lanes = pl.ds(head * HEAD, HEAD)
        read[:, lanes], log_out[0, 0, pl.ds(head, 1), :] = attend(
            sq[:, lanes], [(k[:, lanes], v[:, lanes], seen)]
        )
    total[...] += matmul(read[...], wu[...])

    @pl.when(pair == pl.num_programs(1) - 1)
    def _():
        update = total[...]
        gate = 1.0 / (1.0 + jnp.exp(-gate_bias[...]))
        later = gate * state[...] + (1.0 - gate) * update
        update_out[...] = update
        state[...] = later
        last[...] = later.astype(BF16)


def state_forward(valid, s0, gain, gate_bias, weights, update_weight, k, v):
    rows, width = s0.shape
    blocks, pairs = k.shape[0] // BLOCK, width // PAIR
    columns = pl.BlockSpec((width, PAIR), lambda b, p: (0, p))
    tile = pl.BlockSpec((rows, PAIR), lambda b, p: (b, p))
    band = pl.BlockSpec((rows, width), lambda b, p: (b, 0))
    small = whole((1, width))

    def stack(kind):
        return jax.ShapeDtypeStruct((blocks * rows, width), kind)

    return pl.pallas_call(
        state_forward_kernel,
        grid=(blocks, pairs),
        in_specs=[
            pl.BlockSpec(memory_space=pltpu.SMEM), whole((rows, width)), small, small,
            columns, columns, columns, pl.BlockSpec((PAIR, width), lambda b, p: (p, 0)),
            pl.BlockSpec((BLOCK, PAIR), lambda b, p: (b, p)),
            pl.BlockSpec((BLOCK, PAIR), lambda b, p: (b, p)),
        ],
        out_specs=[
            band, tile, tile, tile, tile,
            pl.BlockSpec((1, 1, 2, rows), lambda b, p: (b, p, 0, 0)),
            band, band, whole((rows, width)),
        ],
        out_shape=[
            stack(BF16), stack(BF16), stack(BF16), stack(BF16), stack(BF16),
            jax.ShapeDtypeStruct((blocks, pairs, 2, rows), F32),
            stack(F32), stack(F32), jax.ShapeDtypeStruct((rows, width), BF16),
        ],
        scratch_shapes=[
            pltpu.VMEM((rows, width), F32), pltpu.VMEM((rows, width), BF16),
            pltpu.VMEM((rows, width), F32),
        ],
        compiler_params=params(),
        name="state_forward",
    )(valid, s0, gain, gate_bias, *weights, update_weight, k, v)


def token_forward_kernel(
    valid, x, gain, q, k, v, sk, sv, wo, mixed, log_out, resid, ynorm
):
    pair = pl.program_id(0)

    @pl.when(pair == 0)
    def _():
        resid[...] = x[...].astype(F32)

    count = valid[0]
    for head in range(2):
        lanes = pl.ds(head * HEAD, HEAD)
        for block in range(q.shape[0] // BLOCK):
            for half in range(BLOCK // TILE):
                rows = pl.ds(block * BLOCK + half * TILE, TILE)
                pieces = []
                for kind, first, size, mask in token_pieces(block, half, count):
                    keys, values = (k, v) if kind == "near" else (sk, sv)
                    there = pl.ds(first, size)
                    pieces.append((keys[there, lanes], values[there, lanes], mask))
                mixed[rows, lanes], log_out[0, pl.ds(head, 1), rows] = attend(
                    q[rows, lanes], pieces
                )
    resid[...] += matmul(mixed[...], wo[...])

    @pl.when(pair == pl.num_programs(0) - 1)
    def _():
        rows = resid[...]
        ynorm[...] = (rows * inverse_rms(rows) * gain[...]).astype(BF16)


def token_forward(valid, x, gain, q, k, v, sk, sv, wo):
    rows, width = x.shape
    pairs = width // PAIR
    tile = pl.BlockSpec((rows, PAIR), lambda p: (0, p))
    states = pl.BlockSpec((sk.shape[0], PAIR), lambda p: (0, p))
    return pl.pallas_call(
        token_forward_kernel,
        grid=(pairs,),
        in_specs=[
            pl.BlockSpec(memory_space=pltpu.SMEM), whole((rows, width)), whole((1, width)),
            tile, tile, tile, states, states, pl.BlockSpec((PAIR, width), lambda p: (p, 0)),
        ],
        out_specs=[
            tile, pl.BlockSpec((1, 2, rows), lambda p: (p, 0, 0)),
            whole((rows, width)), whole((rows, width)),
        ],
        out_shape=[
            jax.ShapeDtypeStruct((rows, width), BF16),
            jax.ShapeDtypeStruct((pairs, 2, rows), F32),
            jax.ShapeDtypeStruct((rows, width), F32),
            jax.ShapeDtypeStruct((rows, width), BF16),
        ],
        compiler_params=params(),
        name="token_forward",
    )(valid, x, gain, q, k, v, sk, sv, wo)


def feed_forward_kernel(
    valid, resid, ynorm, gain, cot, up_w, down_w,
    out, grad_resid, grad_rounded, gain_grad, up_grad, down_grad,
    ynorm_t, masked, masked_t, total, grad_total,
):
    step, last = pl.program_id(0), pl.num_programs(0) - 1

    @pl.when(step == 0)
    def _():
        keep = position(cot.shape, 0) < valid[0]
        grad = jnp.where(keep, cot[...], jnp.zeros_like(cot))
        masked[...] = grad
        masked_t[...] = grad.T
        ynorm_t[...] = ynorm[...].T
        total[...] = resid[...]
        grad_total[...] = jnp.zeros_like(grad_total)

    up_part, down_part = up_w[0], down_w[0]
    up = matmul(ynorm[...], up_part)
    grad_hidden = matmul(masked[...], down_part)
    square = up * up
    bent = jnp.tanh(GELU_C * (up + GELU_K * square * up))
    hidden = (0.5 * up * (1.0 + bent)).astype(BF16)
    slope = 0.5 * (1.0 + bent) + 0.5 * up * (1.0 - bent * bent) * (
        GELU_C * (1.0 + 3.0 * GELU_K * square)
    )
    grad_up = (grad_hidden * slope).astype(BF16)
    total[...] += matmul_nt(hidden, down_part)
    grad_total[...] += matmul_nt(grad_up, up_part)
    down_grad[0] = matmul(masked_t[...], hidden).astype(BF16)
    up_grad[0] = matmul(ynorm_t[...], grad_up).astype(BF16)

    @pl.when(step == last)
    def _():
        out[...] = total[...].astype(BF16)
        grad, gain_rows = rms_backward(resid[...], gain[...], grad_total[...])
        grad = masked[...].astype(F32) + grad
        grad_resid[...] = grad
        grad_rounded[...] = grad.astype(BF16)
        gain_grad[...] = jnp.sum(gain_rows, axis=0, keepdims=True)


def feed_forward(valid, resid, ynorm, gain, cot, up_w, down_w, chunk=512):
    rows, width = resid.shape
    parts, _, part = up_w.shape
    chunk = min(chunk, part)
    each = part // chunk
    weight = pl.BlockSpec((1, width, chunk), lambda j: (j // each, 0, j % each))
    full = whole((rows, width))
    once = pl.BlockSpec((rows, width), lambda j: (0, 0), pipeline_mode=pl.Buffered(1))
    return pl.pallas_call(
        feed_forward_kernel,
        grid=(parts * each,),
        in_specs=[pl.BlockSpec(memory_space=pltpu.SMEM), once, once, whole((1, width)), once, weight, weight],
        out_specs=[once, once, once, whole((1, width)), weight, weight],
        out_shape=[
            jax.ShapeDtypeStruct((rows, width), BF16),
            jax.ShapeDtypeStruct((rows, width), F32),
            jax.ShapeDtypeStruct((rows, width), BF16),
            jax.ShapeDtypeStruct((1, width), F32),
            jax.ShapeDtypeStruct(up_w.shape, BF16),
            jax.ShapeDtypeStruct(down_w.shape, BF16),
        ],
        scratch_shapes=[
            pltpu.VMEM((width, rows), BF16), pltpu.VMEM((rows, width), BF16),
            pltpu.VMEM((width, rows), BF16), pltpu.VMEM((rows, width), F32),
            pltpu.VMEM((rows, width), F32),
        ],
        compiler_params=params(),
        name="feed_forward",
    )(valid, resid, ynorm, gain, cot, up_w, down_w)


def token_backward_kernel(
    valid, grad, q, k, v, sk, sv, wo, mixed, log_total,
    dq, dk, dv, dsk, dsv, wo_grad,
    grad_mixed, near_k, near_v, state_k, state_v,
):
    grad_rows = grad[...]
    grad_mixed[...] = matmul_nt(grad_rows, wo[...]).astype(BF16)
    wo_grad[...] = matmul(mixed[...].T, grad_rows).astype(BF16)
    for ref in (near_k, near_v, state_k, state_v):
        ref[...] = jnp.zeros_like(ref)
    count = valid[0]
    for head in range(2):
        lanes = pl.ds(head * HEAD, HEAD)

        def adder(ref, there):
            def add(term):
                ref[there, lanes] += term

            return add

        for block in range(q.shape[0] // BLOCK):
            for half in range(BLOCK // TILE):
                rows = pl.ds(block * BLOCK + half * TILE, TILE)
                pieces = []
                for kind, first, size, mask in token_pieces(block, half, count):
                    keys, values = (k, v) if kind == "near" else (sk, sv)
                    sums = (near_k, near_v) if kind == "near" else (state_k, state_v)
                    there = pl.ds(first, size)
                    pieces.append(
                        (keys[there, lanes], values[there, lanes], mask)
                        + tuple(adder(ref, there) for ref in sums)
                    )
                out_grad = grad_mixed[rows, lanes]
                dq[rows, lanes] = attend_backward(
                    q[rows, lanes],
                    log_total[0, pl.ds(head, 1), rows],
                    out_grad,
                    centre_of(out_grad, mixed[rows, lanes]),
                    pieces,
                ).astype(BF16)
    dk[...] = near_k[...]
    dv[...] = near_v[...]
    dsk[...] = state_k[...].astype(BF16)
    dsv[...] = state_v[...].astype(BF16)


def token_backward(valid, grad, q, k, v, sk, sv, wo, mixed, log_total):
    rows, width = grad.shape
    pairs = width // PAIR
    tile = pl.BlockSpec((rows, PAIR), lambda p: (0, p))
    states = pl.BlockSpec((sk.shape[0], PAIR), lambda p: (0, p))
    band = pl.BlockSpec((PAIR, width), lambda p: (p, 0))
    return pl.pallas_call(
        token_backward_kernel,
        grid=(pairs,),
        in_specs=[
            pl.BlockSpec(memory_space=pltpu.SMEM), whole((rows, width)),
            tile, tile, tile, states, states, band, tile,
            pl.BlockSpec((1, 2, rows), lambda p: (p, 0, 0)),
        ],
        out_specs=[tile, tile, tile, states, states, band],
        out_shape=[
            jax.ShapeDtypeStruct((rows, width), BF16),
            jax.ShapeDtypeStruct((rows, width), F32),
            jax.ShapeDtypeStruct((rows, width), F32),
            jax.ShapeDtypeStruct(sk.shape, BF16),
            jax.ShapeDtypeStruct(sk.shape, BF16),
            jax.ShapeDtypeStruct((width, width), BF16),
        ],
        scratch_shapes=[
            pltpu.VMEM((rows, PAIR), BF16), pltpu.VMEM((rows, PAIR), F32),
            pltpu.VMEM((rows, PAIR), F32), pltpu.VMEM((sk.shape[0], PAIR), F32),
            pltpu.VMEM((sk.shape[0], PAIR), F32),
        ],
        compiler_params=params(),
        name="token_backward",
    )(valid, grad, q, k, v, sk, sv, wo, mixed, log_total)


def state_backward_kernel(
    valid, cot, gain, gate_bias, wq, wk, wv, wu, states, updates,
    sq, k, v, read, log_total, near_k, near_v, dsk, dsv,
    dsq, dk, dv, dz_out, grad_state, gain_grad, bias_grad,
    later, dz, total, grad_read, sum_q, sum_k, sum_v,
):
    step, pair = pl.program_id(0), pl.program_id(1)
    block = pl.num_programs(0) - 1 - step
    gate = 1.0 / (1.0 + jnp.exp(-gate_bias[...]))

    @pl.when((step == 0) & (pair == 0))
    def _():
        later[...] = cot[...].astype(F32)
        gain_grad[...] = jnp.zeros_like(gain_grad)
        bias_grad[...] = jnp.zeros_like(bias_grad)

    @pl.when(pair == 0)
    def _():
        grad = later[...]
        rounded = (grad * (1.0 - gate)).astype(BF16)
        dz[...] = rounded
        dz_out[...] = rounded
        bias_grad[...] += (
            jnp.sum(grad * (states[...] - updates[...]), axis=0, keepdims=True) * gate * (1.0 - gate)
        )
        total[...] = jnp.zeros_like(total)

    grad_read[...] = matmul_nt(dz[...], wu[...]).astype(BF16)
    seen = block * BLOCK + position((BLOCK, BLOCK), 0) < valid[0]
    sum_k[...] = near_k[...]
    sum_v[...] = near_v[...]
    for head in range(2):
        lanes = pl.ds(head * HEAD, HEAD)

        def adder(ref):
            def add(term):
                ref[:, lanes] += term

            return add

        out_grad = grad_read[:, lanes]
        dsq[:, lanes] = attend_backward(
            sq[:, lanes],
            log_total[0, 0, pl.ds(head, 1), :],
            out_grad,
            centre_of(out_grad, read[:, lanes]),
            [(k[:, lanes], v[:, lanes], seen, adder(sum_k), adder(sum_v))],
        ).astype(BF16)
    dk[...] = sum_k[...].astype(BF16)
    dv[...] = sum_v[...].astype(BF16)
    total[...] += (
        matmul_nt(dsq[...], wq[...]) + matmul_nt(dsk[...], wk[...]) + matmul_nt(dsv[...], wv[...])
    )

    @pl.when(pair == pl.num_programs(1) - 1)
    def _():
        grad, gain_rows = rms_backward(states[...], gain[...], total[...])
        grad = later[...] * gate + grad
        later[...] = grad
        grad_state[...] = grad
        gain_grad[...] += jnp.sum(gain_rows, axis=0, keepdims=True)


def state_backward(
    valid, cot, gain, gate_bias, weights, update_weight, states, updates,
    sq, k, v, read, log_total, near_k, near_v, dsk, dsv,
):
    rows, width = cot.shape
    blocks, pairs = k.shape[0] // BLOCK, width // PAIR
    columns = pl.BlockSpec((width, PAIR), lambda s, p: (0, p))
    tile = pl.BlockSpec((rows, PAIR), lambda s, p: (blocks - 1 - s, p))
    token = pl.BlockSpec((BLOCK, PAIR), lambda s, p: (blocks - 1 - s, p))
    band = pl.BlockSpec((rows, width), lambda s, p: (blocks - 1 - s, 0))
    small = whole((1, width))
    return pl.pallas_call(
        state_backward_kernel,
        grid=(blocks, pairs),
        in_specs=[
            pl.BlockSpec(memory_space=pltpu.SMEM), whole((rows, width)), small, small,
            columns, columns, columns, pl.BlockSpec((PAIR, width), lambda s, p: (p, 0)),
            band, band, tile, token, token, tile,
            pl.BlockSpec((1, 1, 2, rows), lambda s, p: (blocks - 1 - s, p, 0, 0)),
            token, token, tile, tile,
        ],
        out_specs=[tile, token, token, band, whole((rows, width)), small, small],
        out_shape=[
            jax.ShapeDtypeStruct((blocks * rows, width), BF16),
            jax.ShapeDtypeStruct(k.shape, BF16),
            jax.ShapeDtypeStruct(k.shape, BF16),
            jax.ShapeDtypeStruct((blocks * rows, width), BF16),
            jax.ShapeDtypeStruct((rows, width), F32),
            jax.ShapeDtypeStruct((1, width), F32),
            jax.ShapeDtypeStruct((1, width), F32),
        ],
        scratch_shapes=[
            pltpu.VMEM((rows, width), F32), pltpu.VMEM((rows, width), BF16),
            pltpu.VMEM((rows, width), F32), pltpu.VMEM((rows, PAIR), BF16),
            pltpu.VMEM((rows, PAIR), F32), pltpu.VMEM((BLOCK, PAIR), F32),
            pltpu.VMEM((BLOCK, PAIR), F32),
        ],
        compiler_params=params(),
        name="state_backward",
    )(
        valid, cot, gain, gate_bias, *weights, update_weight, states, updates,
        sq, k, v, read, log_total, near_k, near_v, dsk, dsv,
    )


def token_grad_kernel(x, gain, grad_resid, dq, dk, dv, wq, wk, wv, grad_x, gain_grad):
    @pl.when(pl.program_id(0) == 0)
    def _():
        gain_grad[...] = jnp.zeros_like(gain_grad)

    grad_normed = (
        matmul_nt(dq[...], wq[...]) + matmul_nt(dk[...], wk[...]) + matmul_nt(dv[...], wv[...])
    )
    grad, gain_rows = rms_backward(x[...].astype(F32), gain[...], grad_normed)
    grad_x[...] = grad_resid[...] + grad
    gain_grad[...] += jnp.sum(gain_rows, axis=0, keepdims=True)


def token_grad(x, gain, grad_resid, grads, weights):
    rows, width = x.shape
    band = pl.BlockSpec((TILE, width), lambda i: (i, 0))
    weight = whole((width, width))
    return pl.pallas_call(
        token_grad_kernel,
        grid=(rows // TILE,),
        in_specs=[band, whole((1, width)), band, band, band, band, weight, weight, weight],
        out_specs=[band, whole((1, width))],
        out_shape=[
            jax.ShapeDtypeStruct((rows, width), F32), jax.ShapeDtypeStruct((1, width), F32)
        ],
        compiler_params=params(),
        name="token_grad",
    )(x, gain, grad_resid, *grads, *weights)


def weight_grad_kernel(count, left, *refs):
    rights, outs, left_t = refs[:count], refs[count : 2 * count], refs[-1]

    @pl.when(pl.program_id(0) == 0)
    def _():
        left_t[...] = left[...].T

    for right, out in zip(rights, outs):
        out[...] = matmul(left_t[...], right[...]).astype(BF16)


def weight_grad(left, rights, name):
    rows, width = left.shape
    count = len(rights)
    tile = pl.BlockSpec((rows, TILE), lambda j: (0, j))
    out = pl.BlockSpec((width, TILE), lambda j: (0, j))
    return pl.pallas_call(
        functools.partial(weight_grad_kernel, count),
        grid=(rights[0].shape[1] // TILE,),
        in_specs=[whole((rows, width))] + [tile] * count,
        out_specs=[out] * count,
        out_shape=[jax.ShapeDtypeStruct((width, right.shape[1]), BF16) for right in rights],
        scratch_shapes=[pltpu.VMEM((width, rows), BF16)],
        compiler_params=params(),
        name=name,
    )(left, *rights)


def shards(
    mlp_size,
    tokens,
    initial_state,
    valid,
    token_query_weight,
    token_key_weight,
    token_value_weight,
    token_output_weight,
    state_query_weight,
    state_key_weight,
    state_value_weight,
    state_update_weight,
    up_projection_weight,
    down_projection_weight,
    token_norm_gain,
    state_norm_gain,
    feedforward_norm_gain,
    state_gate_bias,
    output_cotangent,
    final_state_cotangent,
):
    rows = token_query_weight.shape[0]
    width = tokens.shape[2]
    seg_size = width // rows
    depth = seg_size // 4
    part = up_projection_weight.shape[1]
    small = jnp.concatenate(
        [token_norm_gain, state_norm_gain, feedforward_norm_gain, state_gate_bias]
    ).reshape(-1, 128)
    small = jnp.pad(small, ((0, 16 - small.shape[0]), (0, 0)))
    square = [
        token_query_weight,
        token_key_weight,
        token_value_weight,
        state_query_weight,
        state_key_weight,
        state_value_weight,
        token_output_weight,
        state_update_weight,
    ]
    half = part // 2
    gathered = gather_call(
        [small] + square + [up_projection_weight, down_projection_weight],
        [(0, "zx", (0, small.shape[1]))]
        + [(1 + i, "zx", (0, width)) for i in range(8)]
        + [(9 + i, "zxm", (h * half, half)) for h in range(2) for i in range(2)],
        seg_size,
        mlp_size,
        "gather_weights",
        1,
    )
    wq, wk, wv, sqw, skw, svw, wo, wu = [w.reshape(width, width) for w in gathered[1:9]]
    up_w, down_w = [w.reshape(mlp_size, width, part) for w in gathered[9:]]
    gains = gathered[0].reshape(seg_size, -1)[:, : 4 * rows].reshape(seg_size, 4, rows)
    gains = gains.transpose(1, 0, 2).reshape(4, 1, width).astype(F32)
    token_gain, state_gain, mlp_gain, gate_bias = [gains[i] for i in range(4)]

    x, s0 = tokens[0], initial_state[0]
    normed, q, k, v = project(x, token_gain, [wq, wk, wv])
    snormed, sq, sk, sv, read, read_log, updates, states, last = state_forward(
        valid, s0, state_gain, gate_bias, [sqw, skw, svw], wu, k, v
    )
    mixed, token_log, resid, ynorm = token_forward(valid, x, mlp_gain, q, k, v, sk, sv, wo)
    out, grad_resid, grad_rounded, mlp_gain_grad, up_grad, down_grad = feed_forward(
        valid, resid, ynorm, mlp_gain, output_cotangent[0], up_w, down_w
    )
    forward_grads = [
        g.reshape(mlp_size, depth, 2, 2, rows, part) for g in (up_grad, down_grad)
    ]
    up_sum, down_sum = scatter_call(
        forward_grads,
        [(i, "mxz", (h * half, half)) for h in range(2) for i in range(2)],
        seg_size,
        mlp_size,
        "scatter_forward",
        2,
    )
    dq, near_k, near_v, dsk, dsv, wo_grad = token_backward(
        valid, grad_rounded, q, k, v, sk, sv, wo, mixed, token_log
    )
    dsq, dk, dv, dz, grad_state, state_gain_grad, bias_grad = state_backward(
        valid, final_state_cotangent[0], state_gain, gate_bias, [sqw, skw, svw], wu,
        states, updates, sq, k, v, read, read_log, near_k, near_v, dsk, dsv,
    )
    grad_tokens, token_gain_grad = token_grad(
        x, token_gain, grad_resid, [dq, dk, dv], [wq, wk, wv]
    )
    square_grads = (
        [wo_grad]
        + list(weight_grad(read, [dz], "weight_grad_update"))
        + list(weight_grad(snormed, [dsq, dsk, dsv], "weight_grad_state"))
        + list(weight_grad(normed, [dq, dk, dv], "weight_grad_tokens"))
    )
    small_grads = jnp.concatenate([token_gain_grad, state_gain_grad, mlp_gain_grad, bias_grad])
    small_grads = small_grads.reshape(4, seg_size, rows).transpose(1, 0, 2)
    small_grads = small_grads.reshape(seg_size, -1, 128)
    lines = small_grads.shape[1]
    small_grads = jnp.pad(small_grads, ((0, 0), (0, 8 - lines), (0, 0)))
    summed = scatter_call(
        [small_grads.reshape(depth, 2, 2, 8, 128)]
        + [grad.reshape(depth, 2, 2, rows, width) for grad in square_grads],
        [(0, "xz", (0, 128))] + [(1 + i, "xz", (0, width)) for i in range(8)],
        seg_size,
        mlp_size,
        "scatter_rest",
        3,
    )
    small_sum, go, gu, gsq, gsk, gsv, gq, gk, gv = summed
    small_sum = small_sum[:lines].reshape(4, rows)
    return (
        out[None],
        last[None],
        grad_tokens[None],
        grad_state[None],
        gq,
        gk,
        gv,
        go,
        gsq,
        gsk,
        gsv,
        gu,
        up_sum,
        down_sum,
        small_sum[0],
        small_sum[1],
        small_sum[2],
        small_sum[3],
    )


def solution(mesh):
    own = P(("seg", "mlp"), None, None)
    square, forward, small = P("seg", None), P("seg", "mlp"), P("seg")
    return jax.shard_map(
        functools.partial(shards, mesh.shape["mlp"]),
        mesh=mesh,
        in_specs=(own, own, P(("seg", "mlp")))
        + (square,) * 8
        + (forward,) * 2
        + (small,) * 4
        + (own, own),
        out_specs=(own,) * 4 + (square,) * 8 + (forward,) * 2 + (small,) * 4,
        check_vma=False,
    )
```

time: 1330 us -> 754 us (0.57)
  matrix products: 404 us -> 0 us
  Pallas kernels: 479 us -> 723 us
  local copies, waits for them, and re-layouts: 205 us -> 17.8 us
  other arithmetic: 173 us -> 0.81 us
  loops' own time: 59.4 us -> 0 us
    dot_general x71 -> x0, matrix products: 404 us -> none  [the longest x16 81.3 us: matmul(): return jnp.dot(left, right, preferred_element_type=jnp.float32)]
    pallas_call x0 -> x10, Pallas kernels: none -> 252 us  [the longest x1 68.3 us: feed_forward(): pl.pallas_call(feed_forward_kernel, grid=(parts * each,), in_specs=[pl.Bl...]
    convert_element_type x15 -> x1, other arithmetic: 65.8 us -> 0.01 us  [shards(): gains = gains.transpose(1, 0, 2).reshape(4, 1, width).astype(F32)]
    another operation x2 -> x0, loops' own time: 59.4 us -> none  [the longest x1 31.4 us: shards(): lax.scan(backward_step, (final_state_cotangent[0].astype(jnp.float32), ze...]
    while x205 -> x0, local copies, waits for them, and re-layouts: 54 us -> none
    reduce_sum x13 -> x0, other arithmetic: 41.3 us -> none  [the longest x4 27.8 us: attend_forward(): row_total = jnp.sum(weights, axis=-1, keepdims=True)]
    slice x24 -> x2, local copies, waits for them, and re-layouts: 28.5 us -> 0.86 us  [the longest x1 0.77 us: shards(): small_sum = small_sum[:lines].reshape(4, rows)]
    dynamic_update_slice x12 -> x0, local copies, waits for them, and re-layouts: 24.2 us -> none  [the longest x8 24 us: shards(): lax.scan(forward_step, (state_start, zero_block, zero_block), (seg_tokens...]
where the time goes in v2:
time: 754 us; the launch traced here: 744 us
  Pallas kernels  723 us (96%)
  local copies, waits for them, and re-layouts  17.8 us (2%)
    pallas_call x2, Pallas kernels, scatter_call(): pl.pallas_call(kernel, out_shape=[jax.ShapeDtypeStruct(grad.shape[-2:], j...  253 us
    pallas_call x1, Pallas kernels, gather_call(): pl.pallas_call(kernel, out_shape=shapes, in_specs=[anywhere] * count, out...  219 us
    pallas_call x1, Pallas kernels, feed_forward(): pl.pallas_call(feed_forward_kernel, grid=(parts * each,), in_specs=[pl.Bl...  68.3 us
    pallas_call x1, Pallas kernels, token_backward(): pl.pallas_call(token_backward_kernel, grid=(pairs,), in_specs=[pl.BlockSp...  38.1 us
    pallas_call x1, Pallas kernels, state_backward(): pl.pallas_call(state_backward_kernel, grid=(blocks, pairs), in_specs=[pl....  34.4 us
    pallas_call x3, Pallas kernels, weight_grad(): pl.pallas_call(functools.partial(weight_grad_kernel, count), grid=(rights...  29.6 us
    pallas_call x1, Pallas kernels, token_forward(): pl.pallas_call(token_forward_kernel, grid=(pairs,), in_specs=[pl.BlockSpe...  28.2 us
    pallas_call x1, Pallas kernels, state_forward(): pl.pallas_call(state_forward_kernel, grid=(blocks, pairs), in_specs=[pl.B...  27.8 us

profile of v2, /device:TPU:0, one launch (start us, length us, event | category | flops | bytes accessed | tf_op | source)
XLA Modules:
  0.0 743.5 jit_solution(16163859320809871089)
XLA Ops:
  1.3 0.8 maximum_bitcast_fusion
  2.1 0.6 pad.8.refs_0_
  2.7 218.8 %gather_weights.1 = (bf16[4,2,2,16,128]{4,3,2,1,0:T(8,128)(2,1)}, bf16[4,2,2,64,1024]{4,3,2,1,0:T(8,128)(2,1)}, bf16[4,2,2,64,1024]{4,3,2,1,0:T(8,128)(2,1)}, bf...) custom-call(bf16[16,128]{1,0:T(8,128)(2,1)} %pad.8.refs_0_, ...), custom_call_target="tpu_custom_call" | custom-call | tf_op jit(solution)/shard_map/gather_weights/pallas_call | solution.py:289
  221.5 0.9 copy.41
  222.4 0.1 reshape.165
  222.5 0.1 slice_reduce_fusion
  222.6 0.7 squeeze.41.gate_bias
  223.2 0.7 squeeze.40.gain
  223.9 0.7 squeeze.38.gain_ref.gain
  224.6 0.7 squeeze.37.gain
  225.2 11.5 %project_tokens.1 = (bf16[1024,1024]{1,0:T(8,128)(2,1)}, bf16[1024,1024]{1,0:T(8,128)(2,1)}, bf16[1024,1024]{1,0:T(8,128)(2,1)}, bf16[1024,1024]{1,0:T(8,128)(2,1)}) custom-call(bf16[1024,1024]{1,0:T(8,128)(2,1)} %bitcast.46, f32[1,1024]{1,0:T(1,128)} %squeeze.38.gain_ref.gain, bf16[1024,1024]{1,0:T(8,128)(2,1)} %bitcast.55, bf16[1024,1024]{1,0:T(8,128)(2,1)} %bitcast.57, ...), custom_call_target="tpu_custom_call" | custom-call | tf_op jit(solution)/shard_map/project_tokens/pallas_call | solution.py:426
  236.7 27.8 %state_forward.1 = (bf16[1024,1024]{1,0:T(8,128)(2,1)}, bf16[1024,1024]{1,0:T(8,128)(2,1)}, bf16[1024,1024]{1,0:T(8,128)(2,1)}, bf16[1024,1024]{1,0:T(8,128)(2,1...) custom-call(s32[1]{0:T(128)S(6)} %copy.52.valid, ...), custom_call_target="tpu_custom_call" | custom-call | tf_op jit(solution)/shard_map/state_forward/pallas_call | solution.py:548
  264.5 28.2 %token_forward.1 = (bf16[1024,1024]{1,0:T(8,128)(2,1)}, f32[4,2,1024]{2,1,0:T(2,128)}, f32[1024,1024]{1,0:T(8,128)}, bf16[1024,1024]{1,0:T(8,128)(2,1)}) custom-call(s32[1]{0:T(128)S(6)} %copy.52.valid, bf16[1024,1024]{1,0:T(8,128)(2,1)} %bitcast.47, f32[1,1024]{1,0:T(1,128)} %squeeze.37.gain, bf16[1024,1024]{1,0:T(8,128)(2,1)} %get-tuple-element.88.q, ...), custom_call_target="tpu_custom_call" | custom-call | tf_op jit(solution)/shard_map/token_forward/pallas_call | solution.py:612
  292.7 68.3 %feed_forward.1 = (bf16[1024,1024]{1,0:T(8,128)(2,1)}, f32[1024,1024]{1,0:T(8,128)}, bf16[1024,1024]{1,0:T(8,128)(2,1)}, f32[1,1024]{1,0:T(1,128)}, bf16[2,1024,...) custom-call(s32[1]{0:T(128)S(6)} %copy.52.valid, f32[1024,1024]{1,0:T(8,128)} %get-tuple-element.98.resid, ...), custom_call_target="tpu_custom_call" | custom-call | tf_op jit(solution)/shard_map/feed_forward/pallas_call | solution.py:684
  361.0 131.9 %scatter_forward.1 = (f32[64,2048]{1,0:T(8,128)}, f32[64,2048]{1,0:T(8,128)}) custom-call(bf16[2,4,2,2,64,2048]{5,4,3,2,1,0:T(8,128)(2,1)} %bitcast.53, bf16[2,4,2,2,64,2048]{5,4,3,2,1,0:T(8,128)(2,1)} %bitcast.54), custom_call_target="tpu_custom_call" | custom-call | tf_op jit(solution)/shard_map/scatter_forward/pallas_call | solution.py:350
  492.9 38.1 %token_backward.1 = (bf16[1024,1024]{1,0:T(8,128)(2,1)}, f32[1024,1024]{1,0:T(8,128)}, f32[1024,1024]{1,0:T(8,128)}, bf16[1024,1024]{1,0:T(8,128)(2,1)}, bf16[10...) custom-call(s32[1]{0:T(128)S(6)} %copy.52.valid, bf16[1024,1024]{1,0:T(8,128)(2,1)} %get-tuple-element.105.grad, ...), custom_call_target="tpu_custom_call" | custom-call | tf_op jit(solution)/shard_map/token_backward/pallas_call | solution.py:759
  531.1 34.4 %state_backward.1 = (bf16[1024,1024]{1,0:T(8,128)(2,1)}, bf16[1024,1024]{1,0:T(8,128)(2,1)}, bf16[1024,1024]{1,0:T(8,128)(2,1)}, bf16[1024,1024]{1,0:T(8,128)(2,...) custom-call(s32[1]{0:T(128)S(6)} %copy.52.valid, bf16[512,1024]{1,0:T(8,128)(2,1)} %bitcast.79, ...), custom_call_target="tpu_custom_call" | custom-call | tf_op jit(solution)/shard_map/state_backward/pallas_call | solution.py:860
  565.5 13.9 %token_grad.1 = (f32[1024,1024]{1,0:T(8,128)}, f32[1,1024]{1,0:T(1,128)}) custom-call(bf16[1024,1024]{1,0:T(8,128)(2,1)} %bitcast.48, f32[1,1024]{1,0:T(1,128)} %squeeze.38.gain_ref.gain, f32[1024,1024]{1,0:T(8,128)} %get-tuple-element.104.grad_resid, bf16[1024,1024]{1,0:T(8,128)(2,1)} %get-tuple-element.108.dq.refs_0_, ...), custom_call_target="tpu_custom_call" | custom-call | tf_op jit(solution)/shard_map/token_grad/pallas_call | solution.py:911
  579.3 6.7 weight_grad_update.1
  586.1 0.0 copy-start.9
  586.1 11.4 %weight_grad_state.1 = (bf16[1024,1024]{1,0:T(8,128)(2,1)}, bf16[1024,1024]{1,0:T(8,128)(2,1)}, bf16[1024,1024]{1,0:T(8,128)(2,1)}) custom-call(bf16[1024,1024]{1,0:T(8,128)(2,1)} %get-tuple-element.128.left, bf16[1024,1024]{1,0:T(8,128)(2,1)} %get-tuple-element.129.refs_0_, bf16[1024,1024]{1,0:T(8,128)(2,1)} %get-tuple-element.116.dsk.refs_1_, ...), custom_call_target="tpu_custom_call" | custom-call | tf_op jit(solution)/shard_map/weight_grad_state/pallas_call | solution.py:940
  597.5 0.0 copy-done.6
  597.5 0.0 copy-done.7
  597.5 0.0 copy-done.8
  597.5 0.0 copy-done.9
  597.6 0.1 reshape.151
  597.7 0.1 reshape.152
  597.8 0.6 pad.9
  598.4 11.4 %weight_grad_tokens.1 = (bf16[1024,1024]{1,0:T(8,128)(2,1)}, bf16[1024,1024]{1,0:T(8,128)(2,1)}, bf16[1024,1024]{1,0:T(8,128)(2,1)}) custom-call(bf16[1024,1024]{1,0:T(8,128)(2,1)} %get-tuple-element.133.left, bf16[1024,1024]{1,0:T(8,128)(2,1)} %get-tuple-element.108.dq.refs_0_, bf16[1024,1024]{1,0:T(8,128)(2,1)} %get-tuple-element.118.dk.refs_1_, ...), custom_call_target="tpu_custom_call" | custom-call | tf_op jit(solution)/shard_map/weight_grad_tokens/pallas_call | solution.py:940
  609.8 120.8 %scatter_rest.1 = (f32[8,128]{1,0:T(8,128)}, f32[64,1024]{1,0:T(8,128)}, f32[64,1024]{1,0:T(8,128)}, f32[64,1024]{1,0:T(8,128)}, f32[64,1024]{1,0:T(8,128)}, /*i...) custom-call(f32[4,2,2,8,128]{4,3,2,1,0:T(8,128)} %bitcast.80, ...), custom_call_target="tpu_custom_call" | custom-call | tf_op jit(solution)/shard_map/scatter_rest/pallas_call | solution.py:350
  730.7 0.0 copy-start.5
  730.7 0.0 copy-start.4
  730.7 0.0 copy-start.3
  730.7 0.8 slice.39
  731.5 0.1 reshape.164
  731.5 0.5 slice_bitcast_fusion
  732.1 1.7 copy.53
  733.8 1.7 copy.54
  735.5 1.7 copy.55
  737.2 1.7 copy.56
  738.9 0.7 copy.57
  739.6 0.0 copy-done.4
  739.6 0.7 copy.58
  740.3 0.7 copy.59
  741.0 0.0 copy-done.2
  741.0 0.7 copy.60
  741.7 0.8 copy.61
  742.5 0.8 copy.62
  (13 shorter events, 0.1 us)
Async XLA Ops:
  586.1 11.5 %copy-start.6 = (f32[1,1024]{1,0:T(1,128)S(1)}, f32[1,1024]{1,0:T(1,128)}, u32[]{:S(2)}) copy-start(f32[1,1024]{1,0:T(1,128)} %get-tuple-element.124) | copy-start | bytes 12292
  586.1 11.5 %copy-start.7 = (f32[1,1024]{1,0:T(1,128)S(1)}, f32[1,1024]{1,0:T(1,128)}, u32[]{:S(2)}) copy-start(f32[1,1024]{1,0:T(1,128)} %get-tuple-element.123) | copy-start | bytes 12292
  586.1 11.5 %copy-start.8 = (f32[1,1024]{1,0:T(1,128)S(1)}, f32[1,1024]{1,0:T(1,128)}, u32[]{:S(2)}) copy-start(f32[1,1024]{1,0:T(1,128)} %get-tuple-element.125) | copy-start | bytes 12292
  586.1 11.5 %copy-start.9 = (f32[1,1024]{1,0:T(1,128)S(1)}, f32[1,1024]{1,0:T(1,128)}, u32[]{:S(2)}) copy-start(f32[1,1024]{1,0:T(1,128)} %get-tuple-element.122) | copy-start | bytes 12292
  730.7 8.2 %copy-start.5 = (f32[64,1024]{1,0:T(8,128)S(1)}, f32[64,1024]{1,0:T(8,128)}, u32[]{:S(2)}) copy-start(f32[64,1024]{1,0:T(8,128)} %get-tuple-element.184) | copy-start | bytes 786436
  730.7 8.9 %copy-start.4 = (f32[64,1024]{1,0:T(8,128)S(1)}, f32[64,1024]{1,0:T(8,128)}, u32[]{:S(2)}) copy-start(f32[64,1024]{1,0:T(8,128)} %get-tuple-element.185) | copy-start | bytes 786436
  730.7 9.6 %copy-start.3 = (f32[64,1024]{1,0:T(8,128)S(1)}, f32[64,1024]{1,0:T(8,128)}, u32[]{:S(2)}) copy-start(f32[64,1024]{1,0:T(8,128)} %get-tuple-element.186) | copy-start | bytes 786436
  730.7 10.3 %copy-start.2 = (f32[64,1024]{1,0:T(8,128)S(1)}, f32[64,1024]{1,0:T(8,128)}, u32[]{:S(2)}) copy-start(f32[64,1024]{1,0:T(8,128)} %get-tuple-element.187) | copy-start | bytes 786436
  732.1 9.6 %copy-start.1 = (f32[64,2048]{1,0:T(8,128)S(1)}, f32[64,2048]{1,0:T(8,128)}, u32[]{:S(2)}) copy-start(f32[64,2048]{1,0:T(8,128)} %get-tuple-element.188) | copy-start | bytes 1572868
  735.5 7.0 copy-start

commit v3 on v2

v3 whole, which is shorter than its diff:
```python
import functools
import jax
import jax.numpy as jnp
from jax import lax
from jax.experimental import pallas as pl
from jax.experimental.pallas import tpu as pltpu
from jax.sharding import PartitionSpec as P

BF16 = jnp.bfloat16
F32 = jnp.float32
VMEM_LIMIT = 60 << 20
SQUARE_PIECES = 4
FORWARD_PIECES = 2


class Place:
    def __init__(self, sizes):
        seg = lax.axis_index("seg")
        self.sizes = sizes
        self.at = {
            "z": lax.div(seg, 4),
            "x": lax.rem(lax.div(seg, 2), 2),
            "c": lax.rem(seg, 2),
            "m": lax.axis_index("mlp"),
        }

    def device(self, moved):
        at = {**self.at, **moved}
        return (at["z"] * 4 + at["x"] * 2 + at["c"], at["m"])

    def ahead(self, axis, step):
        return lax.rem(self.at[axis] + step, self.sizes[axis])

    def behind(self, axis, step):
        return lax.rem(self.at[axis] + self.sizes[axis] - step, self.sizes[axis])

    def greet(self):
        barrier = pltpu.get_barrier_semaphore()
        count = 0
        for axis in "zxcm":
            for step in range(1, self.sizes[axis]):
                pl.semaphore_signal(
                    barrier,
                    inc=1,
                    device_id=self.device({axis: self.ahead(axis, step)}),
                    device_id_type=pl.DeviceIdType.MESH,
                )
                count += 1
        pl.semaphore_wait(barrier, count)


class Flow:
    def __init__(self, place, send, recv, taken):
        self.place, self.send, self.recv, self.taken = place, send, recv, taken
        self.steps, self.arriving, self.sent = [], [], []

    def move(self, actions, make):
        pair = self.taken[0]
        self.taken[0] += 1

        def copy(source, target, moved):
            return pltpu.make_async_remote_copy(
                src_ref=source,
                dst_ref=target,
                send_sem=self.send.at[pair],
                recv_sem=self.recv.at[pair],
                device_id=self.place.device(moved),
                device_id_type=pl.DeviceIdType.MESH,
            )

        def outgoing():
            source, target, moved, _ = make()
            return copy(source, target, moved)

        def incoming():
            _, _, moved, landing = make()
            return copy(landing, landing, moved)

        actions.append(lambda: outgoing().start())
        self.sent.append(lambda: outgoing().wait_send())
        self.arriving.append(lambda: incoming().wait_recv())

    def arrived(self):
        waits, self.arriving = self.arriving, []
        return waits


def gather_steps(flow, source, target, order, split, columns, local_sem, begin, end):
    place = flow.place
    at, sizes = place.at, place.sizes
    lead = ("m" if len(target.shape) == 6 else "") + "zxc"
    first_column, width = columns
    share = width // sizes["m"] if split else width

    def block(done, moved):
        if not split or "m" in done:
            lanes = pl.ds(first_column, width)
        else:
            lanes = pl.ds(pl.multiple_of(first_column + moved.get("m", at["m"]) * share, 128), share)
        return (pl.ds(0, source.shape[0]), lanes)

    def view(done, **moved):
        index = tuple(
            moved[a] if a in moved else pl.ds(0, sizes[a]) if a in done else at[a] for a in lead
        )
        return target.at[index + block(done, moved)]

    def own_source():
        return source.at[block("", {})]

    def own():
        return pltpu.make_async_copy(own_source(), view(""), local_sem)

    waits = []
    for i, axis in enumerate(order + "c"):
        done = order[:i]
        if not begin <= i < end:
            continue
        actions = flow.arrived() + waits
        waits = []
        if i == 0:
            actions.append(lambda: own().start())
            waits.append(lambda: own().wait())
        for step in range(1, sizes[axis]):

            def make(axis=axis, step=step, done=done):
                return (
                    view(done) if done else own_source(),
                    view(done),
                    {axis: place.ahead(axis, step)},
                    view(done, **{axis: place.behind(axis, step)}),
                )

            flow.move(actions, make)
        flow.steps.append(actions)
    flow.last = flow.arrived() + waits + flow.sent


def add_into(total, term):
    lead = total.shape[:-2]

    def body(i, carry):
        index, rest = [], i
        for size in reversed(lead):
            index.append(lax.rem(rest, size))
            rest = lax.div(rest, size)
        there = tuple(reversed(index)) + (Ellipsis,)
        total[there] = total[there] + term[there]
        return carry

    lax.fori_loop(0, functools.reduce(lambda a, b: a * b, lead, 1), body, 0)


def scatter_shapes(grad_shape, order, split, columns, sizes):
    lead = ("m" if len(grad_shape) == 6 else "") + "zx"
    rows, width = grad_shape[-2], columns[1]

    def left(done):
        share = width // sizes["m"] if split and "m" in done else width
        return tuple(sizes[a] for a in lead if a not in done) + (rows, share)

    shapes = [left(""), left("")]
    for i, axis in enumerate(order):
        shapes.append((sizes[axis] - 1,) + left(order[: i + 1]))
    if "m" not in lead:
        shapes.append((rows, width) if split else (sizes["m"], rows, width))
    return shapes


def scatter_steps(flow, grad, result, buffers, order, split, columns, local_sem):
    place = flow.place
    at, sizes = place.at, place.sizes
    whole_m = len(grad.shape) == 6
    lead = ("m" if whole_m else "") + "zx"
    own, core_in = buffers[:2]
    landing = dict(zip(order, buffers[2:]))
    last = buffers[-1]
    rows, width = grad.shape[-2], columns[1]
    share = width // sizes["m"] if split else width

    def lanes_of(place_m):
        return pl.ds(pl.multiple_of(place_m * share, 128), share)

    def grad_half(core):
        return grad.at[
            tuple(pl.ds(0, sizes[a]) for a in lead) + (core, pl.ds(0, rows), pl.ds(*columns))
        ]

    def view(done, **moved):
        index = tuple(
            moved[a] if a in moved else at[a] if a in done else pl.ds(0, sizes[a]) for a in lead
        )
        lanes = pl.ds(0, width)
        if split and ("m" in done or "m" in moved):
            lanes = lanes_of(moved.get("m", at["m"]))
        return own.at[index + (pl.ds(0, rows), lanes)]

    def load():
        return pltpu.make_async_copy(grad_half(at["c"]), own, local_sem)

    actions = [lambda: load().start()]
    flow.move(actions, lambda: (grad_half(1 - at["c"]), core_in, {"c": 1 - at["c"]}, core_in))
    flow.steps.append(actions)
    actions = [lambda: load().wait()] + flow.arrived() + [lambda: add_into(own, core_in)]
    done = ""
    for axis in order:
        for step in range(1, sizes[axis]):

            def make(axis=axis, step=step, done=done):
                there = place.ahead(axis, step)
                slot = landing[axis].at[step - 1]
                return (view(done, **{axis: there}), slot, {axis: there}, slot)

            flow.move(actions, make)
        flow.steps.append(actions)
        done += axis
        actions = flow.arrived()
        for step in range(1, sizes[axis]):
            actions.append(
                lambda axis=axis, step=step, done=done: add_into(
                    view(done), landing[axis].at[step - 1]
                )
            )
    block = (pl.ds(0, rows), pl.ds(*columns))
    if whole_m:

        def store():
            result[block] = view(done)[...].astype(F32)

        actions.append(store)
    elif split:

        def part(place_m):
            return last.at[pl.ds(0, rows), lanes_of(place_m)]

        def keep():
            part(at["m"])[...] = view(done)[...]

        actions.append(keep)
        for step in range(1, sizes["m"]):
            flow.move(
                actions,
                lambda step=step: (
                    part(at["m"]),
                    part(at["m"]),
                    {"m": place.ahead("m", step)},
                    part(place.behind("m", step)),
                ),
            )
        flow.steps.append(actions)
        actions = flow.arrived()

        def store():
            result[block] = last[...].astype(F32)

        actions.append(store)
    else:

        def keep():
            last[at["m"]] = view(done)[...]

        actions.append(keep)
        for step in range(1, sizes["m"]):
            flow.move(
                actions,
                lambda step=step: (
                    last.at[at["m"]],
                    last.at[at["m"]],
                    {"m": place.ahead("m", step)},
                    last.at[place.behind("m", step)],
                ),
            )
        flow.steps.append(actions)
        actions = flow.arrived()

        def store():
            total = last[0].astype(F32)
            for i in range(1, sizes["m"]):
                total = total + last[i].astype(F32)
            result[block] = total

        actions.append(store)
    flow.last = actions + flow.sent


class Gather:
    def __init__(self, sizes, arrays, units, together):
        self.sizes, self.arrays, self.units = sizes, arrays, units
        self.targets = [None] * len(arrays)
        self.starts, self.round = [], 0
        for start, count in enumerate(together):
            self.starts += [start] * count
        assert len(self.starts) == len(units)

    def ready(self, names):
        return max(
            start + len(unit[1]) + 1 for start, unit in zip(self.starts, self.units) if unit[0] in names
        )

    def until(self, end, collective_id):
        begin, self.round = self.round, max(end, self.round)
        return GatherPart(self, begin, end, collective_id) if begin < end else None


class GatherPart:
    def __init__(self, plan, begin, end, collective_id):
        self.plan, self.begin, self.end, self.collective_id = plan, begin, end, collective_id
        self.units = [
            (start, unit)
            for start, unit in zip(plan.starts, plan.units)
            if start < end and start + len(unit[1]) + 1 > begin
        ]
        self.names = sorted({unit[0] for _, unit in self.units})
        split = {unit[0]: unit[2] for _, unit in self.units}
        order = {unit[0]: unit[1] for _, unit in self.units}
        sizes = plan.sizes
        anywhere = pl.BlockSpec(memory_space=pl.ANY)
        old = [n for n in self.names if plan.targets[n] is not None]
        self.arrays = [plan.arrays[n] for n in self.names] + [plan.targets[n] for n in old]
        self.specs = [anywhere] * len(self.arrays)
        self.out_shape = [
            jax.ShapeDtypeStruct(
                ((sizes["m"],) if "m" in order[n] and not split[n] else ())
                + (sizes["z"], 2, 2)
                + plan.arrays[n].shape,
                plan.arrays[n].dtype,
            )
            for n in self.names
        ]
        self.out_specs = [anywhere] * len(self.names)
        self.aliases = {len(self.names) + i: self.names.index(n) for i, n in enumerate(old)}
        pairs = len(self.units) * (sum(sizes.values()) - 4)
        self.scratch = [
            pltpu.SemaphoreType.DMA((pairs,)),
            pltpu.SemaphoreType.DMA((pairs,)),
            pltpu.SemaphoreType.DMA((len(self.units),)),
        ]

    def rounds(self, ins, outs, scratch):
        place = Place(self.plan.sizes)
        send, recv, local = scratch
        taken = [0]
        rounds = [[] for _ in range(self.end - self.begin)]
        last = []
        for i, (start, (n, order, split, columns)) in enumerate(self.units):
            flow = Flow(place, send, recv, taken)
            begin = max(self.begin - start, 0)
            slot = self.names.index(n)
            gather_steps(
                flow, ins[slot], outs[slot], order, split, columns, local.at[i], begin, self.end - start
            )
            for step, actions in enumerate(flow.steps):
                rounds[start + begin + step - self.begin] += actions
            last += flow.last
        rounds[0].insert(0, place.greet)
        return rounds, last

    def received(self, outs):
        for n, out in zip(self.names, outs):
            self.plan.targets[n] = out


class Scatter:
    aliases = {}

    def __init__(self, sizes, arrays, units, together, collective_id):
        self.sizes, self.arrays, self.units = sizes, arrays, units
        self.collective_id = collective_id
        self.starts = []
        for start, count in enumerate(together):
            self.starts += [start] * count
        assert len(self.starts) == len(units)
        self.specs = [pl.BlockSpec(memory_space=pl.ANY)] * len(arrays)
        self.out_shape = [jax.ShapeDtypeStruct(a.shape[-2:], F32) for a in arrays]
        self.out_specs = [
            pl.BlockSpec(a.shape[-2:], lambda *_: (0, 0), pipeline_mode=pl.Buffered(1)) for a in arrays
        ]
        buffers = []
        for i, order, split, columns in units:
            buffers += [
                pltpu.VMEM(shape, arrays[i].dtype)
                for shape in scatter_shapes(arrays[i].shape, order, split, columns, sizes)
            ]
        pairs = len(units) * (sum(sizes.values()) - 4 + sizes["m"] - 1)
        self.scratch = buffers + [
            pltpu.SemaphoreType.DMA((pairs,)),
            pltpu.SemaphoreType.DMA((pairs,)),
            pltpu.SemaphoreType.DMA((len(units),)),
        ]

    def rounds(self, ins, outs, scratch):
        place = Place(self.sizes)
        send, recv, local = scratch[-3:]
        buffers = list(scratch[:-3])
        taken, flows, last = [0], [], []
        for unit, (i, order, split, columns) in enumerate(self.units):
            flow = Flow(place, send, recv, taken)
            count = len(scatter_shapes(ins[i].shape, order, split, columns, self.sizes))
            mine, buffers = buffers[:count], buffers[count:]
            scatter_steps(flow, ins[i], outs[i], mine, order, split, columns, local.at[unit])
            flows.append(flow)
        rounds = [[] for _ in range(max(s + len(f.steps) for s, f in zip(self.starts, flows)) + 1)]
        for start, flow in zip(self.starts, flows):
            for i, actions in enumerate(flow.steps + [flow.last]):
                rounds[start + i] += actions
        rounds[0].insert(0, place.greet)
        return rounds[:-1], rounds[-1]

    def received(self, outs):
        self.sums = outs


def run_all(actions):
    for action in actions:
        action()


def run_kernel(
    body, args, *, grid, in_specs, out_specs, out_shape, name, scratch_shapes=(), exchange=None, polls=1
):
    if exchange is None:
        return pl.pallas_call(
            functools.partial(body, lambda: None),
            grid=grid,
            in_specs=in_specs,
            out_specs=out_specs,
            out_shape=out_shape,
            scratch_shapes=scratch_shapes,
            compiler_params=pltpu.CompilerParams(vmem_limit_bytes=VMEM_LIMIT),
            name=name,
        )(*args)
    counts = (len(args), len(exchange.arrays), len(out_shape), len(exchange.out_shape))
    total = functools.reduce(lambda a, b: a * b, grid, 1)

    def kernel(*refs):
        refs = list(refs)
        ins, sent, outs, received = [[refs.pop(0) for _ in range(n)] for n in counts]
        own = [refs.pop(0) for _ in range(len(scratch_shapes))]
        step = 0
        for i, size in enumerate(grid):
            step = step * size + pl.program_id(i)
        rounds, last = exchange.rounds(sent, received, refs)
        slots = {}
        for i, actions in enumerate(rounds):
            slot = i * total * polls // len(rounds)
            slots.setdefault((slot % polls, slot // polls), []).extend(actions)
        called = [0]

        def poll():
            for at_step in range(total):
                actions = slots.get((called[0], at_step))
                if actions:
                    pl.when(step == at_step)(functools.partial(run_all, actions))
            called[0] += 1

        body(poll, *ins, *outs, *own)
        assert called[0] == polls
        pl.when(step == total - 1)(functools.partial(run_all, last))

    outs = pl.pallas_call(
        kernel,
        grid=grid,
        in_specs=list(in_specs) + exchange.specs,
        out_specs=list(out_specs) + exchange.out_specs,
        out_shape=list(out_shape) + exchange.out_shape,
        scratch_shapes=list(scratch_shapes) + exchange.scratch,
        input_output_aliases={counts[0] + i: counts[2] + o for i, o in exchange.aliases.items()},
        compiler_params=pltpu.CompilerParams(
            vmem_limit_bytes=VMEM_LIMIT,
            collective_id=exchange.collective_id,
            has_side_effects=True,
        ),
        name=name,
    )(*args, *exchange.arrays)
    exchange.received(outs[counts[2] :])
    return outs[: counts[2]]


def exchange_alone(exchange, name):
    run_kernel(
        lambda poll: poll(), [], grid=(1,), in_specs=[], out_specs=[], out_shape=[], name=name,
        exchange=exchange,
    )


HEAD = 128
BLOCK = 512
EPS = 1e-06
NEGATIVE = -1e30
GELU_C = 0.7978845608
GELU_K = 0.044715
SCALE = HEAD**-0.5
LOG2E = 1.4426950408889634
PAIR = 2 * HEAD
TILE = 256


def matmul(left, right):
    return jnp.dot(left, right, preferred_element_type=F32)


def matmul_nt(left, right):
    return lax.dot_general(left, right, (((1,), (1,)), ((), ())), preferred_element_type=F32)


def inverse_rms(values):
    return lax.rsqrt(jnp.mean(values * values, axis=-1, keepdims=True) + EPS)


def rms_backward(values, gain, grad):
    inverse = inverse_rms(values)
    unit = values * inverse
    weighted = grad * gain
    inner = jnp.mean(weighted * unit, axis=-1, keepdims=True)
    return inverse * (weighted - unit * inner), grad * unit


def whole(shape):
    return pl.BlockSpec(shape, lambda *_: (0,) * len(shape))


def project_kernel(poll, x_ref, gain_ref, wq, wk, wv, normed, q, k, v):
    @pl.when(pl.program_id(0) == 0)
    def _():
        x = x_ref[...].astype(F32)
        normed[...] = (x * inverse_rms(x) * gain_ref[...]).astype(BF16)

    poll()
    rows = normed[...]
    for weight, out in ((wq, q), (wk, k), (wv, v)):
        out[...] = matmul(rows, weight[...]).astype(BF16)


def project(x, gain, weights, exchange):
    rows, width = x.shape
    tile = pl.BlockSpec((width, TILE), lambda j: (0, j))
    out = pl.BlockSpec((rows, TILE), lambda j: (0, j))
    return run_kernel(
        project_kernel,
        (x, gain, *weights),
        grid=(width // TILE,),
        in_specs=[whole((rows, width)), whole((1, width)), tile, tile, tile],
        out_specs=[whole((rows, width)), out, out, out],
        out_shape=[jax.ShapeDtypeStruct((rows, width), BF16)] * 4,
        name="project_tokens",
        exchange=exchange,
    )


def attend(query, pieces):
    scores = []
    for keys, _, mask in pieces:
        score = matmul_nt(keys, query) * (SCALE * LOG2E)
        scores.append(score if mask is None else jnp.where(mask, score, NEGATIVE))
    top = functools.reduce(jnp.maximum, [jnp.max(s, axis=0, keepdims=True) for s in scores])
    total, mixed = 0.0, 0.0
    for score, (_, values, _) in zip(scores, pieces):
        weights = jnp.exp2(score - top)
        total = total + jnp.sum(weights, axis=0, keepdims=True)
        mixed = mixed + matmul(values.T, weights.astype(BF16))
    return (mixed / total).T.astype(BF16), top + jnp.log2(total)


def attend_backward(query, log_total, grad, centre, pieces):
    grad_query = 0.0
    for keys, values, mask, add_keys, add_values in pieces:
        score = matmul_nt(keys, query) * (SCALE * LOG2E)
        if mask is not None:
            score = jnp.where(mask, score, NEGATIVE)
        probs = jnp.exp2(score - log_total)
        add_values(matmul(probs.astype(BF16), grad))
        grad_probs = matmul_nt(values, grad)
        grad_scores = (probs * (grad_probs - centre)).astype(BF16)
        add_keys(matmul(grad_scores, query) * SCALE)
        grad_query = grad_query + matmul(keys.T, grad_scores)
    return (grad_query * SCALE).T


def centre_of(grad, mixed):
    return jnp.sum((grad.astype(F32) * mixed.astype(F32)).T, axis=0, keepdims=True)


def position(shape, axis):
    return lax.broadcasted_iota(jnp.int32, shape, axis)


def token_pieces(block, half, valid):
    key = position((TILE, TILE), 0)
    query = position((TILE, TILE), 1)
    causal, recent = key <= query, key > query
    pieces = []
    if block:
        start = (block - 1) * BLOCK
        pieces.append(("near", start + half * TILE, TILE, recent))
        if half == 0:
            pieces.append(("near", start + TILE, TILE, None))
    start = block * BLOCK
    for piece in range(half + 1):
        first = start + piece * TILE
        seen = first + key < valid
        mask = causal if piece == half else None
        if block:
            mask = seen if mask is None else mask & seen
        pieces.append(("near", first, TILE, mask))
    pieces.append(("state", block * BLOCK, BLOCK, None))
    return pieces


def state_forward_kernel(
    poll, valid, s0, gain, gate_bias, wq, wk, wv, wu, k, v,
    normed_out, sq, sk, sv, read, log_out, update_out, states, last,
    state, normed, total,
):
    block, pair = pl.program_id(0), pl.program_id(1)

    @pl.when((block == 0) & (pair == 0))
    def _():
        state[...] = s0[...].astype(F32)

    @pl.when(pair == 0)
    def _():
        now = state[...]
        rows = (now * inverse_rms(now) * gain[...]).astype(BF16)
        normed[...] = rows
        normed_out[...] = rows
        states[...] = now
        total[...] = jnp.zeros_like(total)

    poll()
    rows = normed[...]
    for weight, out in ((wq, sq), (wk, sk), (wv, sv)):
        out[...] = matmul(rows, weight[...]).astype(BF16)
    seen = block * BLOCK + position((BLOCK, BLOCK), 0) < valid[0]
    for head in range(2):
        lanes = pl.ds(head * HEAD, HEAD)
        read[:, lanes], log_out[0, 0, pl.ds(head, 1), :] = attend(
            sq[:, lanes], [(k[:, lanes], v[:, lanes], seen)]
        )
    total[...] += matmul(read[...], wu[...])

    @pl.when(pair == pl.num_programs(1) - 1)
    def _():
        update = total[...]
        gate = 1.0 / (1.0 + jnp.exp(-gate_bias[...]))
        later = gate * state[...] + (1.0 - gate) * update
        update_out[...] = update
        state[...] = later
        last[...] = later.astype(BF16)


def state_forward(valid, s0, gain, gate_bias, weights, update_weight, k, v, exchange):
    rows, width = s0.shape
    blocks, pairs = k.shape[0] // BLOCK, width // PAIR
    columns = pl.BlockSpec((width, PAIR), lambda b, p: (0, p))
    tile = pl.BlockSpec((rows, PAIR), lambda b, p: (b, p))
    band = pl.BlockSpec((rows, width), lambda b, p: (b, 0))
    small = whole((1, width))

    def stack(kind):
        return jax.ShapeDtypeStruct((blocks * rows, width), kind)

    return run_kernel(
        state_forward_kernel,
        (valid, s0, gain, gate_bias, *weights, update_weight, k, v),
        grid=(blocks, pairs),
        in_specs=[
            pl.BlockSpec(memory_space=pltpu.SMEM), whole((rows, width)), small, small,
            columns, columns, columns, pl.BlockSpec((PAIR, width), lambda b, p: (p, 0)),
            pl.BlockSpec((BLOCK, PAIR), lambda b, p: (b, p)),
            pl.BlockSpec((BLOCK, PAIR), lambda b, p: (b, p)),
        ],
        out_specs=[
            band, tile, tile, tile, tile,
            pl.BlockSpec((1, 1, 2, rows), lambda b, p: (b, p, 0, 0)),
            band, band, whole((rows, width)),
        ],
        out_shape=[
            stack(BF16), stack(BF16), stack(BF16), stack(BF16), stack(BF16),
            jax.ShapeDtypeStruct((blocks, pairs, 2, rows), F32),
            stack(F32), stack(F32), jax.ShapeDtypeStruct((rows, width), BF16),
        ],
        scratch_shapes=[
            pltpu.VMEM((rows, width), F32), pltpu.VMEM((rows, width), BF16),
            pltpu.VMEM((rows, width), F32),
        ],
        name="state_forward",
        exchange=exchange,
    )


def token_forward_kernel(
    poll, valid, x, gain, q, k, v, sk, sv, wo, mixed, log_out, resid, ynorm
):
    pair = pl.program_id(0)

    @pl.when(pair == 0)
    def _():
        resid[...] = x[...].astype(F32)

    count = valid[0]
    for head in range(2):
        poll()
        lanes = pl.ds(head * HEAD, HEAD)
        for block in range(q.shape[0] // BLOCK):
            for half in range(BLOCK // TILE):
                rows = pl.ds(block * BLOCK + half * TILE, TILE)
                pieces = []
                for kind, first, size, mask in token_pieces(block, half, count):
                    keys, values = (k, v) if kind == "near" else (sk, sv)
                    there = pl.ds(first, size)
                    pieces.append((keys[there, lanes], values[there, lanes], mask))
                mixed[rows, lanes], log_out[0, pl.ds(head, 1), rows] = attend(
                    q[rows, lanes], pieces
                )
    resid[...] += matmul(mixed[...], wo[...])

    @pl.when(pair == pl.num_programs(0) - 1)
    def _():
        rows = resid[...]
        ynorm[...] = (rows * inverse_rms(rows) * gain[...]).astype(BF16)


def token_forward(valid, x, gain, q, k, v, sk, sv, wo, exchange):
    rows, width = x.shape
    pairs = width // PAIR
    tile = pl.BlockSpec((rows, PAIR), lambda p: (0, p))
    states = pl.BlockSpec((sk.shape[0], PAIR), lambda p: (0, p))
    return run_kernel(
        token_forward_kernel,
        (valid, x, gain, q, k, v, sk, sv, wo),
        grid=(pairs,),
        in_specs=[
            pl.BlockSpec(memory_space=pltpu.SMEM), whole((rows, width)), whole((1, width)),
            tile, tile, tile, states, states, pl.BlockSpec((PAIR, width), lambda p: (p, 0)),
        ],
        out_specs=[
            tile, pl.BlockSpec((1, 2, rows), lambda p: (p, 0, 0)),
            whole((rows, width)), whole((rows, width)),
        ],
        out_shape=[
            jax.ShapeDtypeStruct((rows, width), BF16),
            jax.ShapeDtypeStruct((pairs, 2, rows), F32),
            jax.ShapeDtypeStruct((rows, width), F32),
            jax.ShapeDtypeStruct((rows, width), BF16),
        ],
        name="token_forward",
        exchange=exchange,
        polls=2,
    )


def feed_forward_kernel(
    first, final, poll, valid, ynorm, cot, total_in, grad_in, up_w, down_w,
    out, grad_out, up_grad, down_grad,
    ynorm_t, masked, masked_t, total, grad_total, sems,
):
    step, last = pl.program_id(0), pl.num_programs(0) - 1
    loads = [pltpu.make_async_copy(total_in, total, sems.at[0])]
    stores = [pltpu.make_async_copy(grad_total, grad_out, sems.at[1])]
    if not first:
        loads.append(pltpu.make_async_copy(grad_in, grad_total, sems.at[1]))
    if not final:
        stores.append(pltpu.make_async_copy(total, out, sems.at[0]))

    poll()

    @pl.when(step == 0)
    def _():
        for copy in loads:
            copy.start()
        keep = position(cot.shape, 0) < valid[0]
        grad = jnp.where(keep, cot[...], jnp.zeros_like(cot))
        masked[...] = grad
        masked_t[...] = grad.T
        ynorm_t[...] = ynorm[...].T
        if first:
            grad_total[...] = jnp.zeros_like(grad_total)

    up_part, down_part = up_w[0], down_w[0]
    up = matmul(ynorm[...], up_part)
    grad_hidden = matmul(masked[...], down_part)
    square = up * up
    bent = jnp.tanh(GELU_C * (up + GELU_K * square * up))
    hidden = (0.5 * up * (1.0 + bent)).astype(BF16)
    slope = 0.5 * (1.0 + bent) + 0.5 * up * (1.0 - bent * bent) * (
        GELU_C * (1.0 + 3.0 * GELU_K * square)
    )
    grad_up = (grad_hidden * slope).astype(BF16)
    poll()
    down_grad[0] = matmul(masked_t[...], hidden).astype(BF16)
    up_grad[0] = matmul(ynorm_t[...], grad_up).astype(BF16)

    @pl.when(step == 0)
    def _():
        for copy in loads:
            copy.wait()

    total[...] += matmul_nt(hidden, down_part)
    grad_total[...] += matmul_nt(grad_up, up_part)

    @pl.when(step == last)
    def _():
        for copy in stores:
            copy.start()
        if final:
            out[...] = total[...].astype(BF16)
        for copy in stores:
            copy.wait()


def feed_forward(first, final, valid, ynorm, cot, total, grad, up_w, down_w, exchange, chunk=512):
    rows, width = ynorm.shape
    parts, _, part = up_w.shape
    chunk = min(chunk, part)
    each = part // chunk
    weight = pl.BlockSpec((1, width, chunk), lambda j: (j // each, 0, j % each))
    once = pl.BlockSpec((rows, width), lambda j: (0, 0), pipeline_mode=pl.Buffered(1))
    anywhere = pl.BlockSpec(memory_space=pl.ANY)
    return run_kernel(
        functools.partial(feed_forward_kernel, first, final),
        (valid, ynorm, cot, total, grad, up_w, down_w),
        grid=(parts * each,),
        in_specs=[
            pl.BlockSpec(memory_space=pltpu.SMEM), once, once, anywhere, anywhere, weight, weight
        ],
        out_specs=[once if final else anywhere, anywhere, weight, weight],
        out_shape=[
            jax.ShapeDtypeStruct((rows, width), BF16 if final else F32),
            jax.ShapeDtypeStruct((rows, width), F32),
            jax.ShapeDtypeStruct(up_w.shape, BF16),
            jax.ShapeDtypeStruct(down_w.shape, BF16),
        ],
        scratch_shapes=[
            pltpu.VMEM((width, rows), BF16), pltpu.VMEM((rows, width), BF16),
            pltpu.VMEM((width, rows), BF16), pltpu.VMEM((rows, width), F32),
            pltpu.VMEM((rows, width), F32), pltpu.SemaphoreType.DMA((2,)),
        ],
        name="feed_forward_final" if final else "feed_forward_first",
        exchange=exchange,
        polls=2,
    )


def token_backward_kernel(
    poll, valid, resid, gain, cot, grad_ynorm, q, k, v, sk, sv, wo, mixed, log_total,
    grad_resid, gain_grad, dq, dk, dv, dsk, dsv, wo_grad,
    rounded, grad_mixed, near_k, near_v, state_k, state_v,
):
    poll()

    @pl.when(pl.program_id(0) == 0)
    def _():
        grad, gain_rows = rms_backward(resid[...], gain[...], grad_ynorm[...])
        keep = position(cot.shape, 0) < valid[0]
        grad = jnp.where(keep, cot[...].astype(F32), 0.0) + grad
        grad_resid[...] = grad
        rounded[...] = grad.astype(BF16)
        gain_grad[...] = jnp.sum(gain_rows, axis=0, keepdims=True)

    grad_rows = rounded[...]
    grad_mixed[...] = matmul_nt(grad_rows, wo[...]).astype(BF16)
    wo_grad[...] = matmul(mixed[...].T, grad_rows).astype(BF16)
    for ref in (near_k, near_v, state_k, state_v):
        ref[...] = jnp.zeros_like(ref)
    count = valid[0]
    for head in range(2):
        poll()
        lanes = pl.ds(head * HEAD, HEAD)

        def adder(ref, there):
            def add(term):
                ref[there, lanes] += term

            return add

        for block in range(q.shape[0] // BLOCK):
            for half in range(BLOCK // TILE):
                rows = pl.ds(block * BLOCK + half * TILE, TILE)
                pieces = []
                for kind, first, size, mask in token_pieces(block, half, count):
                    keys, values = (k, v) if kind == "near" else (sk, sv)
                    sums = (near_k, near_v) if kind == "near" else (state_k, state_v)
                    there = pl.ds(first, size)
                    pieces.append(
                        (keys[there, lanes], values[there, lanes], mask)
                        + tuple(adder(ref, there) for ref in sums)
                    )
                out_grad = grad_mixed[rows, lanes]
                dq[rows, lanes] = attend_backward(
                    q[rows, lanes],
                    log_total[0, pl.ds(head, 1), rows],
                    out_grad,
                    centre_of(out_grad, mixed[rows, lanes]),
                    pieces,
                ).astype(BF16)
    dk[...] = near_k[...]
    dv[...] = near_v[...]
    dsk[...] = state_k[...].astype(BF16)
    dsv[...] = state_v[...].astype(BF16)


def token_backward(
    valid, resid, gain, cot, grad_ynorm, q, k, v, sk, sv, wo, mixed, log_total, exchange
):
    rows, width = resid.shape
    once = pl.BlockSpec((rows, width), lambda p: (0, 0), pipeline_mode=pl.Buffered(1))
    pairs = width // PAIR
    tile = pl.BlockSpec((rows, PAIR), lambda p: (0, p))
    states = pl.BlockSpec((sk.shape[0], PAIR), lambda p: (0, p))
    band = pl.BlockSpec((PAIR, width), lambda p: (p, 0))
    return run_kernel(
        token_backward_kernel,
        (valid, resid, gain, cot, grad_ynorm, q, k, v, sk, sv, wo, mixed, log_total),
        grid=(pairs,),
        in_specs=[
            pl.BlockSpec(memory_space=pltpu.SMEM), once, whole((1, width)), once, once,
            tile, tile, tile, states, states, band, tile,
            pl.BlockSpec((1, 2, rows), lambda p: (p, 0, 0)),
        ],
        out_specs=[once, whole((1, width)), tile, tile, tile, states, states, band],
        out_shape=[
            jax.ShapeDtypeStruct((rows, width), F32),
            jax.ShapeDtypeStruct((1, width), F32),
            jax.ShapeDtypeStruct((rows, width), BF16),
            jax.ShapeDtypeStruct((rows, width), F32),
            jax.ShapeDtypeStruct((rows, width), F32),
            jax.ShapeDtypeStruct(sk.shape, BF16),
            jax.ShapeDtypeStruct(sk.shape, BF16),
            jax.ShapeDtypeStruct((width, width), BF16),
        ],
        scratch_shapes=[
            pltpu.VMEM((rows, width), BF16),
            pltpu.VMEM((rows, PAIR), BF16), pltpu.VMEM((rows, PAIR), F32),
            pltpu.VMEM((rows, PAIR), F32), pltpu.VMEM((sk.shape[0], PAIR), F32),
            pltpu.VMEM((sk.shape[0], PAIR), F32),
        ],
        name="token_backward",
        exchange=exchange,
        polls=3,
    )


def state_backward_kernel(
    poll, valid, cot, gain, gate_bias, wq, wk, wv, wu, states, updates,
    sq, k, v, read, log_total, near_k, near_v, dsk, dsv,
    dsq, dk, dv, dz_out, grad_state, gain_grad, bias_grad,
    later, dz, total, grad_read, sum_q, sum_k, sum_v,
):
    step, pair = pl.program_id(0), pl.program_id(1)
    block = pl.num_programs(0) - 1 - step
    gate = 1.0 / (1.0 + jnp.exp(-gate_bias[...]))

    @pl.when((step == 0) & (pair == 0))
    def _():
        later[...] = cot[...].astype(F32)
        gain_grad[...] = jnp.zeros_like(gain_grad)
        bias_grad[...] = jnp.zeros_like(bias_grad)

    @pl.when(pair == 0)
    def _():
        grad = later[...]
        rounded = (grad * (1.0 - gate)).astype(BF16)
        dz[...] = rounded
        dz_out[...] = rounded
        bias_grad[...] += (
            jnp.sum(grad * (states[...] - updates[...]), axis=0, keepdims=True) * gate * (1.0 - gate)
        )
        total[...] = jnp.zeros_like(total)

    poll()
    grad_read[...] = matmul_nt(dz[...], wu[...]).astype(BF16)
    seen = block * BLOCK + position((BLOCK, BLOCK), 0) < valid[0]
    sum_k[...] = near_k[...]
    sum_v[...] = near_v[...]
    for head in range(2):
        lanes = pl.ds(head * HEAD, HEAD)

        def adder(ref):
            def add(term):
                ref[:, lanes] += term

            return add

        out_grad = grad_read[:, lanes]
        dsq[:, lanes] = attend_backward(
            sq[:, lanes],
            log_total[0, 0, pl.ds(head, 1), :],
            out_grad,
            centre_of(out_grad, read[:, lanes]),
            [(k[:, lanes], v[:, lanes], seen, adder(sum_k), adder(sum_v))],
        ).astype(BF16)
    dk[...] = sum_k[...].astype(BF16)
    dv[...] = sum_v[...].astype(BF16)
    total[...] += (
        matmul_nt(dsq[...], wq[...]) + matmul_nt(dsk[...], wk[...]) + matmul_nt(dsv[...], wv[...])
    )

    @pl.when(pair == pl.num_programs(1) - 1)
    def _():
        grad, gain_rows = rms_backward(states[...], gain[...], total[...])
        grad = later[...] * gate + grad
        later[...] = grad
        grad_state[...] = grad
        gain_grad[...] += jnp.sum(gain_rows, axis=0, keepdims=True)


def state_backward(
    valid, cot, gain, gate_bias, weights, update_weight, states, updates,
    sq, k, v, read, log_total, near_k, near_v, dsk, dsv, exchange,
):
    rows, width = cot.shape
    blocks, pairs = k.shape[0] // BLOCK, width // PAIR
    columns = pl.BlockSpec((width, PAIR), lambda s, p: (0, p))
    tile = pl.BlockSpec((rows, PAIR), lambda s, p: (blocks - 1 - s, p))
    token = pl.BlockSpec((BLOCK, PAIR), lambda s, p: (blocks - 1 - s, p))
    band = pl.BlockSpec((rows, width), lambda s, p: (blocks - 1 - s, 0))
    small = whole((1, width))
    return run_kernel(
        state_backward_kernel,
        (
            valid, cot, gain, gate_bias, *weights, update_weight, states, updates,
            sq, k, v, read, log_total, near_k, near_v, dsk, dsv,
        ),
        grid=(blocks, pairs),
        in_specs=[
            pl.BlockSpec(memory_space=pltpu.SMEM), whole((rows, width)), small, small,
            columns, columns, columns, pl.BlockSpec((PAIR, width), lambda s, p: (p, 0)),
            band, band, tile, token, token, tile,
            pl.BlockSpec((1, 1, 2, rows), lambda s, p: (blocks - 1 - s, p, 0, 0)),
            token, token, tile, tile,
        ],
        out_specs=[tile, token, token, band, whole((rows, width)), small, small],
        out_shape=[
            jax.ShapeDtypeStruct((blocks * rows, width), BF16),
            jax.ShapeDtypeStruct(k.shape, BF16),
            jax.ShapeDtypeStruct(k.shape, BF16),
            jax.ShapeDtypeStruct((blocks * rows, width), BF16),
            jax.ShapeDtypeStruct((rows, width), F32),
            jax.ShapeDtypeStruct((1, width), F32),
            jax.ShapeDtypeStruct((1, width), F32),
        ],
        scratch_shapes=[
            pltpu.VMEM((rows, width), F32), pltpu.VMEM((rows, width), BF16),
            pltpu.VMEM((rows, width), F32), pltpu.VMEM((rows, PAIR), BF16),
            pltpu.VMEM((rows, PAIR), F32), pltpu.VMEM((BLOCK, PAIR), F32),
            pltpu.VMEM((BLOCK, PAIR), F32),
        ],
        name="state_backward",
        exchange=exchange,
    )


def weight_grad_kernel(counts, poll, *refs):
    refs = list(refs)
    lefts = [refs.pop(0) for _ in counts]
    rights = [[refs.pop(0) for _ in range(n)] for n in counts]
    outs = [[refs.pop(0) for _ in range(n)] for n in counts]
    poll()

    @pl.when(pl.program_id(0) == 0)
    def _():
        for left, left_t in zip(lefts, refs):
            left_t[...] = left[...].T

    for left_t, group, out_group in zip(refs, rights, outs):
        for right, out in zip(group, out_group):
            out[...] = matmul(left_t[...], right[...]).astype(BF16)


def weight_grad(pairs, name, exchange):
    lefts = [left for left, _ in pairs]
    rights = [right for _, group in pairs for right in group]
    rows, width = lefts[0].shape
    tile = pl.BlockSpec((rows, TILE), lambda j: (0, j))
    out = pl.BlockSpec((width, TILE), lambda j: (0, j))
    return run_kernel(
        functools.partial(weight_grad_kernel, [len(group) for _, group in pairs]),
        (*lefts, *rights),
        grid=(width // TILE,),
        in_specs=[whole((rows, width))] * len(lefts) + [tile] * len(rights),
        out_specs=[out] * len(rights),
        out_shape=[jax.ShapeDtypeStruct((width, width), BF16)] * len(rights),
        scratch_shapes=[pltpu.VMEM((width, rows), BF16)] * len(lefts),
        name=name,
        exchange=exchange,
    )


def token_grad_kernel(
    poll, x, gain, grad_resid, dq, dk, dv, wq, wk, wv, normed, dq_tile, dk_tile, dv_tile,
    grad_x, gain_grad, wq_grad, wk_grad, wv_grad, normed_t,
):
    poll()

    @pl.when(pl.program_id(0) == 0)
    def _():
        gain_grad[...] = jnp.zeros_like(gain_grad)
        normed_t[...] = normed[...].T

    for right, out in ((dq_tile, wq_grad), (dk_tile, wk_grad), (dv_tile, wv_grad)):
        out[...] = matmul(normed_t[...], right[...]).astype(BF16)
    poll()
    grad_normed = (
        matmul_nt(dq[...], wq[...]) + matmul_nt(dk[...], wk[...]) + matmul_nt(dv[...], wv[...])
    )
    grad, gain_rows = rms_backward(x[...].astype(F32), gain[...], grad_normed)
    grad_x[...] = grad_resid[...] + grad
    gain_grad[...] += jnp.sum(gain_rows, axis=0, keepdims=True)


def token_grad(x, gain, grad_resid, grads, weights, normed, exchange):
    rows, width = x.shape
    band = pl.BlockSpec((TILE, width), lambda i: (i, 0))
    tile = pl.BlockSpec((rows, TILE), lambda i: (0, i))
    out = pl.BlockSpec((width, TILE), lambda i: (0, i))
    weight = pl.BlockSpec((width, width), lambda i: (0, 0), pipeline_mode=pl.Buffered(1))
    return run_kernel(
        token_grad_kernel,
        (x, gain, grad_resid, *grads, *weights, normed, *grads),
        grid=(rows // TILE,),
        in_specs=[band, whole((1, width)), band, band, band, band, weight, weight, weight]
        + [weight, tile, tile, tile],
        out_specs=[band, whole((1, width)), out, out, out],
        out_shape=[
            jax.ShapeDtypeStruct((rows, width), F32), jax.ShapeDtypeStruct((1, width), F32)
        ]
        + [jax.ShapeDtypeStruct((width, width), BF16)] * 3,
        scratch_shapes=[pltpu.VMEM((width, rows), BF16)],
        name="token_grad",
        exchange=exchange,
        polls=2,
    )


def cut(width, pieces):
    return [(i * width // pieces, width // pieces) for i in range(pieces)]


def plan_gather(sizes, small, square, forward):
    width, part = square[0].shape[1], forward[0].shape[1]
    arrays = [small] + square + forward
    pieces = cut(width, SQUARE_PIECES)
    can_share = pieces[0][1] // sizes["m"] % 128 == 0
    lone = [
        (1 + i, columns)
        for trio in ((0, 1, 2), (3, 4, 5), (6, 7))
        for columns in pieces
        for i in trio
    ]
    units, together = [(0, "zx", False, (0, small.shape[1]))], [4]
    for n, (i, columns) in enumerate(lone):
        shared = can_share and n % 3 > 0
        units.append((i, "zxm" if shared else "zx", shared, columns))
        if n % 3 == 0 and n:
            together.append(0)
        if n >= 3:
            together[-1] += 1
    for i in range(4):
        for columns in cut(part, FORWARD_PIECES):
            units.append((9 + i, "zmx" if len(units) % 2 else "zxm", False, columns))
        together += [2] * (FORWARD_PIECES // 2)
    return Gather(sizes, arrays, units, together)


def plan_scatter(sizes, arrays, pieces, collective_id, group):
    units = []
    for columns in range(pieces):
        for i, array in enumerate(arrays):
            width = array.shape[-1]
            if array.dtype == F32:
                if columns == 0:
                    units.append((i, "xz", False, (0, width)))
                continue
            there = cut(width, pieces)[columns]
            if array.ndim == 6:
                units.append((i, ("mxz", "xmz")[len(units) % 2], False, there))
            else:
                shared = len(units) % 3 > 0 and there[1] // sizes["m"] % 128 == 0
                units.append((i, "mxz" if shared else "xz", shared, there))
    together = [group] * (len(units) // group)
    if len(units) % group:
        together.append(len(units) % group)
    return Scatter(sizes, arrays, units, together, collective_id)


def shards(
    mlp_size,
    tokens,
    initial_state,
    valid,
    token_query_weight,
    token_key_weight,
    token_value_weight,
    token_output_weight,
    state_query_weight,
    state_key_weight,
    state_value_weight,
    state_update_weight,
    up_projection_weight,
    down_projection_weight,
    token_norm_gain,
    state_norm_gain,
    feedforward_norm_gain,
    state_gate_bias,
    output_cotangent,
    final_state_cotangent,
):
    rows = token_query_weight.shape[0]
    width = tokens.shape[2]
    seg_size = width // rows
    sizes = {"z": seg_size // 4, "x": 2, "c": 2, "m": mlp_size}
    half = up_projection_weight.shape[1] // 2
    small = jnp.concatenate(
        [token_norm_gain, state_norm_gain, feedforward_norm_gain, state_gate_bias]
    ).reshape(-1, 128)
    small = jnp.pad(small, ((0, 16 - small.shape[0]), (0, 0)))
    square = [
        token_query_weight,
        token_key_weight,
        token_value_weight,
        state_query_weight,
        state_key_weight,
        state_value_weight,
        state_update_weight,
        token_output_weight,
    ]
    forward = [
        weight[:, first : first + half]
        for first in (0, half)
        for weight in (up_projection_weight, down_projection_weight)
    ]
    plan = plan_gather(sizes, small, square, forward)
    x, s0, cot = tokens[0], initial_state[0], output_cotangent[0]

    def full(*names):
        return [plan.targets[n].reshape(width, width) for n in names]

    def forward_full(*names):
        return [plan.targets[n].reshape(mlp_size, width, half) for n in names]

    exchange_alone(plan.until(plan.ready((0, 1, 2, 3)), 1), "gather_first")
    gains = plan.targets[0].reshape(seg_size, -1)[:, : 4 * rows].reshape(seg_size, 4, rows)
    gains = gains.transpose(1, 0, 2).reshape(4, 1, width).astype(F32)
    token_gain, state_gain, mlp_gain, gate_bias = [gains[i] for i in range(4)]
    token_weights = full(1, 2, 3)
    normed, q, k, v = project(
        x, token_gain, token_weights, plan.until(plan.ready((4, 5, 6, 7)), 2)
    )
    state_weights, (wu,) = full(4, 5, 6), full(7)
    ready = plan.ready((9, 10))
    middle = max(plan.ready((8,)), (plan.round + ready) // 2)
    snormed, sq, sk, sv, read, read_log, updates, states, last = state_forward(
        valid, s0, state_gain, gate_bias, state_weights, wu, k, v, plan.until(middle, 3)
    )
    (wo,) = full(8)
    mixed, token_log, resid, ynorm = token_forward(
        valid, x, mlp_gain, q, k, v, sk, sv, wo, plan.until(ready, 4)
    )
    total, grad_total, *first_grads = feed_forward(
        True, False, valid, ynorm, cot, resid, resid, *forward_full(9, 10),
        plan.until(plan.ready((11, 12)), 5),
    )

    def parted(grads):
        shape = (seg_size // 4, 2, 2, rows)
        return [
            g.reshape((mlp_size,) + shape + (half,)) if g.ndim == 3 else g.reshape(shape + (width,))
            for g in grads
        ]

    first_sums = plan_scatter(sizes, parted(first_grads), FORWARD_PIECES, 6, 2)
    out, grad_total, *last_grads = feed_forward(
        False, True, valid, ynorm, cot, total, grad_total, *forward_full(11, 12), first_sums
    )
    last_sums = plan_scatter(sizes, parted(last_grads), FORWARD_PIECES, 7, 2)
    grad_resid, mlp_gain_grad, dq, near_k, near_v, dsk, dsv, wo_grad = token_backward(
        valid, resid, mlp_gain, cot, grad_total, q, k, v, sk, sv, wo, mixed, token_log, last_sums
    )
    out_sum = plan_scatter(sizes, parted([wo_grad]), SQUARE_PIECES // 2, 8, 1)
    dsq, dk, dv, dz, grad_state, state_gain_grad, bias_grad = state_backward(
        valid, final_state_cotangent[0], state_gain, gate_bias, state_weights, wu,
        states, updates, sq, k, v, read, read_log, near_k, near_v, dsk, dsv, out_sum,
    )
    state_grads = weight_grad([(read, [dz]), (snormed, [dsq, dsk, dsv])], "weight_grad", None)
    state_sums = plan_scatter(sizes, parted(state_grads), SQUARE_PIECES // 2, 9, 4)
    grad_tokens, token_gain_grad, *token_grads = token_grad(
        x, token_gain, grad_resid, [dq, dk, dv], token_weights, normed, state_sums
    )
    small_grads = jnp.concatenate([token_gain_grad, state_gain_grad, mlp_gain_grad, bias_grad])
    small_grads = small_grads.reshape(4, seg_size, rows).transpose(1, 0, 2)
    small_grads = small_grads.reshape(seg_size, -1, 128)
    lines = small_grads.shape[1]
    small_grads = jnp.pad(small_grads, ((0, 0), (0, 8 - lines), (0, 0)))
    small_grads = small_grads.reshape(seg_size // 4, 2, 2, 8, 128)
    token_sums = plan_scatter(
        sizes, [small_grads] + parted(token_grads), SQUARE_PIECES // 2, 10, 4
    )
    exchange_alone(token_sums, "scatter_last")
    small_sum, *token_sums = token_sums.sums
    small_sum = small_sum[:lines].reshape(4, rows)
    update_sum, *state_sums = state_sums.sums
    forward_sums = [
        jnp.concatenate([a, b], axis=1) for a, b in zip(first_sums.sums, last_sums.sums)
    ]
    return (
        out[None],
        last[None],
        grad_tokens[None],
        grad_state[None],
        *token_sums,
        *out_sum.sums,
        *state_sums,
        update_sum,
        *forward_sums,
        *[small_sum[i] for i in range(4)],
    )


def solution(mesh):
    own = P(("seg", "mlp"), None, None)
    square, forward, small = P("seg", None), P("seg", "mlp"), P("seg")
    return jax.shard_map(
        functools.partial(shards, mesh.shape["mlp"]),
        mesh=mesh,
        in_specs=(own, own, P(("seg", "mlp")))
        + (square,) * 8
        + (forward,) * 2
        + (small,) * 4
        + (own, own),
        out_specs=(own,) * 4 + (square,) * 8 + (forward,) * 2 + (small,) * 4,
        check_vma=False,
    )
```

time: 754 us -> 574 us (0.76)
  Pallas kernels: 723 us -> 539 us
    pallas_call x13 -> x11, Pallas kernels: 723 us -> 539 us  [the longest x10 524 us: run_kernel(): pl.pallas_call(kernel, grid=grid, in_specs=list(in_specs) + exchange.spec...]
where the time goes in v3:
time: 574 us; the launch traced here: 566 us
  Pallas kernels  539 us (94%)
  local copies, waits for them, and re-layouts  21.8 us (4%)
    pallas_call x10, Pallas kernels, run_kernel(): pl.pallas_call(kernel, grid=grid, in_specs=list(in_specs) + exchange.spec...  524 us
    pallas_call x1, Pallas kernels, run_kernel(): pl.pallas_call(functools.partial(body, lambda: None), grid=grid, in_specs...  14.8 us
    unnamed x51, local copies, waits for them, and re-layouts  14.3 us

profile of v3, /device:TPU:0, one launch (start us, length us, event | category | flops | bytes accessed | tf_op | source)
XLA Modules:
  0.0 566.0 jit_solution(5506229754656202754)
XLA Ops:
  1.3 0.8 maximum_bitcast_fusion
  2.1 0.6 pad.8.refs_0_
  2.7 1.9 fusion
  4.6 58.8 %gather_first.1 = (bf16[4,2,2,16,128]{4,3,2,1,0:T(8,128)(2,1)}, bf16[4,2,2,64,1024]{4,3,2,1,0:T(8,128)(2,1)}, bf16[4,2,2,64,1024]{4,3,2,1,0:T(8,128)(2,1)}, bf16...) custom-call(bf16[16,128]{1,0:T(8,128)(2,1)} %pad.8.refs_0_, ...), custom_call_target="tpu_custom_call" | custom-call | tf_op jit(solution)/shard_map/gather_first/pallas_call | solution.py:460
  63.4 0.9 copy.52
  64.3 0.1 reshape.181
  64.4 0.1 slice_reduce_fusion
  64.5 0.7 squeeze.41.refs_3_
  65.2 0.7 squeeze.40.refs_2_
  65.8 0.7 squeeze.38.refs_1_
  66.5 0.7 squeeze.37.refs_2_
  67.2 63.3 %project_tokens.1 = (bf16[1024,1024]{1,0:T(8,128)(2,1)}, bf16[1024,1024]{1,0:T(8,128)(2,1)}, bf16[1024,1024]{1,0:T(8,128)(2,1)}, bf16[1024,1024]{1,0:T(8,128)(2,...) custom-call(bf16[1024,1024]{1,0:T(8,128)(2,1)} %bitcast.56, ...), custom_call_target="tpu_custom_call", output_to_operand_aliasing={{4}: (12, {}), {5}: (13, {}), {6}: (14, {})} | custom-call | tf_op jit(solution)/shard_map/project_tokens/pallas_call | solution.py:460
  130.4 31.5 %state_forward.1 = (bf16[1024,1024]{1,0:T(8,128)(2,1)}, bf16[1024,1024]{1,0:T(8,128)(2,1)}, bf16[1024,1024]{1,0:T(8,128)(2,1)}, bf16[1024,1024]{1,0:T(8,128)(2,1...) custom-call(s32[1]{0:T(128)S(6)} %copy.76.refs_0_, ...), custom_call_target="tpu_custom_call", output_to_operand_aliasing={{9}: (14, {}), {10}: (15, {}), {11}: (16, {})} | custom-call | tf_op jit(solution)/shard_map/state_forward/pallas_call | solution.py:460
  161.9 44.6 %token_forward.1 = (bf16[1024,1024]{1,0:T(8,128)(2,1)}, f32[4,2,1024]{2,1,0:T(2,128)}, f32[1024,1024]{1,0:T(8,128)}, bf16[1024,1024]{1,0:T(8,128)(2,1)}, bf16[2,...) custom-call(s32[1]{0:T(128)S(6)} %copy.76.refs_0_, ...), custom_call_target="tpu_custom_call", output_to_operand_aliasing={{4}: (13, {}), {5}: (14, {}), {6}: (15, {})} | custom-call | tf_op jit(solution)/shard_map/token_forward/pallas_call | solution.py:460
  206.5 41.1 %feed_forward_first.1 = (f32[1024,1024]{1,0:T(8,128)}, f32[1024,1024]{1,0:T(8,128)}, bf16[2,1024,1024]{2,1,0:T(8,128)(2,1)}, bf16[2,1024,1024]{2,1,0:T(8,128)(2,...) custom-call(s32[1]{0:T(128)S(6)} %copy.76.refs_0_, ...), custom_call_target="tpu_custom_call", output_to_operand_aliasing={{4}: (9, {}), {5}: (10, {})} | custom-call | tf_op jit(solution)/shard_map/feed_forward_first/pallas_call | solution.py:460
  247.6 63.3 %feed_forward_final.1 = (bf16[1024,1024]{1,0:T(8,128)(2,1)}, f32[1024,1024]{1,0:T(8,128)}, bf16[2,1024,1024]{2,1,0:T(8,128)(2,1)}, bf16[2,1024,1024]{2,1,0:T(8,1...) custom-call(s32[1]{0:T(128)S(6)} %copy.76.refs_0_, bf16[1024,1024]{1,0:T(8,128)(2,1)} %get-tuple-element.127.refs_1_, ...), custom_call_target="tpu_custom_call" | custom-call | tf_op jit(solution)/shard_map/feed_forward_final/pallas_call | solution.py:460
  310.8 67.2 %token_backward.1 = (f32[1024,1024]{1,0:T(8,128)}, f32[1,1024]{1,0:T(1,128)}, bf16[1024,1024]{1,0:T(8,128)(2,1)}, f32[1024,1024]{1,0:T(8,128)}, f32[1024,1024]{1...) custom-call(s32[1]{0:T(128)S(6)} %copy.76.refs_0_, ...), custom_call_target="tpu_custom_call" | custom-call | tf_op jit(solution)/shard_map/token_backward/pallas_call | solution.py:460
  378.1 43.2 %state_backward.1 = (bf16[1024,1024]{1,0:T(8,128)(2,1)}, bf16[1024,1024]{1,0:T(8,128)(2,1)}, bf16[1024,1024]{1,0:T(8,128)(2,1)}, bf16[1024,1024]{1,0:T(8,128)(2,...) custom-call(s32[1]{0:T(128)S(6)} %copy.76.refs_0_, ...), custom_call_target="tpu_custom_call" | custom-call | tf_op jit(solution)/shard_map/state_backward/pallas_call | solution.py:460
  421.3 0.0 copy-done.13
  421.3 0.0 copy-done.15
  421.3 0.8 pad_maximum_fusion
  422.2 0.0 copy-done.14
  422.2 0.8 pad_maximum_fusion.1
  423.0 14.8 %weight_grad.1 = (bf16[1024,1024]{1,0:T(8,128)(2,1)}, bf16[1024,1024]{1,0:T(8,128)(2,1)}, bf16[1024,1024]{1,0:T(8,128)(2,1)}, bf16[1024,1024]{1,0:T(8,128)(2,1)}) custom-call(bf16[1024,1024]{1,0:T(8,128)(2,1)} %get-tuple-element.151.refs_13_.refs_0_, bf16[1024,1024]{1,0:T(8,128)(2,1)} %get-tuple-element.161.refs_1_, ...), custom_call_target="tpu_custom_call" | custom-call | tf_op jit(solution)/shard_map/weight_grad/pallas_call | solution.py:422
  437.9 63.9 %token_grad.1 = (f32[1024,1024]{1,0:T(8,128)}, f32[1,1024]{1,0:T(1,128)}, bf16[1024,1024]{1,0:T(8,128)(2,1)}, bf16[1024,1024]{1,0:T(8,128)(2,1)}, bf16[1024,1024...) custom-call(bf16[1024,1024]{1,0:T(8,128)(2,1)} %bitcast.58, ...), custom_call_target="tpu_custom_call" | custom-call | tf_op jit(solution)/shard_map/token_grad/pallas_call | solution.py:460
  501.8 0.7 pad_maximum_fusion.2
  502.5 0.1 reshape.174
  502.6 0.1 reshape.175
  502.7 0.6 pad.9
  503.4 47.4 %scatter_last.1 = (f32[8,128]{1,0:T(8,128)}, f32[64,1024]{1,0:T(8,128)}, f32[64,1024]{1,0:T(8,128)}, f32[64,1024]{1,0:T(8,128)}) custom-call(f32[4,2,2,8,128]{4,3,2,1,0:T(8,128)} %bitcast.94, bf16[4,2,2,64,1024]{4,3,2,1,0:T(8,128)(2,1)} %bitcast.81, bf16[4,2,2,64,1024]{4,3,2,1,0:T(8,128)(2,1)} %bitcast.82, bf16[4,2,2,64,1024]{4,3,2,1,0:T(8,128)(2,1)} %bitcast.83), custom_call_target="tpu_custom_call" | custom-call | tf_op jit(solution)/shard_map/scatter_last/pallas_call | solution.py:460
  550.8 0.7 slice.55
  551.5 0.1 reshape.180
  551.6 0.5 slice_bitcast_fusion
  552.1 0.0 copy-done.1
  552.1 1.3 copy.77
  553.4 1.0 copy.78
  554.4 1.0 copy-done
  555.4 2.1 copy.79
  557.6 1.0 copy-done.2
  558.5 1.3 copy.80
  559.9 0.7 copy.81
  560.6 0.7 copy.82
  561.3 0.7 copy.83
  562.0 0.7 copy.84
  562.7 0.7 copy.85
  563.4 0.7 copy.86
  564.1 0.7 copy.87
  564.8 0.7 copy.88
  (34 shorter events, 0.1 us)
Async XLA Ops:
  378.0 43.3 %copy-start.13 = (f32[64,1024]{1,0:T(8,128)S(1)}, f32[64,1024]{1,0:T(8,128)}, u32[]{:S(2)}) copy-start(f32[64,1024]{1,0:T(8,128)} %get-tuple-element.185) | copy-start | bytes 786436
  378.1 43.3 %copy-start.15 = (f32[64,1024]{1,0:T(8,128)S(1)}, f32[64,1024]{1,0:T(8,128)}, u32[]{:S(2)}) copy-start(f32[64,1024]{1,0:T(8,128)} %get-tuple-element.186) | copy-start | bytes 786436
  378.1 44.1 %copy-start.12 = (f32[64,1024]{1,0:T(8,128)S(1)}, f32[64,1024]{1,0:T(8,128)}, u32[]{:S(2)}) copy-start(f32[64,1024]{1,0:T(8,128)} %get-tuple-element.187) | copy-start | bytes 786436
  378.1 44.1 %copy-start.14 = (f32[64,1024]{1,0:T(8,128)S(1)}, f32[64,1024]{1,0:T(8,128)}, u32[]{:S(2)}) copy-start(f32[64,1024]{1,0:T(8,128)} %get-tuple-element.188) | copy-start | bytes 786436
  437.8 63.9 %copy-start.16 = (f32[1,1024]{1,0:T(1,128)S(1)}, f32[1,1024]{1,0:T(1,128)}, u32[]{:S(2)}) copy-start(f32[1,1024]{1,0:T(1,128)} %get-tuple-element.172) | copy-start | bytes 12292
  437.8 63.9 %copy-start.17 = (f32[1,1024]{1,0:T(1,128)S(1)}, f32[1,1024]{1,0:T(1,128)}, u32[]{:S(2)}) copy-start(f32[1,1024]{1,0:T(1,128)} %get-tuple-element.171) | copy-start | bytes 12292
  437.9 63.9 %copy-start.18 = (f32[1,1024]{1,0:T(1,128)S(1)}, f32[1,1024]{1,0:T(1,128)}, u32[]{:S(2)}) copy-start(f32[1,1024]{1,0:T(1,128)} %get-tuple-element.173) | copy-start | bytes 12292
  503.3 48.8 %copy-start.1 = (bf16[1024,1024]{1,0:T(8,128)(2,1)S(1)}, bf16[1024,1024]{1,0:T(8,128)(2,1)}, u32[]{:S(2)}) copy-start(bf16[1024,1024]{1,0:T(8,128)(2,1)} %get-tuple-element.139) | copy-start | bytes 6291460
  503.3 50.1 %copy-start.3 = (bf16[512,1024]{1,0:T(8,128)(2,1)S(1)}, bf16[512,1024]{1,0:T(8,128)(2,1)}, u32[]{:S(2)}) copy-start(bf16[512,1024]{1,0:T(8,128)(2,1)} %get-tuple-element.140) | copy-start | bytes 3145732
  552.1 3.3 copy-start
  555.4 3.1 copy-start.2
  558.5 1.3 copy-start.11
  558.5 2.1 copy-start.10
  558.5 2.8 copy-start.9
  558.5 3.5 copy-start.4
  559.9 2.8 copy-start.8
  559.9 3.5 copy-start.7
  559.9 4.3 copy-start.6
  559.9 5.0 copy-start.5

commit v4 on v3

--- a/solution.py
+++ b/solution.py
@@ -9,8 +9,16 @@
 BF16 = jnp.bfloat16
 F32 = jnp.float32
 VMEM_LIMIT = 60 << 20
-SQUARE_PIECES = 4
+SQUARE_PIECES = 2
 FORWARD_PIECES = 2
+SCATTER_PIECES = 2
+GATHER_SQUARE = (0, 2, 4, 5)
+GATHER_FORWARD = (7, 8, 10, 11)
+GATHER_MIDDLE = 10
+SCATTER_ROUNDS = (3, 3, 3)
+LINK_RATE = 92e3
+CORE_RATE = 560e3
+ROUND_COST = 2.0
 
 
 class Place:
@@ -151,151 +159,170 @@
     lax.fori_loop(0, functools.reduce(lambda a, b: a * b, lead, 1), body, 0)
 
 
-def scatter_shapes(grad_shape, order, split, columns, sizes):
-    lead = ("m" if len(grad_shape) == 6 else "") + "zx"
-    rows, width = grad_shape[-2], columns[1]
-
-    def left(done):
-        share = width // sizes["m"] if split and "m" in done else width
-        return tuple(sizes[a] for a in lead if a not in done) + (rows, share)
-
-    shapes = [left(""), left("")]
-    for i, axis in enumerate(order):
-        shapes.append((sizes[axis] - 1,) + left(order[: i + 1]))
-    if "m" not in lead:
-        shapes.append((rows, width) if split else (sizes["m"], rows, width))
-    return shapes
-
-
-def scatter_steps(flow, grad, result, buffers, order, split, columns, local_sem):
-    place = flow.place
-    at, sizes = place.at, place.sizes
-    whole_m = len(grad.shape) == 6
-    lead = ("m" if whole_m else "") + "zx"
-    own, core_in = buffers[:2]
-    landing = dict(zip(order, buffers[2:]))
-    last = buffers[-1]
-    rows, width = grad.shape[-2], columns[1]
-    share = width // sizes["m"] if split else width
-
-    def lanes_of(place_m):
-        return pl.ds(pl.multiple_of(place_m * share, 128), share)
-
-    def grad_half(core):
-        return grad.at[
-            tuple(pl.ds(0, sizes[a]) for a in lead) + (core, pl.ds(0, rows), pl.ds(*columns))
-        ]
-
-    def view(done, **moved):
-        index = tuple(
-            moved[a] if a in moved else at[a] if a in done else pl.ds(0, sizes[a]) for a in lead
-        )
-        lanes = pl.ds(0, width)
-        if split and ("m" in done or "m" in moved):
-            lanes = lanes_of(moved.get("m", at["m"]))
-        return own.at[index + (pl.ds(0, rows), lanes)]
-
-    def load():
-        return pltpu.make_async_copy(grad_half(at["c"]), own, local_sem)
-
-    actions = [lambda: load().start()]
-    flow.move(actions, lambda: (grad_half(1 - at["c"]), core_in, {"c": 1 - at["c"]}, core_in))
-    flow.steps.append(actions)
-    actions = [lambda: load().wait()] + flow.arrived() + [lambda: add_into(own, core_in)]
-    done = ""
-    for axis in order:
-        for step in range(1, sizes[axis]):
-
-            def make(axis=axis, step=step, done=done):
-                there = place.ahead(axis, step)
-                slot = landing[axis].at[step - 1]
-                return (view(done, **{axis: there}), slot, {axis: there}, slot)
-
-            flow.move(actions, make)
-        flow.steps.append(actions)
-        done += axis
-        actions = flow.arrived()
-        for step in range(1, sizes[axis]):
-            actions.append(
-                lambda axis=axis, step=step, done=done: add_into(
-                    view(done), landing[axis].at[step - 1]
+class ScatterUnit:
+    def __init__(self, sizes, grad, order, split, columns, start):
+        self.sizes, self.grad, self.order, self.split = sizes, grad, order, split
+        self.columns, self.start = columns, start
+        self.whole_m = grad.ndim == 6
+        self.lead = ("m" if self.whole_m else "") + "zx"
+        self.rows, self.width = grad.shape[-2], columns[1]
+        self.share = self.width // sizes["m"] if split else self.width
+        self.count = 1 + len(order) + (not self.whole_m)
+        self.spec = pl.BlockSpec(memory_space=pl.ANY)
+        self.state = self.result = None
+
+    def left(self, done):
+        width = self.share if "m" in done else self.width
+        return tuple(self.sizes[a] for a in self.lead if a not in done) + (self.rows, width)
+
+    def shapes(self, begin, end):
+        shapes = [self.left(self.order[: max(begin - 1, 0)])]
+        for i in range(begin, end):
+            if i == 0:
+                shapes.append(self.left(""))
+            elif i <= len(self.order):
+                axis = self.order[i - 1]
+                shapes.append((self.sizes[axis] - 1,) + self.left(self.order[:i]))
+            elif self.split:
+                shapes.append((self.rows, self.width))
+            else:
+                shapes.append((self.sizes["m"], self.rows, self.width))
+        return shapes
+
+    def steps(self, flow, grad, state, saved, result, buffers, local_sem, begin, end):
+        place, at, sizes, order = flow.place, flow.place.at, self.sizes, self.order
+        own, landings = buffers[0], dict(zip(range(begin, end), buffers[1:]))
+        gone = order[: max(begin - 1, 0)]
+        lead = [a for a in self.lead if a not in gone]
+        narrow = self.split and "m" in gone
+
+        def lanes_of(place_m):
+            return pl.ds(pl.multiple_of(place_m * self.share, 128), self.share)
+
+        def grad_half(core):
+            index = tuple(pl.ds(0, sizes[a]) for a in self.lead)
+            return grad.at[index + (core, pl.ds(0, self.rows), pl.ds(*self.columns))]
+
+        def view(done, **moved):
+            index = tuple(
+                moved[a] if a in moved else at[a] if a in done else pl.ds(0, sizes[a]) for a in lead
+            )
+            lanes = pl.ds(0, self.share if narrow else self.width)
+            if self.split and not narrow and ("m" in done or "m" in moved):
+                lanes = lanes_of(moved.get("m", at["m"]))
+            return own.at[index + (pl.ds(0, self.rows), lanes)]
+
+        def load():
+            return pltpu.make_async_copy(grad_half(at["c"]) if begin == 0 else state, own, local_sem)
+
+        def added(axis, done, landing):
+            return [
+                lambda step=step: add_into(view(done), landing.at[step - 1])
+                for step in range(1, sizes[axis])
+            ]
+
+        ahead = [lambda: load().start()]
+        actions = []
+        if begin > 0:
+            actions.append(lambda: load().wait())
+        for i in range(begin, end):
+            landing = landings[i]
+            if i == 0:
+                flow.move(
+                    actions,
+                    lambda landing=landing: (
+                        grad_half(1 - at["c"]), landing, {"c": 1 - at["c"]}, landing
+                    ),
                 )
-            )
-    block = (pl.ds(0, rows), pl.ds(*columns))
-    if whole_m:
-
-        def store():
-            result[block] = view(done)[...].astype(F32)
-
-        actions.append(store)
-    elif split:
-
-        def part(place_m):
-            return last.at[pl.ds(0, rows), lanes_of(place_m)]
-
-        def keep():
-            part(at["m"])[...] = view(done)[...]
-
-        actions.append(keep)
-        for step in range(1, sizes["m"]):
-            flow.move(
-                actions,
-                lambda step=step: (
-                    part(at["m"]),
-                    part(at["m"]),
-                    {"m": place.ahead("m", step)},
-                    part(place.behind("m", step)),
-                ),
-            )
-        flow.steps.append(actions)
-        actions = flow.arrived()
-
-        def store():
-            result[block] = last[...].astype(F32)
-
-        actions.append(store)
-    else:
-
-        def keep():
-            last[at["m"]] = view(done)[...]
-
-        actions.append(keep)
-        for step in range(1, sizes["m"]):
-            flow.move(
-                actions,
-                lambda step=step: (
-                    last.at[at["m"]],
-                    last.at[at["m"]],
-                    {"m": place.ahead("m", step)},
-                    last.at[place.behind("m", step)],
-                ),
-            )
-        flow.steps.append(actions)
-        actions = flow.arrived()
-
-        def store():
-            total = last[0].astype(F32)
-            for i in range(1, sizes["m"]):
-                total = total + last[i].astype(F32)
-            result[block] = total
-
-        actions.append(store)
-    flow.last = actions + flow.sent
+                flow.steps.append(actions)
+                actions = [lambda: load().wait()] + flow.arrived()
+                actions.append(lambda landing=landing: add_into(own, landing))
+            elif i <= len(order):
+                axis, done = order[i - 1], order[: i - 1]
+                for step in range(1, sizes[axis]):
+
+                    def make(axis=axis, step=step, done=done, landing=landing):
+                        there = place.ahead(axis, step)
+                        slot = landing.at[step - 1]
+                        return (view(done, **{axis: there}), slot, {axis: there}, slot)
+
+                    flow.move(actions, make)
+                flow.steps.append(actions)
+                actions = flow.arrived() + added(axis, order[:i], landing)
+            else:
+
+                def part(place_m, landing=landing):
+                    if self.split:
+                        return landing.at[pl.ds(0, self.rows), lanes_of(place_m)]
+                    return landing.at[place_m]
+
+                def keep():
+                    part(at["m"])[...] = view(order)[...]
+
+                actions.append(keep)
+                for step in range(1, sizes["m"]):
+                    flow.move(
+                        actions,
+                        lambda step=step: (
+                            part(at["m"]),
+                            part(at["m"]),
+                            {"m": place.ahead("m", step)},
+                            part(place.behind("m", step)),
+                        ),
+                    )
+                flow.steps.append(actions)
+                actions = flow.arrived()
+        if end == self.count:
+
+            def store():
+                if self.whole_m:
+                    total = view(order)[...].astype(F32)
+                elif self.split:
+                    total = landing[...].astype(F32)
+                else:
+                    total = landing[0].astype(F32)
+                    for i in range(1, sizes["m"]):
+                        total = total + landing[i].astype(F32)
+                result[...] = total
+
+            return ahead, actions + [store], flow.sent
+
+        def save():
+            return pltpu.make_async_copy(view(order[: end - 1]), saved, local_sem)
+
+        return ahead, actions + [lambda: save().start()], flow.sent + [lambda: save().wait()]
+
+
+def step_time(sizes, axis, size):
+    if axis == "c":
+        return size / CORE_RATE
+    return 2 * size * ((sizes["z"] // 2) ** 2 if axis == "z" else sizes[axis] - 1) / LINK_RATE
+
+
+def round_times(sizes, rounds):
+    times = []
+    for there in rounds:
+        load = {axis: 0.0 for axis in "zxcm"}
+        for axis, size in there:
+            load[axis] += step_time(sizes, axis, size)
+        times.append(max(load.values()) + ROUND_COST)
+    return times
 
 
 class Gather:
-    def __init__(self, sizes, arrays, units, together):
-        self.sizes, self.arrays, self.units = sizes, arrays, units
+    def __init__(self, sizes, arrays, units):
+        self.sizes, self.arrays, self.round = sizes, arrays, 0
+        self.units = [unit[:-1] for unit in units]
+        self.starts = [unit[-1] for unit in units]
         self.targets = [None] * len(arrays)
-        self.starts, self.round = [], 0
-        for start, count in enumerate(together):
-            self.starts += [start] * count
-        assert len(self.starts) == len(units)
 
     def ready(self, names):
         return max(
-            start + len(unit[1]) + 1 for start, unit in zip(self.starts, self.units) if unit[0] in names
+            self.stop(start, unit) for start, unit in zip(self.starts, self.units) if unit[0] in names
         )
+
+    def stop(self, start, unit):
+        return start + len(unit[1]) + 1
 
     def until(self, end, collective_id):
         begin, self.round = self.round, max(end, self.round)
@@ -308,7 +335,7 @@
         self.units = [
             (start, unit)
             for start, unit in zip(plan.starts, plan.units)
-            if start < end and start + len(unit[1]) + 1 > begin
+            if start < end and plan.stop(start, unit) > begin
         ]
         self.names = sorted({unit[0] for _, unit in self.units})
         split = {unit[0]: unit[2] for _, unit in self.units}
@@ -336,6 +363,19 @@
             pltpu.SemaphoreType.DMA((len(self.units),)),
         ]
 
+    def times(self):
+        rounds = [[] for _ in range(self.end - self.begin)]
+        sizes = self.plan.sizes
+        for start, (n, order, split, columns) in self.units:
+            size = self.plan.arrays[n].shape[0] * columns[1] * self.plan.arrays[n].dtype.itemsize
+            if split:
+                size //= sizes["m"]
+            for i, axis in enumerate(order + "c"):
+                if self.begin <= start + i < self.end:
+                    rounds[start + i - self.begin].append((axis, size))
+                size *= sizes[axis]
+        return round_times(sizes, rounds)
+
     def rounds(self, ins, outs, scratch):
         place = Place(self.plan.sizes)
         send, recv, local = scratch
@@ -344,14 +384,14 @@
         last = []
         for i, (start, (n, order, split, columns)) in enumerate(self.units):
             flow = Flow(place, send, recv, taken)
-            begin = max(self.begin - start, 0)
+            begin, end = max(self.begin - start, 0), self.end - start
             slot = self.names.index(n)
-            gather_steps(
-                flow, ins[slot], outs[slot], order, split, columns, local.at[i], begin, self.end - start
-            )
+            gather_steps(flow, ins[slot], outs[slot], order, split, columns, local.at[i], begin, end)
             for step, actions in enumerate(flow.steps):
-                rounds[start + begin + step - self.begin] += actions
+                there = rounds[start + begin + step - self.begin]
+                there.insert(0 if begin + step == 0 else len(there), actions)
             last += flow.last
+        rounds = [[action for actions in there for action in actions] for there in rounds]
         rounds[0].insert(0, place.greet)
         return rounds, last
 
@@ -360,54 +400,166 @@
             self.plan.targets[n] = out
 
 
+class SmallUnit:
+    def __init__(self, plan, rows, start):
+        self.plan, self.grad, self.start = plan, rows, start
+        self.order, self.count = "xzm", 4
+        self.rows, self.width = rows.shape
+        self.share = self.width
+        self.spec = pl.BlockSpec(rows.shape, lambda *_: (0, 0))
+        self.state = self.result = None
+
+    def left(self, done):
+        return (self.rows, self.width)
+
+    def shapes(self, begin, end):
+        sizes = self.plan.sizes
+        return [self.left("")] + [(sizes[axis],) + self.left("") for axis in "c" + self.order]
+
+    def steps(self, flow, rows, state, saved, result, buffers, local_sem, begin, end):
+        place, at = flow.place, flow.place.at
+        own, landings = buffers[0], buffers[1:]
+        actions = []
+
+        def fill():
+            own[...] = rows[...]
+            own[pl.ds(0, 1), :] = self.plan.first_row[...]
+
+        actions.append(fill)
+        for axis, landing in zip("c" + self.order, landings):
+
+            def keep(axis=axis, landing=landing):
+                landing[at[axis]] = own[...]
+
+            actions.append(keep)
+            for step in range(1, place.sizes[axis]):
+
+                def make(axis=axis, landing=landing, step=step):
+                    slot = landing.at[at[axis]]
+                    return (slot, slot, {axis: place.ahead(axis, step)}, landing.at[place.behind(axis, step)])
+
+                flow.move(actions, make)
+            flow.steps.append(actions)
+
+            def add(axis=axis, landing=landing):
+                total = landing[0]
+                for i in range(1, place.sizes[axis]):
+                    total = total + landing[i]
+                own[...] = total
+
+            actions = flow.arrived() + [add]
+
+        def store():
+            result[...] = own[...]
+
+        return [], actions + [store], flow.sent
+
+
 class Scatter:
+    def __init__(self, sizes):
+        self.sizes, self.units, self.round = sizes, [], 0
+
+    def add(self, arrays, units):
+        for i, order, split, columns, start in units:
+            assert start >= self.round
+            self.units.append(ScatterUnit(self.sizes, arrays[i], order, split, columns, start))
+        return self.units[len(self.units) - len(units) :]
+
+    def add_small(self, rows):
+        self.units.append(SmallUnit(self, rows, self.all() - 4))
+        return self.units[-1]
+
+    def all(self):
+        return max(unit.start + unit.count for unit in self.units)
+
+    def until(self, end, collective_id):
+        begin, self.round = self.round, max(end, self.round)
+        part = ScatterPart(self, begin, end, collective_id)
+        return part if part.units else None
+
+
+class ScatterPart:
     aliases = {}
 
-    def __init__(self, sizes, arrays, units, together, collective_id):
-        self.sizes, self.arrays, self.units = sizes, arrays, units
-        self.collective_id = collective_id
-        self.starts = []
-        for start, count in enumerate(together):
-            self.starts += [start] * count
-        assert len(self.starts) == len(units)
-        self.specs = [pl.BlockSpec(memory_space=pl.ANY)] * len(arrays)
-        self.out_shape = [jax.ShapeDtypeStruct(a.shape[-2:], F32) for a in arrays]
-        self.out_specs = [
-            pl.BlockSpec(a.shape[-2:], lambda *_: (0, 0), pipeline_mode=pl.Buffered(1)) for a in arrays
-        ]
-        buffers = []
-        for i, order, split, columns in units:
-            buffers += [
-                pltpu.VMEM(shape, arrays[i].dtype)
-                for shape in scatter_shapes(arrays[i].shape, order, split, columns, sizes)
-            ]
-        pairs = len(units) * (sum(sizes.values()) - 4 + sizes["m"] - 1)
+    def __init__(self, plan, begin, end, collective_id):
+        self.sizes, self.begin, self.end, self.collective_id = plan.sizes, begin, end, collective_id
+        self.units = []
+        buffers, pairs = [], 0
+        self.arrays, self.out_shape, self.out_specs = [], [], []
+        for unit in plan.units:
+            first, stop = max(begin - unit.start, 0), min(end - unit.start, unit.count)
+            if first >= stop:
+                continue
+            self.units.append((unit, first, stop))
+            self.arrays.append(unit.state if first else unit.grad)
+            if stop == unit.count:
+                shape = (unit.rows, unit.width)
+                self.out_shape.append(jax.ShapeDtypeStruct(shape, F32))
+                self.out_specs.append(
+                    pl.BlockSpec(shape, lambda *_: (0, 0), pipeline_mode=pl.Buffered(1))
+                )
+            else:
+                shape = unit.left(unit.order[: stop - 1])
+                self.out_shape.append(jax.ShapeDtypeStruct(shape, unit.grad.dtype))
+                self.out_specs.append(pl.BlockSpec(memory_space=pl.ANY))
+            buffers += [pltpu.VMEM(shape, unit.grad.dtype) for shape in unit.shapes(first, stop)]
+            pairs += sum(self.sizes.values()) - 4 + self.sizes["m"] - 1
+        self.specs = [unit.spec for unit, _, _ in self.units]
         self.scratch = buffers + [
             pltpu.SemaphoreType.DMA((pairs,)),
             pltpu.SemaphoreType.DMA((pairs,)),
-            pltpu.SemaphoreType.DMA((len(units),)),
+            pltpu.SemaphoreType.DMA((len(self.units),)),
         ]
+
+    def times(self):
+        rounds = [[] for _ in range(self.end - self.begin)]
+        for unit, first, stop in self.units:
+            for i in range(first, stop):
+                done = unit.order[:i]
+                axis = ("c" + unit.order + "m")[i]
+                shape = unit.left(done) if i <= len(unit.order) else (unit.rows, unit.share)
+                size = functools.reduce(lambda a, b: a * b, shape, unit.grad.dtype.itemsize)
+                rounds[unit.start + i - self.begin].append((axis, size))
+        return round_times(self.sizes, rounds)
 
     def rounds(self, ins, outs, scratch):
         place = Place(self.sizes)
         send, recv, local = scratch[-3:]
         buffers = list(scratch[:-3])
-        taken, flows, last = [0], [], []
-        for unit, (i, order, split, columns) in enumerate(self.units):
+        taken = [0]
+        rounds = [[] for _ in range(self.end - self.begin)]
+        start_up, ends, waits = [], [], []
+        for i, (unit, first, stop) in enumerate(self.units):
             flow = Flow(place, send, recv, taken)
-            count = len(scatter_shapes(ins[i].shape, order, split, columns, self.sizes))
+            count = 1 + stop - first
             mine, buffers = buffers[:count], buffers[count:]
-            scatter_steps(flow, ins[i], outs[i], mine, order, split, columns, local.at[unit])
-            flows.append(flow)
-        rounds = [[] for _ in range(max(s + len(f.steps) for s, f in zip(self.starts, flows)) + 1)]
-        for start, flow in zip(self.starts, flows):
-            for i, actions in enumerate(flow.steps + [flow.last]):
-                rounds[start + i] += actions
-        rounds[0].insert(0, place.greet)
-        return rounds[:-1], rounds[-1]
+            done = stop == unit.count
+            ahead, end, wait = unit.steps(
+                flow, ins[i], ins[i], None if done else outs[i], outs[i] if done else None,
+                mine, local.at[i], first, stop,
+            )
+            if first:
+                start_up += ahead
+            else:
+                flow.steps[0][:0] = ahead
+            for step, actions in enumerate(flow.steps):
+                rounds[unit.start + first + step - self.begin].append(actions)
+            after = unit.start + stop - self.begin
+            if after < len(rounds):
+                rounds[after].append(end)
+            else:
+                ends += end
+            waits += wait
+        rounds = [[action for actions in there for action in actions] for there in rounds]
+        rounds[0][:0] = start_up + [place.greet]
+        return rounds, ends + waits
 
     def received(self, outs):
-        self.sums = outs
+        for (unit, first, stop), out in zip(self.units, outs):
+            if stop == unit.count:
+                unit.result = out
+            else:
+                unit.state = out
 
 
 def run_all(actions):
@@ -416,7 +568,8 @@
 
 
 def run_kernel(
-    body, args, *, grid, in_specs, out_specs, out_shape, name, scratch_shapes=(), exchange=None, polls=1
+    body, args, *, grid, in_specs, out_specs, out_shape, name, scratch_shapes=(), exchange=None, polls=1,
+    busy=0.0,
 ):
     if exchange is None:
         return pl.pallas_call(
@@ -431,6 +584,7 @@
         )(*args)
     counts = (len(args), len(exchange.arrays), len(out_shape), len(exchange.out_shape))
     total = functools.reduce(lambda a, b: a * b, grid, 1)
+    times = exchange.times()
 
     def kernel(*refs):
         refs = list(refs)
@@ -440,10 +594,14 @@
         for i, size in enumerate(grid):
             step = step * size + pl.program_id(i)
         rounds, last = exchange.rounds(sent, received, refs)
-        slots = {}
-        for i, actions in enumerate(rounds):
-            slot = i * total * polls // len(rounds)
-            slots.setdefault((slot % polls, slot // polls), []).extend(actions)
+        slots, spent, after = {}, 0.0, []
+        for actions, time in zip(rounds, times):
+            slot = int(total * polls * spent / busy + 0.5) if busy else total * polls
+            spent += time
+            if slot and slot >= total * polls:
+                after += actions
+            else:
+                slots.setdefault((slot % polls, slot // polls), []).extend(actions)
         called = [0]
 
         def poll():
@@ -455,7 +613,7 @@
 
         body(poll, *ins, *outs, *own)
         assert called[0] == polls
-        pl.when(step == total - 1)(functools.partial(run_all, last))
+        pl.when(step == total - 1)(functools.partial(run_all, after + last))
 
     outs = pl.pallas_call(
         kernel,
@@ -519,31 +677,50 @@
     return pl.BlockSpec(shape, lambda *_: (0,) * len(shape))
 
 
-def project_kernel(poll, x_ref, gain_ref, wq, wk, wv, normed, q, k, v):
+def project_kernel(
+    poll, valid, x_ref, gain_ref, cot, wq, wk, wv, normed_t, masked, masked_t, q, k, v, normed
+):
     @pl.when(pl.program_id(0) == 0)
     def _():
         x = x_ref[...].astype(F32)
-        normed[...] = (x * inverse_rms(x) * gain_ref[...]).astype(BF16)
-
-    poll()
+        rows = (x * inverse_rms(x) * gain_ref[...]).astype(BF16)
+        normed[...] = rows
+        normed_t[...] = rows.T
+        keep = position(cot.shape, 0) < valid[0]
+        grad = jnp.where(keep, cot[...], jnp.zeros_like(cot))
+        masked[...] = grad
+        masked_t[...] = grad.T
+
     rows = normed[...]
     for weight, out in ((wq, q), (wk, k), (wv, v)):
+        poll()
         out[...] = matmul(rows, weight[...]).astype(BF16)
 
 
-def project(x, gain, weights, exchange):
+def project(valid, x, gain, cot, weights, exchange):
     rows, width = x.shape
     tile = pl.BlockSpec((width, TILE), lambda j: (0, j))
     out = pl.BlockSpec((rows, TILE), lambda j: (0, j))
+    full = whole((rows, width))
+    turned = whole((width, rows))
     return run_kernel(
         project_kernel,
-        (x, gain, *weights),
+        (valid, x, gain, cot, *weights),
         grid=(width // TILE,),
-        in_specs=[whole((rows, width)), whole((1, width)), tile, tile, tile],
-        out_specs=[whole((rows, width)), out, out, out],
-        out_shape=[jax.ShapeDtypeStruct((rows, width), BF16)] * 4,
+        in_specs=[pl.BlockSpec(memory_space=pltpu.SMEM), full, whole((1, width)), full]
+        + [tile] * 3,
+        out_specs=[turned, full, turned, out, out, out],
+        out_shape=[
+            jax.ShapeDtypeStruct((width, rows), BF16),
+            jax.ShapeDtypeStruct((rows, width), BF16),
+            jax.ShapeDtypeStruct((width, rows), BF16),
+        ]
+        + [jax.ShapeDtypeStruct((rows, width), BF16)] * 3,
+        scratch_shapes=[pltpu.VMEM((rows, width), BF16)],
         name="project_tokens",
         exchange=exchange,
+        busy=14.0,
+        polls=3,
     )
 
 
@@ -608,7 +785,7 @@
 
 def state_forward_kernel(
     poll, valid, s0, gain, gate_bias, wq, wk, wv, wu, k, v,
-    normed_out, sq, sk, sv, read, log_out, update_out, states, last,
+    normed_t, sq, sk, sv, read, log_out, update_out, states, last,
     state, normed, total,
 ):
     block, pair = pl.program_id(0), pl.program_id(1)
@@ -622,7 +799,7 @@
         now = state[...]
         rows = (now * inverse_rms(now) * gain[...]).astype(BF16)
         normed[...] = rows
-        normed_out[...] = rows
+        normed_t[...] = rows.T
         states[...] = now
         total[...] = jnp.zeros_like(total)
 
@@ -630,6 +807,7 @@
     rows = normed[...]
     for weight, out in ((wq, sq), (wk, sk), (wv, sv)):
         out[...] = matmul(rows, weight[...]).astype(BF16)
+    poll()
     seen = block * BLOCK + position((BLOCK, BLOCK), 0) < valid[0]
     for head in range(2):
         lanes = pl.ds(head * HEAD, HEAD)
@@ -670,12 +848,13 @@
             pl.BlockSpec((BLOCK, PAIR), lambda b, p: (b, p)),
         ],
         out_specs=[
-            band, tile, tile, tile, tile,
+            pl.BlockSpec((width, rows), lambda b, p: (0, b)), tile, tile, tile, tile,
             pl.BlockSpec((1, 1, 2, rows), lambda b, p: (b, p, 0, 0)),
             band, band, whole((rows, width)),
         ],
         out_shape=[
-            stack(BF16), stack(BF16), stack(BF16), stack(BF16), stack(BF16),
+            jax.ShapeDtypeStruct((width, blocks * rows), BF16),
+            stack(BF16), stack(BF16), stack(BF16), stack(BF16),
             jax.ShapeDtypeStruct((blocks, pairs, 2, rows), F32),
             stack(F32), stack(F32), jax.ShapeDtypeStruct((rows, width), BF16),
         ],
@@ -685,11 +864,13 @@
         ],
         name="state_forward",
         exchange=exchange,
+        busy=27.7,
+        polls=2,
     )
 
 
 def token_forward_kernel(
-    poll, valid, x, gain, q, k, v, sk, sv, wo, mixed, log_out, resid, ynorm
+    poll, valid, x, gain, q, k, v, sk, sv, wo, mixed, log_out, resid, ynorm, ynorm_t
 ):
     pair = pl.program_id(0)
 
@@ -699,9 +880,9 @@
 
     count = valid[0]
     for head in range(2):
-        poll()
         lanes = pl.ds(head * HEAD, HEAD)
         for block in range(q.shape[0] // BLOCK):
+            poll()
             for half in range(BLOCK // TILE):
                 rows = pl.ds(block * BLOCK + half * TILE, TILE)
                 pieces = []
@@ -717,7 +898,9 @@
     @pl.when(pair == pl.num_programs(0) - 1)
     def _():
         rows = resid[...]
-        ynorm[...] = (rows * inverse_rms(rows) * gain[...]).astype(BF16)
+        rounded = (rows * inverse_rms(rows) * gain[...]).astype(BF16)
+        ynorm[...] = rounded
+        ynorm_t[...] = rounded.T
 
 
 def token_forward(valid, x, gain, q, k, v, sk, sv, wo, exchange):
@@ -735,24 +918,26 @@
         ],
         out_specs=[
             tile, pl.BlockSpec((1, 2, rows), lambda p: (p, 0, 0)),
-            whole((rows, width)), whole((rows, width)),
+            whole((rows, width)), whole((rows, width)), whole((width, rows)),
         ],
         out_shape=[
             jax.ShapeDtypeStruct((rows, width), BF16),
             jax.ShapeDtypeStruct((pairs, 2, rows), F32),
             jax.ShapeDtypeStruct((rows, width), F32),
             jax.ShapeDtypeStruct((rows, width), BF16),
+            jax.ShapeDtypeStruct((width, rows), BF16),
         ],
         name="token_forward",
         exchange=exchange,
-        polls=2,
+        busy=28.4,
+        polls=2 * rows // BLOCK,
     )
 
 
 def feed_forward_kernel(
-    first, final, poll, valid, ynorm, cot, total_in, grad_in, up_w, down_w,
+    first, final, poll, ynorm, ynorm_t, masked, masked_t, total_in, grad_in, up_w, down_w,
     out, grad_out, up_grad, down_grad,
-    ynorm_t, masked, masked_t, total, grad_total, sems,
+    total, grad_total, sems,
 ):
     step, last = pl.program_id(0), pl.num_programs(0) - 1
     loads = [pltpu.make_async_copy(total_in, total, sems.at[0])]
@@ -768,11 +953,6 @@
     def _():
         for copy in loads:
             copy.start()
-        keep = position(cot.shape, 0) < valid[0]
-        grad = jnp.where(keep, cot[...], jnp.zeros_like(cot))
-        masked[...] = grad
-        masked_t[...] = grad.T
-        ynorm_t[...] = ynorm[...].T
         if first:
             grad_total[...] = jnp.zeros_like(grad_total)
 
@@ -788,6 +968,7 @@
     grad_up = (grad_hidden * slope).astype(BF16)
     poll()
     down_grad[0] = matmul(masked_t[...], hidden).astype(BF16)
+    poll()
     up_grad[0] = matmul(ynorm_t[...], grad_up).astype(BF16)
 
     @pl.when(step == 0)
@@ -795,6 +976,7 @@
         for copy in loads:
             copy.wait()
 
+    poll()
     total[...] += matmul_nt(hidden, down_part)
     grad_total[...] += matmul_nt(grad_up, up_part)
 
@@ -808,21 +990,20 @@
             copy.wait()
 
 
-def feed_forward(first, final, valid, ynorm, cot, total, grad, up_w, down_w, exchange, chunk=512):
-    rows, width = ynorm.shape
+def feed_forward(first, final, rows_in, total, grad, up_w, down_w, exchange, chunk=512):
+    rows, width = total.shape
     parts, _, part = up_w.shape
     chunk = min(chunk, part)
     each = part // chunk
     weight = pl.BlockSpec((1, width, chunk), lambda j: (j // each, 0, j % each))
     once = pl.BlockSpec((rows, width), lambda j: (0, 0), pipeline_mode=pl.Buffered(1))
+    turned = pl.BlockSpec((width, rows), lambda j: (0, 0), pipeline_mode=pl.Buffered(1))
     anywhere = pl.BlockSpec(memory_space=pl.ANY)
     return run_kernel(
         functools.partial(feed_forward_kernel, first, final),
-        (valid, ynorm, cot, total, grad, up_w, down_w),
+        (*rows_in, total, grad, up_w, down_w),
         grid=(parts * each,),
-        in_specs=[
-            pl.BlockSpec(memory_space=pltpu.SMEM), once, once, anywhere, anywhere, weight, weight
-        ],
+        in_specs=[once, turned, once, turned, anywhere, anywhere, weight, weight],
         out_specs=[once if final else anywhere, anywhere, weight, weight],
         out_shape=[
             jax.ShapeDtypeStruct((rows, width), BF16 if final else F32),
@@ -831,31 +1012,49 @@
             jax.ShapeDtypeStruct(down_w.shape, BF16),
         ],
         scratch_shapes=[
-            pltpu.VMEM((width, rows), BF16), pltpu.VMEM((rows, width), BF16),
-            pltpu.VMEM((width, rows), BF16), pltpu.VMEM((rows, width), F32),
-            pltpu.VMEM((rows, width), F32), pltpu.SemaphoreType.DMA((2,)),
+            pltpu.VMEM((rows, width), F32), pltpu.VMEM((rows, width), F32),
+            pltpu.SemaphoreType.DMA((2,)),
         ],
         name="feed_forward_final" if final else "feed_forward_first",
         exchange=exchange,
-        polls=2,
+        busy=38.0,
+        polls=4,
     )
 
 
 def token_backward_kernel(
-    poll, valid, resid, gain, cot, grad_ynorm, q, k, v, sk, sv, wo, mixed, log_total,
-    grad_resid, gain_grad, dq, dk, dv, dsk, dsv, wo_grad,
-    rounded, grad_mixed, near_k, near_v, state_k, state_v,
+    poll, valid, resid, gain, masked, grad_ynorm, normed_t, snormed_t,
+    q, k, v, sk, sv, wo, mixed, log_total,
+    grad_resid, gain_grad, dq, dk, dv, dsk, dsv, wo_grad, wq_grad, skw_grad, svw_grad,
+    rounded, work, other, sems, grad_mixed, near_k, near_v, state_k, state_v,
 ):
+    loads = [
+        pltpu.make_async_copy(source, target, sems.at[i])
+        for i, (source, target) in enumerate(((resid, work), (grad_ynorm, other), (masked, rounded)))
+    ]
+    store = pltpu.make_async_copy(work, grad_resid, sems.at[3])
+
+    @pl.when(pl.program_id(0) == 0)
+    def _():
+        for copy in loads:
+            copy.start()
+
     poll()
 
     @pl.when(pl.program_id(0) == 0)
     def _():
-        grad, gain_rows = rms_backward(resid[...], gain[...], grad_ynorm[...])
-        keep = position(cot.shape, 0) < valid[0]
-        grad = jnp.where(keep, cot[...].astype(F32), 0.0) + grad
-        grad_resid[...] = grad
+        for copy in loads:
+            copy.wait()
+        grad, gain_rows = rms_backward(work[...], gain[...], other[...])
+        grad = rounded[...].astype(F32) + grad
+        work[...] = grad
         rounded[...] = grad.astype(BF16)
         gain_grad[...] = jnp.sum(gain_rows, axis=0, keepdims=True)
+        store.start()
+
+    @pl.when(pl.program_id(0) == pl.num_programs(0) - 1)
+    def _():
+        store.wait()
 
     grad_rows = rounded[...]
     grad_mixed[...] = matmul_nt(grad_rows, wo[...]).astype(BF16)
@@ -864,7 +1063,6 @@
         ref[...] = jnp.zeros_like(ref)
     count = valid[0]
     for head in range(2):
-        poll()
         lanes = pl.ds(head * HEAD, HEAD)
 
         def adder(ref, there):
@@ -874,6 +1072,7 @@
             return add
 
         for block in range(q.shape[0] // BLOCK):
+            poll()
             for half in range(BLOCK // TILE):
                 rows = pl.ds(block * BLOCK + half * TILE, TILE)
                 pieces = []
@@ -897,12 +1096,20 @@
     dv[...] = near_v[...]
     dsk[...] = state_k[...].astype(BF16)
     dsv[...] = state_v[...].astype(BF16)
+    wq_grad[...] = matmul(normed_t[...], dq[...]).astype(BF16)
+    skw_grad[...] = matmul(snormed_t[...], dsk[...]).astype(BF16)
+    svw_grad[...] = matmul(snormed_t[...], dsv[...]).astype(BF16)
 
 
 def token_backward(
-    valid, resid, gain, cot, grad_ynorm, q, k, v, sk, sv, wo, mixed, log_total, exchange
+    valid, resid, gain, masked, grad_ynorm, normed_t, snormed_t,
+    q, k, v, sk, sv, wo, mixed, log_total, exchange,
 ):
     rows, width = resid.shape
+    anywhere = pl.BlockSpec(memory_space=pl.ANY)
+    turned = pl.BlockSpec((width, rows), lambda p: (0, 0), pipeline_mode=pl.Buffered(1))
+    turned_state = pl.BlockSpec(snormed_t.shape, lambda p: (0, 0), pipeline_mode=pl.Buffered(1))
+    columns = pl.BlockSpec((width, PAIR), lambda p: (0, p))
     once = pl.BlockSpec((rows, width), lambda p: (0, 0), pipeline_mode=pl.Buffered(1))
     pairs = width // PAIR
     tile = pl.BlockSpec((rows, PAIR), lambda p: (0, p))
@@ -910,14 +1117,18 @@
     band = pl.BlockSpec((PAIR, width), lambda p: (p, 0))
     return run_kernel(
         token_backward_kernel,
-        (valid, resid, gain, cot, grad_ynorm, q, k, v, sk, sv, wo, mixed, log_total),
+        (
+            valid, resid, gain, masked, grad_ynorm, normed_t, snormed_t,
+            q, k, v, sk, sv, wo, mixed, log_total,
+        ),
         grid=(pairs,),
         in_specs=[
-            pl.BlockSpec(memory_space=pltpu.SMEM), once, whole((1, width)), once, once,
-            tile, tile, tile, states, states, band, tile,
+            pl.BlockSpec(memory_space=pltpu.SMEM), anywhere, whole((1, width)), anywhere, anywhere,
+            turned, turned_state, tile, tile, tile, states, states, band, tile,
             pl.BlockSpec((1, 2, rows), lambda p: (p, 0, 0)),
         ],
-        out_specs=[once, whole((1, width)), tile, tile, tile, states, states, band],
+        out_specs=[anywhere, whole((1, width)), tile, tile, tile, states, states, band]
+        + [columns] * 3,
         out_shape=[
             jax.ShapeDtypeStruct((rows, width), F32),
             jax.ShapeDtypeStruct((1, width), F32),
@@ -926,25 +1137,27 @@
             jax.ShapeDtypeStruct((rows, width), F32),
             jax.ShapeDtypeStruct(sk.shape, BF16),
             jax.ShapeDtypeStruct(sk.shape, BF16),
-            jax.ShapeDtypeStruct((width, width), BF16),
-        ],
+        ]
+        + [jax.ShapeDtypeStruct((width, width), BF16)] * 4,
         scratch_shapes=[
-            pltpu.VMEM((rows, width), BF16),
+            pltpu.VMEM((rows, width), BF16), pltpu.VMEM((rows, width), F32),
+            pltpu.VMEM((rows, width), F32), pltpu.SemaphoreType.DMA((4,)),
             pltpu.VMEM((rows, PAIR), BF16), pltpu.VMEM((rows, PAIR), F32),
             pltpu.VMEM((rows, PAIR), F32), pltpu.VMEM((sk.shape[0], PAIR), F32),
             pltpu.VMEM((sk.shape[0], PAIR), F32),
         ],
         name="token_backward",
         exchange=exchange,
-        polls=3,
+        busy=55.0,
+        polls=1 + 2 * rows // BLOCK,
     )
 
 
 def state_backward_kernel(
     poll, valid, cot, gain, gate_bias, wq, wk, wv, wu, states, updates,
-    sq, k, v, read, log_total, near_k, near_v, dsk, dsv,
-    dsq, dk, dv, dz_out, grad_state, gain_grad, bias_grad,
-    later, dz, total, grad_read, sum_q, sum_k, sum_v,
+    sq, k, v, read, log_total, near_k, near_v, dsk, dsv, read_last, normed_t, snormed_t,
+    dk, dv, grad_state, gain_grad, bias_grad, wk_grad, wv_grad, sqw_grad, wu_grad,
+    later, dz, total, grad_read, sum_k, sum_v, dsq, kept_dz, kept,
 ):
     step, pair = pl.program_id(0), pl.program_id(1)
     block = pl.num_programs(0) - 1 - step
@@ -961,7 +1174,11 @@
         grad = later[...]
         rounded = (grad * (1.0 - gate)).astype(BF16)
         dz[...] = rounded
-        dz_out[...] = rounded
+
+        @pl.when(step == 0)
+        def _():
+            kept_dz[...] = rounded
+
         bias_grad[...] += (
             jnp.sum(grad * (states[...] - updates[...]), axis=0, keepdims=True) * gate * (1.0 - gate)
         )
@@ -989,11 +1206,30 @@
             centre_of(out_grad, read[:, lanes]),
             [(k[:, lanes], v[:, lanes], seen, adder(sum_k), adder(sum_v))],
         ).astype(BF16)
+    poll()
     dk[...] = sum_k[...].astype(BF16)
     dv[...] = sum_v[...].astype(BF16)
     total[...] += (
         matmul_nt(dsq[...], wq[...]) + matmul_nt(dsk[...], wk[...]) + matmul_nt(dsv[...], wv[...])
     )
+
+    @pl.when(step == 0)
+    def _():
+        for i, ref in enumerate((dk, dv, dsq)):
+            kept[i, pair] = ref[...]
+
+    @pl.when(step == 1)
+    def _():
+        for i, (left, ref, out) in enumerate(
+            ((normed_t, dk, wk_grad), (normed_t, dv, wv_grad), (snormed_t, dsq, sqw_grad))
+        ):
+            half = left.shape[1] // 2
+            out[...] = (
+                matmul(left[:, :half], ref[...]) + matmul(left[:, half:], kept[i, pair])
+            ).astype(BF16)
+        wu_grad[...] = (
+            matmul(read[...].T, dz[...]) + matmul(read_last[...].T, kept_dz[...])
+        ).astype(BF16)
 
     @pl.when(pair == pl.num_programs(1) - 1)
     def _():
@@ -1006,7 +1242,7 @@
 
 def state_backward(
     valid, cot, gain, gate_bias, weights, update_weight, states, updates,
-    sq, k, v, read, log_total, near_k, near_v, dsk, dsv, exchange,
+    sq, k, v, read, log_total, near_k, near_v, dsk, dsv, normed_t, snormed_t, exchange,
 ):
     rows, width = cot.shape
     blocks, pairs = k.shape[0] // BLOCK, width // PAIR
@@ -1019,7 +1255,7 @@
         state_backward_kernel,
         (
             valid, cot, gain, gate_bias, *weights, update_weight, states, updates,
-            sq, k, v, read, log_total, near_k, near_v, dsk, dsv,
+            sq, k, v, read, log_total, near_k, near_v, dsk, dsv, read, normed_t, snormed_t,
         ),
         grid=(blocks, pairs),
         in_specs=[
@@ -1028,106 +1264,69 @@
             band, band, tile, token, token, tile,
             pl.BlockSpec((1, 1, 2, rows), lambda s, p: (blocks - 1 - s, p, 0, 0)),
             token, token, tile, tile,
+            pl.BlockSpec((rows, PAIR), lambda s, p: (blocks - 1, p)),
+            pl.BlockSpec(normed_t.shape, lambda s, p: (0, 0), pipeline_mode=pl.Buffered(1)),
+            pl.BlockSpec(snormed_t.shape, lambda s, p: (0, 0), pipeline_mode=pl.Buffered(1)),
         ],
-        out_specs=[tile, token, token, band, whole((rows, width)), small, small],
+        out_specs=[token, token, whole((rows, width)), small, small]
+        + [pl.BlockSpec((width, PAIR), lambda s, p: (0, p * s))] * 3
+        + [pl.BlockSpec((PAIR, width), lambda s, p: (p * s, 0))],
         out_shape=[
-            jax.ShapeDtypeStruct((blocks * rows, width), BF16),
             jax.ShapeDtypeStruct(k.shape, BF16),
             jax.ShapeDtypeStruct(k.shape, BF16),
-            jax.ShapeDtypeStruct((blocks * rows, width), BF16),
             jax.ShapeDtypeStruct((rows, width), F32),
             jax.ShapeDtypeStruct((1, width), F32),
             jax.ShapeDtypeStruct((1, width), F32),
-        ],
+        ]
+        + [jax.ShapeDtypeStruct((width, width), BF16)] * 4,
         scratch_shapes=[
             pltpu.VMEM((rows, width), F32), pltpu.VMEM((rows, width), BF16),
             pltpu.VMEM((rows, width), F32), pltpu.VMEM((rows, PAIR), BF16),
-            pltpu.VMEM((rows, PAIR), F32), pltpu.VMEM((BLOCK, PAIR), F32),
-            pltpu.VMEM((BLOCK, PAIR), F32),
+            pltpu.VMEM((BLOCK, PAIR), F32), pltpu.VMEM((BLOCK, PAIR), F32),
+            pltpu.VMEM((rows, PAIR), BF16), pltpu.VMEM((rows, width), BF16),
+            pltpu.VMEM((3, pairs, BLOCK, PAIR), BF16),
         ],
         name="state_backward",
         exchange=exchange,
-    )
-
-
-def weight_grad_kernel(counts, poll, *refs):
-    refs = list(refs)
-    lefts = [refs.pop(0) for _ in counts]
-    rights = [[refs.pop(0) for _ in range(n)] for n in counts]
-    outs = [[refs.pop(0) for _ in range(n)] for n in counts]
+        busy=51.0,
+        polls=2,
+    )
+
+
+def token_grad_kernel(
+    plan, poll, x, gain, grad_resid, dq, dk, dv, wq, wk, wv, grad_x, gain_grad
+):
+    plan.first_row = gain_grad
     poll()
 
     @pl.when(pl.program_id(0) == 0)
     def _():
-        for left, left_t in zip(lefts, refs):
-            left_t[...] = left[...].T
-
-    for left_t, group, out_group in zip(refs, rights, outs):
-        for right, out in zip(group, out_group):
-            out[...] = matmul(left_t[...], right[...]).astype(BF16)
-
-
-def weight_grad(pairs, name, exchange):
-    lefts = [left for left, _ in pairs]
-    rights = [right for _, group in pairs for right in group]
-    rows, width = lefts[0].shape
-    tile = pl.BlockSpec((rows, TILE), lambda j: (0, j))
-    out = pl.BlockSpec((width, TILE), lambda j: (0, j))
-    return run_kernel(
-        functools.partial(weight_grad_kernel, [len(group) for _, group in pairs]),
-        (*lefts, *rights),
-        grid=(width // TILE,),
-        in_specs=[whole((rows, width))] * len(lefts) + [tile] * len(rights),
-        out_specs=[out] * len(rights),
-        out_shape=[jax.ShapeDtypeStruct((width, width), BF16)] * len(rights),
-        scratch_shapes=[pltpu.VMEM((width, rows), BF16)] * len(lefts),
-        name=name,
-        exchange=exchange,
-    )
-
-
-def token_grad_kernel(
-    poll, x, gain, grad_resid, dq, dk, dv, wq, wk, wv, normed, dq_tile, dk_tile, dv_tile,
-    grad_x, gain_grad, wq_grad, wk_grad, wv_grad, normed_t,
-):
+        gain_grad[...] = jnp.zeros_like(gain_grad)
+
+    grad_normed = matmul_nt(dq[...], wq[...]) + matmul_nt(dk[...], wk[...])
     poll()
-
-    @pl.when(pl.program_id(0) == 0)
-    def _():
-        gain_grad[...] = jnp.zeros_like(gain_grad)
-        normed_t[...] = normed[...].T
-
-    for right, out in ((dq_tile, wq_grad), (dk_tile, wk_grad), (dv_tile, wv_grad)):
-        out[...] = matmul(normed_t[...], right[...]).astype(BF16)
-    poll()
-    grad_normed = (
-        matmul_nt(dq[...], wq[...]) + matmul_nt(dk[...], wk[...]) + matmul_nt(dv[...], wv[...])
-    )
+    grad_normed = grad_normed + matmul_nt(dv[...], wv[...])
     grad, gain_rows = rms_backward(x[...].astype(F32), gain[...], grad_normed)
     grad_x[...] = grad_resid[...] + grad
     gain_grad[...] += jnp.sum(gain_rows, axis=0, keepdims=True)
 
 
-def token_grad(x, gain, grad_resid, grads, weights, normed, exchange):
+def token_grad(x, gain, grad_resid, grads, weights, plan, exchange):
     rows, width = x.shape
     band = pl.BlockSpec((TILE, width), lambda i: (i, 0))
-    tile = pl.BlockSpec((rows, TILE), lambda i: (0, i))
-    out = pl.BlockSpec((width, TILE), lambda i: (0, i))
     weight = pl.BlockSpec((width, width), lambda i: (0, 0), pipeline_mode=pl.Buffered(1))
     return run_kernel(
-        token_grad_kernel,
-        (x, gain, grad_resid, *grads, *weights, normed, *grads),
+        functools.partial(token_grad_kernel, plan),
+        (x, gain, grad_resid, *grads, *weights),
         grid=(rows // TILE,),
-        in_specs=[band, whole((1, width)), band, band, band, band, weight, weight, weight]
-        + [weight, tile, tile, tile],
-        out_specs=[band, whole((1, width)), out, out, out],
+        in_specs=[band, whole((1, width)), band, band, band, band, weight, weight, weight],
+        out_specs=[band, whole((1, width))],
         out_shape=[
             jax.ShapeDtypeStruct((rows, width), F32), jax.ShapeDtypeStruct((1, width), F32)
-        ]
-        + [jax.ShapeDtypeStruct((width, width), BF16)] * 3,
-        scratch_shapes=[pltpu.VMEM((width, rows), BF16)],
+        ],
         name="token_grad",
         exchange=exchange,
+        busy=13.8,
         polls=2,
     )
 
@@ -1137,50 +1336,62 @@
 
 
 def plan_gather(sizes, small, square, forward):
-    width, part = square[0].shape[1], forward[0].shape[1]
-    arrays = [small] + square + forward
+    width, half = square[0].shape[1], forward[0].shape[1]
     pieces = cut(width, SQUARE_PIECES)
     can_share = pieces[0][1] // sizes["m"] % 128 == 0
-    lone = [
-        (1 + i, columns)
-        for trio in ((0, 1, 2), (3, 4, 5), (6, 7))
-        for columns in pieces
-        for i in trio
+    units = [(0, "zx", False, (0, small.shape[1]), 0)]
+    for group, start in zip(((0, 1, 2), (3, 4, 5), (6,), (7,)), GATHER_SQUARE):
+        if len(group) == 1:
+            spans = [pieces]
+        else:
+            spans = [[columns] for columns in pieces]
+        for n, span in enumerate(spans):
+            for j, (i, columns) in enumerate((i, columns) for columns in span for i in group):
+                shared = can_share and j > 0
+                units.append((1 + i, "zxm" if shared else "zx", shared, columns, start + n))
+    for i, start in enumerate(GATHER_FORWARD):
+        for n, columns in enumerate(cut(half, FORWARD_PIECES)):
+            units.append((9 + i, ("zxm", "zmx")[n % 2], False, columns, start + n // 2))
+    return Gather(sizes, [small] + square + forward, units)
+
+
+def forward_units(arrays, start):
+    units = []
+    for i, array in enumerate(arrays):
+        for n, columns in enumerate(cut(array.shape[-1], FORWARD_PIECES)):
+            units.append((i, ("mxz", "xmz")[n % 2], False, columns))
+    return [unit + (start + n // 2,) for n, unit in enumerate(units)]
+
+
+def square_units(sizes, arrays, start, group, pieces):
+    units = []
+    for columns in cut(arrays[0].shape[-1], pieces):
+        for i in range(len(arrays)):
+            shared = len(units) % 3 > 0 and columns[1] // sizes["m"] % 128 == 0
+            units.append((i, "mxz" if shared else "xz", shared, columns))
+    return [unit + (start + n // group,) for n, unit in enumerate(units)]
+
+
+def finish_kernel(counts, *refs):
+    refs = list(refs)
+    parts = [[refs.pop(0) for _ in range(n)] for n in counts]
+    for group, out in zip(parts, refs):
+        first = 0
+        for part in group:
+            out[:, pl.ds(first, part.shape[1])] = part[...]
+            first += part.shape[1]
+
+
+def finish(groups):
+    shapes = [
+        jax.ShapeDtypeStruct((g[0].shape[0], sum(p.shape[1] for p in g)), F32) for g in groups
     ]
-    units, together = [(0, "zx", False, (0, small.shape[1]))], [4]
-    for n, (i, columns) in enumerate(lone):
-        shared = can_share and n % 3 > 0
-        units.append((i, "zxm" if shared else "zx", shared, columns))
-        if n % 3 == 0 and n:
-            together.append(0)
-        if n >= 3:
-            together[-1] += 1
-    for i in range(4):
-        for columns in cut(part, FORWARD_PIECES):
-            units.append((9 + i, "zmx" if len(units) % 2 else "zxm", False, columns))
-        together += [2] * (FORWARD_PIECES // 2)
-    return Gather(sizes, arrays, units, together)
-
-
-def plan_scatter(sizes, arrays, pieces, collective_id, group):
-    units = []
-    for columns in range(pieces):
-        for i, array in enumerate(arrays):
-            width = array.shape[-1]
-            if array.dtype == F32:
-                if columns == 0:
-                    units.append((i, "xz", False, (0, width)))
-                continue
-            there = cut(width, pieces)[columns]
-            if array.ndim == 6:
-                units.append((i, ("mxz", "xmz")[len(units) % 2], False, there))
-            else:
-                shared = len(units) % 3 > 0 and there[1] // sizes["m"] % 128 == 0
-                units.append((i, "mxz" if shared else "xz", shared, there))
-    together = [group] * (len(units) // group)
-    if len(units) % group:
-        together.append(len(units) % group)
-    return Scatter(sizes, arrays, units, together, collective_id)
+    return pl.pallas_call(
+        functools.partial(finish_kernel, [len(g) for g in groups]),
+        out_shape=shapes,
+        compiler_params=pltpu.CompilerParams(vmem_limit_bytes=VMEM_LIMIT),
+        name="finish",
+    )(*[part for g in groups for part in g])
 
 
 def shards(
@@ -1243,21 +1454,21 @@
     gains = gains.transpose(1, 0, 2).reshape(4, 1, width).astype(F32)
     token_gain, state_gain, mlp_gain, gate_bias = [gains[i] for i in range(4)]
     token_weights = full(1, 2, 3)
-    normed, q, k, v = project(
-        x, token_gain, token_weights, plan.until(plan.ready((4, 5, 6, 7)), 2)
+    normed_t, masked, masked_t, q, k, v = project(
+        valid, x, token_gain, cot, token_weights, plan.until(plan.ready((4, 5, 6, 7)), 2)
     )
     state_weights, (wu,) = full(4, 5, 6), full(7)
     ready = plan.ready((9, 10))
-    middle = max(plan.ready((8,)), (plan.round + ready) // 2)
-    snormed, sq, sk, sv, read, read_log, updates, states, last = state_forward(
+    middle = max(plan.ready((8,)), GATHER_MIDDLE)
+    snormed_t, sq, sk, sv, read, read_log, updates, states, last = state_forward(
         valid, s0, state_gain, gate_bias, state_weights, wu, k, v, plan.until(middle, 3)
     )
     (wo,) = full(8)
-    mixed, token_log, resid, ynorm = token_forward(
+    mixed, token_log, resid, *ynorms = token_forward(
         valid, x, mlp_gain, q, k, v, sk, sv, wo, plan.until(ready, 4)
     )
     total, grad_total, *first_grads = feed_forward(
-        True, False, valid, ynorm, cot, resid, resid, *forward_full(9, 10),
+        True, False, (*ynorms, masked, masked_t), resid, resid, *forward_full(9, 10),
         plan.until(plan.ready((11, 12)), 5),
     )
 
@@ -1268,50 +1479,75 @@
             for g in grads
         ]
 
-    first_sums = plan_scatter(sizes, parted(first_grads), FORWARD_PIECES, 6, 2)
+    sums = Scatter(sizes)
+    rounds = iter(SCATTER_ROUNDS)
+
+    def next_rounds(collective_id):
+        return sums.until(sums.round + next(rounds), collective_id)
+
+    units_first = sums.add(parted(first_grads), forward_units(first_grads, 0))
     out, grad_total, *last_grads = feed_forward(
-        False, True, valid, ynorm, cot, total, grad_total, *forward_full(11, 12), first_sums
-    )
-    last_sums = plan_scatter(sizes, parted(last_grads), FORWARD_PIECES, 7, 2)
-    grad_resid, mlp_gain_grad, dq, near_k, near_v, dsk, dsv, wo_grad = token_backward(
-        valid, resid, mlp_gain, cot, grad_total, q, k, v, sk, sv, wo, mixed, token_log, last_sums
-    )
-    out_sum = plan_scatter(sizes, parted([wo_grad]), SQUARE_PIECES // 2, 8, 1)
-    dsq, dk, dv, dz, grad_state, state_gain_grad, bias_grad = state_backward(
+        False, True, (*ynorms, masked, masked_t), total, grad_total, *forward_full(11, 12),
+        next_rounds(6),
+    )
+    units_last = sums.add(parted(last_grads), forward_units(last_grads, sums.round))
+    grad_resid, mlp_gain_grad, dq, near_k, near_v, dsk, dsv, *early_grads = token_backward(
+        valid, resid, mlp_gain, masked, grad_total, normed_t, snormed_t,
+        q, k, v, sk, sv, wo, mixed, token_log, next_rounds(7),
+    )
+    units_early = sums.add(
+        parted(early_grads), square_units(sizes, early_grads, sums.round, 4, SCATTER_PIECES)
+    )
+    dk, dv, grad_state, state_gain_grad, bias_grad, *late_grads = state_backward(
         valid, final_state_cotangent[0], state_gain, gate_bias, state_weights, wu,
-        states, updates, sq, k, v, read, read_log, near_k, near_v, dsk, dsv, out_sum,
-    )
-    state_grads = weight_grad([(read, [dz]), (snormed, [dsq, dsk, dsv])], "weight_grad", None)
-    state_sums = plan_scatter(sizes, parted(state_grads), SQUARE_PIECES // 2, 9, 4)
-    grad_tokens, token_gain_grad, *token_grads = token_grad(
-        x, token_gain, grad_resid, [dq, dk, dv], token_weights, normed, state_sums
-    )
-    small_grads = jnp.concatenate([token_gain_grad, state_gain_grad, mlp_gain_grad, bias_grad])
-    small_grads = small_grads.reshape(4, seg_size, rows).transpose(1, 0, 2)
-    small_grads = small_grads.reshape(seg_size, -1, 128)
-    lines = small_grads.shape[1]
-    small_grads = jnp.pad(small_grads, ((0, 0), (0, 8 - lines), (0, 0)))
-    small_grads = small_grads.reshape(seg_size // 4, 2, 2, 8, 128)
-    token_sums = plan_scatter(
-        sizes, [small_grads] + parted(token_grads), SQUARE_PIECES // 2, 10, 4
-    )
-    exchange_alone(token_sums, "scatter_last")
-    small_sum, *token_sums = token_sums.sums
-    small_sum = small_sum[:lines].reshape(4, rows)
-    update_sum, *state_sums = state_sums.sums
-    forward_sums = [
-        jnp.concatenate([a, b], axis=1) for a, b in zip(first_sums.sums, last_sums.sums)
-    ]
+        states, updates, sq, k, v, read, read_log, near_k, near_v, dsk, dsv, normed_t, snormed_t,
+        next_rounds(8),
+    )
+    units_late = sums.add(
+        parted(late_grads), square_units(sizes, late_grads, sums.round, 4, SCATTER_PIECES)
+    )
+    small_unit = sums.add_small(
+        jnp.concatenate(
+            [jnp.zeros_like(mlp_gain_grad), state_gain_grad, mlp_gain_grad, bias_grad]
+            + [jnp.zeros((4, width), F32)]
+        )
+    )
+    grad_tokens, _ = token_grad(
+        x, token_gain, grad_resid, [dq, dk, dv], token_weights, sums, sums.until(sums.all(), 9)
+    )
+    small_sum = small_unit.result[:4].reshape(4, seg_size, rows)
+    small_sum = lax.dynamic_index_in_dim(small_sum, lax.axis_index("seg"), 1, keepdims=False)
+
+    def group(units, i, count):
+        return [unit.result for unit in units[i::count]]
+
+    def forward_group(i):
+        return [
+            unit.result
+            for units in (units_first, units_last)
+            for unit in units[i * FORWARD_PIECES : (i + 1) * FORWARD_PIECES]
+        ]
+
+    weight_sums = finish(
+        [
+            group(units_early, 1, 4),
+            group(units_late, 0, 4),
+            group(units_late, 1, 4),
+            group(units_early, 0, 4),
+            group(units_late, 2, 4),
+            group(units_early, 2, 4),
+            group(units_early, 3, 4),
+            group(units_late, 3, 4),
+            forward_group(0),
+            forward_group(1),
+        ]
+    )
     return (
         out[None],
         last[None],
         grad_tokens[None],
         grad_state[None],
-        *token_sums,
-        *out_sum.sums,
-        *state_sums,
-        update_sum,
-        *forward_sums,
+        *weight_sums,
         *[small_sum[i] for i in range(4)],
     )
 

time: 574 us -> 503 us (0.88)
  Pallas kernels: 539 us -> 477 us
  local copies, waits for them, and re-layouts: 21.8 us -> 15.9 us
    pallas_call x10 -> x9, Pallas kernels: 524 us -> 473 us  [run_kernel(): pl.pallas_call(kernel, grid=grid, in_specs=list(in_specs) + exchange.spec...]
    pallas_call x1, Pallas kernels: 14.8 us -> 3.78 us  [finish(): pl.pallas_call(functools.partial(finish_kernel, [len(g) for g in groups])...]
    unnamed x51 -> x17, local copies, waits for them, and re-layouts: 14.3 us -> 8.62 us
where the time goes in v4:
time: 503 us; the launch traced here: 495 us
  Pallas kernels  477 us (95%)
  local copies, waits for them, and re-layouts  15.9 us (3%)
    pallas_call x9, Pallas kernels, run_kernel(): pl.pallas_call(kernel, grid=grid, in_specs=list(in_specs) + exchange.spec...  473 us

profile of v4, /device:TPU:0, one launch (start us, length us, event | category | flops | bytes accessed | tf_op | source)
XLA Modules:
  0.0 495.1 jit_solution(9033947877047740992)
XLA Ops:
  0.7 0.8 maximum_bitcast_fusion
  1.4 0.6 pad.4.refs_0_
  2.0 71.3 %gather_first.1 = (bf16[4,2,2,16,128]{4,3,2,1,0:T(8,128)(2,1)}, bf16[4,2,2,64,1024]{4,3,2,1,0:T(8,128)(2,1)}, bf16[4,2,2,64,1024]{4,3,2,1,0:T(8,128)(2,1)}, bf16...) custom-call(bf16[16,128]{1,0:T(8,128)(2,1)} %pad.4.refs_0_, ...), custom_call_target="tpu_custom_call" | custom-call | tf_op jit(solution)/shard_map/gather_first/pallas_call | solution.py:618
  73.3 0.9 copy.49
  74.2 0.1 reshape.177
  74.3 0.1 slice_reduce_fusion
  74.4 0.7 squeeze.40.refs_2_.refs_1_
  75.0 1.9 fusion.4
  77.6 41.7 %project_tokens.1 = (bf16[1024,1024]{1,0:T(8,128)(2,1)}, bf16[1024,1024]{1,0:T(8,128)(2,1)}, bf16[1024,1024]{1,0:T(8,128)(2,1)}, bf16[1024,1024]{1,0:T(8,128)(2,...) custom-call(s32[1]{0:T(128)S(6)} %copy.64.refs_0_, ...), custom_call_target="tpu_custom_call", output_to_operand_aliasing={{6}: (13, {}), {7}: (14, {}), {8}: (15, {}), {9}: (16, {})} | custom-call | tf_op jit(solution)/shard_map/project_tokens/pallas_call | solution.py:618
  119.3 0.7 squeeze.43.refs_2_
  120.0 0.7 squeeze.44.refs_3_
  120.6 38.1 %state_forward.1 = (bf16[1024,1024]{1,0:T(8,128)(2,1)}, bf16[1024,1024]{1,0:T(8,128)(2,1)}, bf16[1024,1024]{1,0:T(8,128)(2,1)}, bf16[1024,1024]{1,0:T(8,128)(2,1...) custom-call(s32[1]{0:T(128)S(6)} %copy.64.refs_0_, ...), custom_call_target="tpu_custom_call", output_to_operand_aliasing={{9}: (13, {}), {10}: (14, {})} | custom-call | tf_op jit(solution)/shard_map/state_forward/pallas_call | solution.py:618
  158.8 0.7 squeeze.39.refs_2_
  159.4 34.3 %token_forward.1 = (bf16[1024,1024]{1,0:T(8,128)(2,1)}, f32[4,2,1024]{2,1,0:T(2,128)}, f32[1024,1024]{1,0:T(8,128)}, bf16[1024,1024]{1,0:T(8,128)(2,1)}, bf16[10...) custom-call(s32[1]{0:T(128)S(6)} %copy.64.refs_0_, ...), custom_call_target="tpu_custom_call", output_to_operand_aliasing={{5}: (13, {}), {6}: (14, {})} | custom-call | tf_op jit(solution)/shard_map/token_forward/pallas_call | solution.py:618
  193.7 44.1 %feed_forward_first.1 = (f32[1024,1024]{1,0:T(8,128)}, f32[1024,1024]{1,0:T(8,128)}, bf16[2,1024,1024]{2,1,0:T(8,128)(2,1)}, bf16[2,1024,1024]{2,1,0:T(8,128)(2,...) custom-call(bf16[1024,1024]{1,0:T(8,128)(2,1)} %get-tuple-element.16, ...), custom_call_target="tpu_custom_call", output_to_operand_aliasing={{4}: (10, {}), {5}: (11, {})} | custom-call | tf_op jit(solution)/shard_map/feed_forward_first/pallas_call | solution.py:618
  237.8 47.6 %feed_forward_final.1 = (bf16[1024,1024]{1,0:T(8,128)(2,1)}, f32[1024,1024]{1,0:T(8,128)}, bf16[2,1024,1024]{2,1,0:T(8,128)(2,1)}, bf16[2,1024,1024]{2,1,0:T(8,1...) custom-call(bf16[1024,1024]{1,0:T(8,128)(2,1)} %get-tuple-element.16, ...), custom_call_target="tpu_custom_call" | custom-call | tf_op jit(solution)/shard_map/feed_forward_final/pallas_call | solution.py:618
  285.5 58.7 %token_backward.1 = (f32[1024,1024]{1,0:T(8,128)}, f32[1,1024]{1,0:T(1,128)}, bf16[1024,1024]{1,0:T(8,128)(2,1)}, f32[1024,1024]{1,0:T(8,128)}, f32[1024,1024]{1...) custom-call(s32[1]{0:T(128)S(6)} %copy.64.refs_0_, ...), custom_call_target="tpu_custom_call" | custom-call | tf_op jit(solution)/shard_map/token_backward/pallas_call | solution.py:618
  344.2 0.0 copy-start.5
  344.2 62.2 %state_backward.1 = (bf16[1024,1024]{1,0:T(8,128)(2,1)}, bf16[1024,1024]{1,0:T(8,128)(2,1)}, f32[512,1024]{1,0:T(8,128)}, f32[1,1024]{1,0:T(1,128)}, f32[1,1024]...) custom-call(s32[1]{0:T(128)S(6)} %copy.64.refs_0_, ...), custom_call_target="tpu_custom_call" | custom-call | tf_op jit(solution)/shard_map/state_backward/pallas_call | solution.py:618
  406.4 0.0 copy-done.5
  406.5 1.3 concatenate.7.refs_25_
  407.8 74.9 %token_grad.1 = (f32[1024,1024]{1,0:T(8,128)}, f32[1,1024]{1,0:T(1,128)}, f32[64,512]{1,0:T(8,128)}, f32[64,512]{1,0:T(8,128)}, f32[64,512]{1,0:T(8,128)}, /*ind...) custom-call(bf16[1024,1024]{1,0:T(8,128)(2,1)} %bitcast.51, ...), custom_call_target="tpu_custom_call" | custom-call | tf_op jit(solution)/shard_map/token_grad/pallas_call | solution.py:618
  482.7 0.0 copy-start.4
  482.7 0.0 copy-start.1
  482.7 0.0 copy-start.3
  482.7 3.8 finish.1
  486.5 0.0 copy-done.4
  486.5 0.1 reshape.176
  486.6 0.5 fusion
  487.1 0.0 copy-done.1
  487.1 0.0 copy-start
  487.1 1.3 copy.65
  488.4 0.0 copy-done.3
  488.4 1.0 copy.66
  489.4 1.0 copy-done
  490.4 0.0 copy-start.2
  490.4 2.1 copy.67
  492.6 1.0 copy-done.2
  493.6 1.3 copy.68
  (4 shorter events, 0.0 us)
Async XLA Ops:
  344.2 62.3 %copy-start.5 = (f32[1,1024]{1,0:T(1,128)S(1)}, f32[1,1024]{1,0:T(1,128)}, u32[]{:S(2)}) copy-start(f32[1,1024]{1,0:T(1,128)} %get-tuple-element.225) | copy-start | bytes 12292
  482.7 3.8 copy-start.4
  482.7 4.4 copy-start.1
  482.7 5.8 %copy-start.3 = (bf16[512,1024]{1,0:T(8,128)(2,1)S(1)}, bf16[512,1024]{1,0:T(8,128)(2,1)}, u32[]{:S(2)}) copy-start(bf16[512,1024]{1,0:T(8,128)(2,1)} %get-tuple-element.179) | copy-start | bytes 3145732
  487.1 3.3 copy-start
  490.4 3.1 copy-start.2

commit v5 on v4

--- a/solution.py
+++ b/solution.py
@@ -9,16 +9,27 @@
 BF16 = jnp.bfloat16
 F32 = jnp.float32
 VMEM_LIMIT = 60 << 20
-SQUARE_PIECES = 2
-FORWARD_PIECES = 2
-SCATTER_PIECES = 2
-GATHER_SQUARE = (0, 2, 4, 5)
-GATHER_FORWARD = (7, 8, 10, 11)
-GATHER_MIDDLE = 10
+GATHER_SQUARE = (
+    ((0, 1), ("zx", "zxm", "zxm"), 1),
+    ((2, 3), ("zx", "zxm", "zxm"), 1),
+    ((4, 4), ("zx", "zxm"), 1),
+    ((5, 5), ("zx", "zxm"), 1),
+)
+GATHER_FORWARD = (((6, 6), 1), ((7, 7), 1), ((9, 9), 1), ((10, 10), 1))
+GATHER_MIDDLE = 9
+SCATTER_FIRST = ((("mxz", 0, 1), ("xmz", 0, 1)), (("mxz", 1, 1), ("xmz", 1, 1)))
+SCATTER_LAST = SCATTER_FIRST
+SCATTER_EARLY = (
+    (("xz", 0, 1), ("mxz", 0, 1), ("mxz", 0, 1), ("xz", 0, 1)),
+    (("mxz", 1, 1), ("mxz", 1, 1), ("xz", 1, 1), ("mxz", 1, 1)),
+)
+SCATTER_LATE = SCATTER_EARLY
 SCATTER_ROUNDS = (3, 3, 3)
-LINK_RATE = 92e3
+LINK_RATE = 85e3
 CORE_RATE = 560e3
-ROUND_COST = 2.0
+START_COST = 2.5
+STEP_COST = 0.3
+LATENCY = 2.0
 
 
 class Place:
@@ -93,18 +104,19 @@
         return waits
 
 
-def gather_steps(flow, source, target, order, split, columns, local_sem, begin, end):
+def gather_steps(flow, source, target, order, split, columns, skipped, local_sem, begin, end):
     place = flow.place
     at, sizes = place.at, place.sizes
     lead = ("m" if len(target.shape) == 6 else "") + "zxc"
     first_column, width = columns
     share = width // sizes["m"] if split else width
 
-    def block(done, moved):
+    def block(done, moved, skip=0):
+        first = first_column + skip
         if not split or "m" in done:
-            lanes = pl.ds(first_column, width)
+            lanes = pl.ds(first, width)
         else:
-            lanes = pl.ds(pl.multiple_of(first_column + moved.get("m", at["m"]) * share, 128), share)
+            lanes = pl.ds(pl.multiple_of(first + moved.get("m", at["m"]) * share, 128), share)
         return (pl.ds(0, source.shape[0]), lanes)
 
     def view(done, **moved):
@@ -114,7 +126,7 @@
         return target.at[index + block(done, moved)]
 
     def own_source():
-        return source.at[block("", {})]
+        return source.at[block("", {}, skipped)]
 
     def own():
         return pltpu.make_async_copy(own_source(), view(""), local_sem)
@@ -160,9 +172,9 @@
 
 
 class ScatterUnit:
-    def __init__(self, sizes, grad, order, split, columns, start):
+    def __init__(self, sizes, grad, order, split, columns, start, stride):
         self.sizes, self.grad, self.order, self.split = sizes, grad, order, split
-        self.columns, self.start = columns, start
+        self.columns, self.start, self.stride = columns, start, stride
         self.whole_m = grad.ndim == 6
         self.lead = ("m" if self.whole_m else "") + "zx"
         self.rows, self.width = grad.shape[-2], columns[1]
@@ -300,20 +312,21 @@
 
 
 def round_times(sizes, rounds):
-    times = []
+    now, free, ended, times = START_COST, {axis: 0.0 for axis in "zxcm"}, {}, []
     for there in rounds:
-        load = {axis: 0.0 for axis in "zxcm"}
-        for axis, size in there:
-            load[axis] += step_time(sizes, axis, size)
-        times.append(max(load.values()) + ROUND_COST)
-    return times
+        for unit, step, axis, size in there:
+            now = max(now, ended.get((unit, step - 1), 0.0)) + STEP_COST
+            free[axis] = max(free[axis], now) + step_time(sizes, axis, size)
+            ended[unit, step] = free[axis] + LATENCY
+        times.append(now)
+    return times, max(ended.values())
 
 
 class Gather:
-    def __init__(self, sizes, arrays, units):
-        self.sizes, self.arrays, self.round = sizes, arrays, 0
-        self.units = [unit[:-1] for unit in units]
-        self.starts = [unit[-1] for unit in units]
+    def __init__(self, sizes, arrays, spans, units):
+        self.sizes, self.arrays, self.spans, self.round = sizes, arrays, spans, 0
+        self.units = [unit[:-2] for unit in units]
+        self.starts = [unit[-2:] for unit in units]
         self.targets = [None] * len(arrays)
 
     def ready(self, names):
@@ -322,7 +335,7 @@
         )
 
     def stop(self, start, unit):
-        return start + len(unit[1]) + 1
+        return start[0] + len(unit[1]) * start[1] + 1
 
     def until(self, end, collective_id):
         begin, self.round = self.round, max(end, self.round)
@@ -335,7 +348,7 @@
         self.units = [
             (start, unit)
             for start, unit in zip(plan.starts, plan.units)
-            if start < end and plan.stop(start, unit) > begin
+            if start[0] < end and plan.stop(start, unit) > begin
         ]
         self.names = sorted({unit[0] for _, unit in self.units})
         split = {unit[0]: unit[2] for _, unit in self.units}
@@ -349,7 +362,7 @@
             jax.ShapeDtypeStruct(
                 ((sizes["m"],) if "m" in order[n] and not split[n] else ())
                 + (sizes["z"], 2, 2)
-                + plan.arrays[n].shape,
+                + (plan.arrays[n].shape[0], plan.spans[n][1]),
                 plan.arrays[n].dtype,
             )
             for n in self.names
@@ -363,18 +376,21 @@
             pltpu.SemaphoreType.DMA((len(self.units),)),
         ]
 
-    def times(self):
-        rounds = [[] for _ in range(self.end - self.begin)]
+    def times(self, busy):
         sizes = self.plan.sizes
-        for start, (n, order, split, columns) in self.units:
+        loads = [{axis: 0.0 for axis in "zxcm"} for _ in range(self.end - self.begin)]
+        for (start, stride), (n, order, split, columns) in self.units:
             size = self.plan.arrays[n].shape[0] * columns[1] * self.plan.arrays[n].dtype.itemsize
             if split:
                 size //= sizes["m"]
             for i, axis in enumerate(order + "c"):
-                if self.begin <= start + i < self.end:
-                    rounds[start + i - self.begin].append((axis, size))
+                if self.begin <= start + i * stride < self.end:
+                    loads[start + i * stride - self.begin][axis] += step_time(sizes, axis, size)
                 size *= sizes[axis]
-        return round_times(sizes, rounds)
+        times = [0.0]
+        for load in loads:
+            times.append(times[-1] + max(load.values()) + LATENCY)
+        return times[:-1], busy
 
     def rounds(self, ins, outs, scratch):
         place = Place(self.plan.sizes)
@@ -382,13 +398,16 @@
         taken = [0]
         rounds = [[] for _ in range(self.end - self.begin)]
         last = []
-        for i, (start, (n, order, split, columns)) in enumerate(self.units):
+        for i, ((start, stride), (n, order, split, columns)) in enumerate(self.units):
             flow = Flow(place, send, recv, taken)
-            begin, end = max(self.begin - start, 0), self.end - start
+            begin, end = [max(-((start - to) // stride), 0) for to in (self.begin, self.end)]
             slot = self.names.index(n)
-            gather_steps(flow, ins[slot], outs[slot], order, split, columns, local.at[i], begin, end)
+            gather_steps(
+                flow, ins[slot], outs[slot], order, split, columns, self.plan.spans[n][0],
+                local.at[i], begin, end,
+            )
             for step, actions in enumerate(flow.steps):
-                there = rounds[start + begin + step - self.begin]
+                there = rounds[start + (begin + step) * stride - self.begin]
                 there.insert(0 if begin + step == 0 else len(there), actions)
             last += flow.last
         rounds = [[action for actions in there for action in actions] for there in rounds]
@@ -401,12 +420,12 @@
 
 
 class SmallUnit:
-    def __init__(self, plan, rows, start):
-        self.plan, self.grad, self.start = plan, rows, start
+    def __init__(self, plan, row, start):
+        self.plan, self.grad, self.start, self.stride = plan, row, start, 1
         self.order, self.count = "xzm", 4
-        self.rows, self.width = rows.shape
+        self.rows, self.width = 8, row.shape[1]
         self.share = self.width
-        self.spec = pl.BlockSpec(rows.shape, lambda *_: (0, 0))
+        self.spec = pl.BlockSpec(memory_space=pl.ANY)
         self.state = self.result = None
 
     def left(self, done):
@@ -416,14 +435,15 @@
         sizes = self.plan.sizes
         return [self.left("")] + [(sizes[axis],) + self.left("") for axis in "c" + self.order]
 
-    def steps(self, flow, rows, state, saved, result, buffers, local_sem, begin, end):
+    def steps(self, flow, row, state, saved, result, buffers, local_sem, begin, end):
         place, at = flow.place, flow.place.at
         own, landings = buffers[0], buffers[1:]
         actions = []
 
         def fill():
-            own[...] = rows[...]
-            own[pl.ds(0, 1), :] = self.plan.first_row[...]
+            own[...] = jnp.zeros_like(own)
+            for i, row in enumerate(self.plan.rows):
+                own[pl.ds(i, 1), :] = row[...]
 
         actions.append(fill)
         for axis, landing in zip("c" + self.order, landings):
@@ -460,17 +480,19 @@
         self.sizes, self.units, self.round = sizes, [], 0
 
     def add(self, arrays, units):
-        for i, order, split, columns, start in units:
+        for i, order, split, columns, start, stride in units:
             assert start >= self.round
-            self.units.append(ScatterUnit(self.sizes, arrays[i], order, split, columns, start))
+            self.units.append(
+                ScatterUnit(self.sizes, arrays[i], order, split, columns, start, stride)
+            )
         return self.units[len(self.units) - len(units) :]
 
-    def add_small(self, rows):
-        self.units.append(SmallUnit(self, rows, self.all() - 4))
+    def add_small(self, row):
+        self.units.append(SmallUnit(self, row, self.all() - 4))
         return self.units[-1]
 
     def all(self):
-        return max(unit.start + unit.count for unit in self.units)
+        return max(unit.start + (unit.count - 1) * unit.stride + 1 for unit in self.units)
 
     def until(self, end, collective_id):
         begin, self.round = self.round, max(end, self.round)
@@ -487,7 +509,9 @@
         buffers, pairs = [], 0
         self.arrays, self.out_shape, self.out_specs = [], [], []
         for unit in plan.units:
-            first, stop = max(begin - unit.start, 0), min(end - unit.start, unit.count)
+            first, stop = [
+                min(max(-((unit.start - to) // unit.stride), 0), unit.count) for to in (begin, end)
+            ]
             if first >= stop:
                 continue
             self.units.append((unit, first, stop))
@@ -511,16 +535,17 @@
             pltpu.SemaphoreType.DMA((len(self.units),)),
         ]
 
-    def times(self):
+    def times(self, busy):
         rounds = [[] for _ in range(self.end - self.begin)]
-        for unit, first, stop in self.units:
+        for n, (unit, first, stop) in enumerate(self.units):
             for i in range(first, stop):
                 done = unit.order[:i]
                 axis = ("c" + unit.order + "m")[i]
                 shape = unit.left(done) if i <= len(unit.order) else (unit.rows, unit.share)
                 size = functools.reduce(lambda a, b: a * b, shape, unit.grad.dtype.itemsize)
-                rounds[unit.start + i - self.begin].append((axis, size))
-        return round_times(self.sizes, rounds)
+                rounds[unit.start + i * unit.stride - self.begin].append((n, i, axis, size))
+        times, length = round_times(self.sizes, rounds)
+        return times, busy if length > 2.0 * busy else length
 
     def rounds(self, ins, outs, scratch):
         place = Place(self.sizes)
@@ -543,9 +568,9 @@
             else:
                 flow.steps[0][:0] = ahead
             for step, actions in enumerate(flow.steps):
-                rounds[unit.start + first + step - self.begin].append(actions)
-            after = unit.start + stop - self.begin
-            if after < len(rounds):
+                rounds[unit.start + (first + step) * unit.stride - self.begin].append(actions)
+            after = unit.start + stop * unit.stride - self.begin
+            if done and after < len(rounds):
                 rounds[after].append(end)
             else:
                 ends += end
@@ -584,7 +609,7 @@
         )(*args)
     counts = (len(args), len(exchange.arrays), len(out_shape), len(exchange.out_shape))
     total = functools.reduce(lambda a, b: a * b, grid, 1)
-    times = exchange.times()
+    times, pace = exchange.times(busy)
 
     def kernel(*refs):
         refs = list(refs)
@@ -594,11 +619,10 @@
         for i, size in enumerate(grid):
             step = step * size + pl.program_id(i)
         rounds, last = exchange.rounds(sent, received, refs)
-        slots, spent, after = {}, 0.0, []
-        for actions, time in zip(rounds, times):
-            slot = int(total * polls * spent / busy + 0.5) if busy else total * polls
-            spent += time
-            if slot and slot >= total * polls:
+        slots, after = {}, []
+        for i, (actions, time) in enumerate(zip(rounds, times)):
+            slot = int(total * polls * time / pace + 0.5) if busy and i else 0
+            if slot >= total * polls or i and not busy:
                 after += actions
             else:
                 slots.setdefault((slot % polls, slot // polls), []).extend(actions)
@@ -673,17 +697,21 @@
     return inverse * (weighted - unit * inner), grad * unit
 
 
+def row_of(gains, i):
+    return gains[pl.ds(i, 1), :]
+
+
 def whole(shape):
     return pl.BlockSpec(shape, lambda *_: (0,) * len(shape))
 
 
 def project_kernel(
-    poll, valid, x_ref, gain_ref, cot, wq, wk, wv, normed_t, masked, masked_t, q, k, v, normed
+    poll, valid, x_ref, gains, cot, wq, wk, wv, normed_t, masked, masked_t, q, k, v, normed
 ):
     @pl.when(pl.program_id(0) == 0)
     def _():
         x = x_ref[...].astype(F32)
-        rows = (x * inverse_rms(x) * gain_ref[...]).astype(BF16)
+        rows = (x * inverse_rms(x) * row_of(gains, 0)).astype(BF16)
         normed[...] = rows
         normed_t[...] = rows.T
         keep = position(cot.shape, 0) < valid[0]
@@ -697,7 +725,7 @@
         out[...] = matmul(rows, weight[...]).astype(BF16)
 
 
-def project(valid, x, gain, cot, weights, exchange):
+def project(valid, x, gains, cot, weights, exchange):
     rows, width = x.shape
     tile = pl.BlockSpec((width, TILE), lambda j: (0, j))
     out = pl.BlockSpec((rows, TILE), lambda j: (0, j))
@@ -705,9 +733,9 @@
     turned = whole((width, rows))
     return run_kernel(
         project_kernel,
-        (valid, x, gain, cot, *weights),
+        (valid, x, gains, cot, *weights),
         grid=(width // TILE,),
-        in_specs=[pl.BlockSpec(memory_space=pltpu.SMEM), full, whole((1, width)), full]
+        in_specs=[pl.BlockSpec(memory_space=pltpu.SMEM), full, whole(gains.shape), full]
         + [tile] * 3,
         out_specs=[turned, full, turned, out, out, out],
         out_shape=[
@@ -784,7 +812,7 @@
 
 
 def state_forward_kernel(
-    poll, valid, s0, gain, gate_bias, wq, wk, wv, wu, k, v,
+    poll, valid, s0, gains, wq, wk, wv, wu, k, v,
     normed_t, sq, sk, sv, read, log_out, update_out, states, last,
     state, normed, total,
 ):
@@ -797,7 +825,7 @@
     @pl.when(pair == 0)
     def _():
         now = state[...]
-        rows = (now * inverse_rms(now) * gain[...]).astype(BF16)
+        rows = (now * inverse_rms(now) * row_of(gains, 1)).astype(BF16)
         normed[...] = rows
         normed_t[...] = rows.T
         states[...] = now
@@ -819,30 +847,29 @@
     @pl.when(pair == pl.num_programs(1) - 1)
     def _():
         update = total[...]
-        gate = 1.0 / (1.0 + jnp.exp(-gate_bias[...]))
+        gate = 1.0 / (1.0 + jnp.exp(-row_of(gains, 3)))
         later = gate * state[...] + (1.0 - gate) * update
         update_out[...] = update
         state[...] = later
         last[...] = later.astype(BF16)
 
 
-def state_forward(valid, s0, gain, gate_bias, weights, update_weight, k, v, exchange):
+def state_forward(valid, s0, gains, weights, update_weight, k, v, exchange):
     rows, width = s0.shape
     blocks, pairs = k.shape[0] // BLOCK, width // PAIR
     columns = pl.BlockSpec((width, PAIR), lambda b, p: (0, p))
     tile = pl.BlockSpec((rows, PAIR), lambda b, p: (b, p))
     band = pl.BlockSpec((rows, width), lambda b, p: (b, 0))
-    small = whole((1, width))
 
     def stack(kind):
         return jax.ShapeDtypeStruct((blocks * rows, width), kind)
 
     return run_kernel(
         state_forward_kernel,
-        (valid, s0, gain, gate_bias, *weights, update_weight, k, v),
+        (valid, s0, gains, *weights, update_weight, k, v),
         grid=(blocks, pairs),
         in_specs=[
-            pl.BlockSpec(memory_space=pltpu.SMEM), whole((rows, width)), small, small,
+            pl.BlockSpec(memory_space=pltpu.SMEM), whole((rows, width)), whole(gains.shape),
             columns, columns, columns, pl.BlockSpec((PAIR, width), lambda b, p: (p, 0)),
             pl.BlockSpec((BLOCK, PAIR), lambda b, p: (b, p)),
             pl.BlockSpec((BLOCK, PAIR), lambda b, p: (b, p)),
@@ -870,7 +897,7 @@
 
 
 def token_forward_kernel(
-    poll, valid, x, gain, q, k, v, sk, sv, wo, mixed, log_out, resid, ynorm, ynorm_t
+    poll, valid, x, gains, q, k, v, sk, sv, wo, mixed, log_out, resid, ynorm, ynorm_t
 ):
     pair = pl.program_id(0)
 
@@ -898,22 +925,22 @@
     @pl.when(pair == pl.num_programs(0) - 1)
     def _():
         rows = resid[...]
-        rounded = (rows * inverse_rms(rows) * gain[...]).astype(BF16)
+        rounded = (rows * inverse_rms(rows) * row_of(gains, 2)).astype(BF16)
         ynorm[...] = rounded
         ynorm_t[...] = rounded.T
 
 
-def token_forward(valid, x, gain, q, k, v, sk, sv, wo, exchange):
+def token_forward(valid, x, gains, q, k, v, sk, sv, wo, exchange):
     rows, width = x.shape
     pairs = width // PAIR
     tile = pl.BlockSpec((rows, PAIR), lambda p: (0, p))
     states = pl.BlockSpec((sk.shape[0], PAIR), lambda p: (0, p))
     return run_kernel(
         token_forward_kernel,
-        (valid, x, gain, q, k, v, sk, sv, wo),
+        (valid, x, gains, q, k, v, sk, sv, wo),
         grid=(pairs,),
         in_specs=[
-            pl.BlockSpec(memory_space=pltpu.SMEM), whole((rows, width)), whole((1, width)),
+            pl.BlockSpec(memory_space=pltpu.SMEM), whole((rows, width)), whole(gains.shape),
             tile, tile, tile, states, states, pl.BlockSpec((PAIR, width), lambda p: (p, 0)),
         ],
         out_specs=[
@@ -1023,7 +1050,7 @@
 
 
 def token_backward_kernel(
-    poll, valid, resid, gain, masked, grad_ynorm, normed_t, snormed_t,
+    poll, valid, resid, gains, masked, grad_ynorm, normed_t, snormed_t,
     q, k, v, sk, sv, wo, mixed, log_total,
     grad_resid, gain_grad, dq, dk, dv, dsk, dsv, wo_grad, wq_grad, skw_grad, svw_grad,
     rounded, work, other, sems, grad_mixed, near_k, near_v, state_k, state_v,
@@ -1045,7 +1072,7 @@
     def _():
         for copy in loads:
             copy.wait()
-        grad, gain_rows = rms_backward(work[...], gain[...], other[...])
+        grad, gain_rows = rms_backward(work[...], row_of(gains, 2), other[...])
         grad = rounded[...].astype(F32) + grad
         work[...] = grad
         rounded[...] = grad.astype(BF16)
@@ -1102,7 +1129,7 @@
 
 
 def token_backward(
-    valid, resid, gain, masked, grad_ynorm, normed_t, snormed_t,
+    valid, resid, gains, masked, grad_ynorm, normed_t, snormed_t,
     q, k, v, sk, sv, wo, mixed, log_total, exchange,
 ):
     rows, width = resid.shape
@@ -1118,12 +1145,12 @@
     return run_kernel(
         token_backward_kernel,
         (
-            valid, resid, gain, masked, grad_ynorm, normed_t, snormed_t,
+            valid, resid, gains, masked, grad_ynorm, normed_t, snormed_t,
             q, k, v, sk, sv, wo, mixed, log_total,
         ),
         grid=(pairs,),
         in_specs=[
-            pl.BlockSpec(memory_space=pltpu.SMEM), anywhere, whole((1, width)), anywhere, anywhere,
+            pl.BlockSpec(memory_space=pltpu.SMEM), anywhere, whole(gains.shape), anywhere, anywhere,
             turned, turned_state, tile, tile, tile, states, states, band, tile,
             pl.BlockSpec((1, 2, rows), lambda p: (p, 0, 0)),
         ],
@@ -1154,14 +1181,14 @@
 
 
 def state_backward_kernel(
-    poll, valid, cot, gain, gate_bias, wq, wk, wv, wu, states, updates,
+    poll, valid, cot, gains, wq, wk, wv, wu, states, updates,
     sq, k, v, read, log_total, near_k, near_v, dsk, dsv, read_last, normed_t, snormed_t,
     dk, dv, grad_state, gain_grad, bias_grad, wk_grad, wv_grad, sqw_grad, wu_grad,
     later, dz, total, grad_read, sum_k, sum_v, dsq, kept_dz, kept,
 ):
     step, pair = pl.program_id(0), pl.program_id(1)
     block = pl.num_programs(0) - 1 - step
-    gate = 1.0 / (1.0 + jnp.exp(-gate_bias[...]))
+    gate = 1.0 / (1.0 + jnp.exp(-row_of(gains, 3)))
 
     @pl.when((step == 0) & (pair == 0))
     def _():
@@ -1233,7 +1260,7 @@
 
     @pl.when(pair == pl.num_programs(1) - 1)
     def _():
-        grad, gain_rows = rms_backward(states[...], gain[...], total[...])
+        grad, gain_rows = rms_backward(states[...], row_of(gains, 1), total[...])
         grad = later[...] * gate + grad
         later[...] = grad
         grad_state[...] = grad
@@ -1241,7 +1268,7 @@
 
 
 def state_backward(
-    valid, cot, gain, gate_bias, weights, update_weight, states, updates,
+    valid, cot, gains, weights, update_weight, states, updates,
     sq, k, v, read, log_total, near_k, near_v, dsk, dsv, normed_t, snormed_t, exchange,
 ):
     rows, width = cot.shape
@@ -1254,12 +1281,12 @@
     return run_kernel(
         state_backward_kernel,
         (
-            valid, cot, gain, gate_bias, *weights, update_weight, states, updates,
+            valid, cot, gains, *weights, update_weight, states, updates,
             sq, k, v, read, log_total, near_k, near_v, dsk, dsv, read, normed_t, snormed_t,
         ),
         grid=(blocks, pairs),
         in_specs=[
-            pl.BlockSpec(memory_space=pltpu.SMEM), whole((rows, width)), small, small,
+            pl.BlockSpec(memory_space=pltpu.SMEM), whole((rows, width)), whole(gains.shape),
             columns, columns, columns, pl.BlockSpec((PAIR, width), lambda s, p: (p, 0)),
             band, band, tile, token, token, tile,
             pl.BlockSpec((1, 1, 2, rows), lambda s, p: (blocks - 1 - s, p, 0, 0)),
@@ -1294,9 +1321,10 @@
 
 
 def token_grad_kernel(
-    plan, poll, x, gain, grad_resid, dq, dk, dv, wq, wk, wv, grad_x, gain_grad
+    plan, poll, x, gains, grad_resid, dq, dk, dv, wq, wk, wv, *refs
 ):
-    plan.first_row = gain_grad
+    *others, grad_x, gain_grad = refs
+    plan.rows = [gain_grad] + others
     poll()
 
     @pl.when(pl.program_id(0) == 0)
@@ -1306,20 +1334,21 @@
     grad_normed = matmul_nt(dq[...], wq[...]) + matmul_nt(dk[...], wk[...])
     poll()
     grad_normed = grad_normed + matmul_nt(dv[...], wv[...])
-    grad, gain_rows = rms_backward(x[...].astype(F32), gain[...], grad_normed)
+    grad, gain_rows = rms_backward(x[...].astype(F32), row_of(gains, 0), grad_normed)
     grad_x[...] = grad_resid[...] + grad
     gain_grad[...] += jnp.sum(gain_rows, axis=0, keepdims=True)
 
 
-def token_grad(x, gain, grad_resid, grads, weights, plan, exchange):
+def token_grad(x, gains, grad_resid, grads, weights, other_rows, plan, exchange):
     rows, width = x.shape
     band = pl.BlockSpec((TILE, width), lambda i: (i, 0))
     weight = pl.BlockSpec((width, width), lambda i: (0, 0), pipeline_mode=pl.Buffered(1))
     return run_kernel(
         functools.partial(token_grad_kernel, plan),
-        (x, gain, grad_resid, *grads, *weights),
+        (x, gains, grad_resid, *grads, *weights, *other_rows),
         grid=(rows // TILE,),
-        in_specs=[band, whole((1, width)), band, band, band, band, weight, weight, weight],
+        in_specs=[band, whole(gains.shape), band, band, band, band, weight, weight, weight]
+        + [whole((1, width))] * len(other_rows),
         out_specs=[band, whole((1, width))],
         out_shape=[
             jax.ShapeDtypeStruct((rows, width), F32), jax.ShapeDtypeStruct((1, width), F32)
@@ -1337,61 +1366,87 @@
 
 def plan_gather(sizes, small, square, forward):
     width, half = square[0].shape[1], forward[0].shape[1]
-    pieces = cut(width, SQUARE_PIECES)
-    can_share = pieces[0][1] // sizes["m"] % 128 == 0
-    units = [(0, "zx", False, (0, small.shape[1]), 0)]
-    for group, start in zip(((0, 1, 2), (3, 4, 5), (6,), (7,)), GATHER_SQUARE):
-        if len(group) == 1:
-            spans = [pieces]
-        else:
-            spans = [[columns] for columns in pieces]
-        for n, span in enumerate(spans):
-            for j, (i, columns) in enumerate((i, columns) for columns in span for i in group):
-                shared = can_share and j > 0
-                units.append((1 + i, "zxm" if shared else "zx", shared, columns, start + n))
-    for i, start in enumerate(GATHER_FORWARD):
-        for n, columns in enumerate(cut(half, FORWARD_PIECES)):
-            units.append((9 + i, ("zxm", "zmx")[n % 2], False, columns, start + n // 2))
-    return Gather(sizes, [small] + square + forward, units)
-
-
-def forward_units(arrays, start):
+    units = [(0, "zx", False, (0, small.shape[1]), 0, 1)]
+    for group, (starts, routes, stride) in zip(((1, 2, 3), (4, 5, 6), (7,), (8,)), GATHER_SQUARE):
+        pieces = cut(width, len(starts))
+        can_share = pieces[0][1] // sizes["m"] % 128 == 0
+        for n, (columns, start) in enumerate(zip(pieces, starts)):
+            for j, i in enumerate(group):
+                order = routes[(n * len(group) + j) % len(routes)]
+                shared = can_share and "m" in order
+                units.append((i, order if shared else "zx", shared, columns, start, stride))
+    for i, (starts, stride) in enumerate(GATHER_FORWARD):
+        for n, columns in enumerate(cut(half, min(len(starts), half // 128))):
+            order = ("zxm", "zmx")[n % 2]
+            units.append((9 + i, order, False, columns, starts[n], stride))
+    arrays = [small] + square + forward
+    return Gather(sizes, arrays, [(0, array.shape[1]) for array in arrays], units)
+
+
+def forward_units(arrays, start, table):
     units = []
-    for i, array in enumerate(arrays):
-        for n, columns in enumerate(cut(array.shape[-1], FORWARD_PIECES)):
-            units.append((i, ("mxz", "xmz")[n % 2], False, columns))
-    return [unit + (start + n // 2,) for n, unit in enumerate(units)]
-
-
-def square_units(sizes, arrays, start, group, pieces):
+    for i, (array, pieces) in enumerate(zip(arrays, table)):
+        columns = cut(array.shape[-1], min(len(pieces), array.shape[-1] // 128))
+        units += [
+            (i, order, False, there, start + offset, stride)
+            for there, (order, offset, stride) in zip(columns, pieces)
+        ]
+    return units
+
+
+def square_units(sizes, arrays, start, table):
     units = []
-    for columns in cut(arrays[0].shape[-1], pieces):
-        for i in range(len(arrays)):
-            shared = len(units) % 3 > 0 and columns[1] // sizes["m"] % 128 == 0
-            units.append((i, "mxz" if shared else "xz", shared, columns))
-    return [unit + (start + n // group,) for n, unit in enumerate(units)]
-
-
-def finish_kernel(counts, *refs):
+    for columns, pieces in zip(cut(arrays[0].shape[-1], len(table)), table):
+        can_share = columns[1] // sizes["m"] % 128 == 0
+        for i, (order, offset, stride) in enumerate(pieces):
+            shared = can_share and "m" in order
+            units.append(
+                (i, order if shared else "xz", shared, columns, start + offset, stride)
+            )
+    return units
+
+
+def finish_kernel(kept, counts, *refs):
     refs = list(refs)
+    sources = [refs.pop(0) for _ in range(kept)]
     parts = [[refs.pop(0) for _ in range(n)] for n in counts]
+    targets = [refs.pop(0) for _ in range(kept)]
+    stages, sems = refs[-1 - kept : -1], refs[-1]
+    loads, stores = [], []
+    for i, (source, stage, target) in enumerate(zip(sources, stages, targets)):
+        loads.append(pltpu.make_async_copy(source, stage, sems.at[i]))
+        stores.append(pltpu.make_async_copy(stage, target, sems.at[kept + i]))
+    for load in loads:
+        load.start()
+    for load, store in zip(loads, stores):
+        load.wait()
+        store.start()
     for group, out in zip(parts, refs):
         first = 0
         for part in group:
             out[:, pl.ds(first, part.shape[1])] = part[...]
             first += part.shape[1]
-
-
-def finish(groups):
+    for store in stores:
+        store.wait()
+
+
+def finish(arrays, groups):
+    anywhere, inside = pl.BlockSpec(memory_space=pl.ANY), pl.BlockSpec(memory_space=pltpu.VMEM)
     shapes = [
         jax.ShapeDtypeStruct((g[0].shape[0], sum(p.shape[1] for p in g)), F32) for g in groups
     ]
-    return pl.pallas_call(
-        functools.partial(finish_kernel, [len(g) for g in groups]),
-        out_shape=shapes,
+    parts = [part for g in groups for part in g]
+    outs = pl.pallas_call(
+        functools.partial(finish_kernel, len(arrays), [len(g) for g in groups]),
+        in_specs=[anywhere] * len(arrays) + [inside] * len(parts),
+        out_specs=[anywhere] * len(arrays) + [inside] * len(groups),
+        out_shape=[jax.ShapeDtypeStruct(a.shape, a.dtype) for a in arrays] + shapes,
+        scratch_shapes=[pltpu.VMEM(a.shape, a.dtype) for a in arrays]
+        + [pltpu.SemaphoreType.DMA((2 * len(arrays),))],
         compiler_params=pltpu.CompilerParams(vmem_limit_bytes=VMEM_LIMIT),
         name="finish",
-    )(*[part for g in groups for part in g])
+    )(*arrays, *parts)
+    return outs[: len(arrays)], outs[len(arrays) :]
 
 
 def shards(
@@ -1451,21 +1506,20 @@
 
     exchange_alone(plan.until(plan.ready((0, 1, 2, 3)), 1), "gather_first")
     gains = plan.targets[0].reshape(seg_size, -1)[:, : 4 * rows].reshape(seg_size, 4, rows)
-    gains = gains.transpose(1, 0, 2).reshape(4, 1, width).astype(F32)
-    token_gain, state_gain, mlp_gain, gate_bias = [gains[i] for i in range(4)]
+    gains = gains.transpose(1, 0, 2).reshape(4, width).astype(F32)
     token_weights = full(1, 2, 3)
     normed_t, masked, masked_t, q, k, v = project(
-        valid, x, token_gain, cot, token_weights, plan.until(plan.ready((4, 5, 6, 7)), 2)
+        valid, x, gains, cot, token_weights, plan.until(plan.ready((4, 5, 6, 7)), 2)
     )
     state_weights, (wu,) = full(4, 5, 6), full(7)
     ready = plan.ready((9, 10))
     middle = max(plan.ready((8,)), GATHER_MIDDLE)
     snormed_t, sq, sk, sv, read, read_log, updates, states, last = state_forward(
-        valid, s0, state_gain, gate_bias, state_weights, wu, k, v, plan.until(middle, 3)
+        valid, s0, gains, state_weights, wu, k, v, plan.until(middle, 3)
     )
     (wo,) = full(8)
     mixed, token_log, resid, *ynorms = token_forward(
-        valid, x, mlp_gain, q, k, v, sk, sv, wo, plan.until(ready, 4)
+        valid, x, gains, q, k, v, sk, sv, wo, plan.until(ready, 4)
     )
     total, grad_total, *first_grads = feed_forward(
         True, False, (*ynorms, masked, masked_t), resid, resid, *forward_full(9, 10),
@@ -1485,35 +1539,31 @@
     def next_rounds(collective_id):
         return sums.until(sums.round + next(rounds), collective_id)
 
-    units_first = sums.add(parted(first_grads), forward_units(first_grads, 0))
+    units_first = sums.add(parted(first_grads), forward_units(first_grads, 0, SCATTER_FIRST))
     out, grad_total, *last_grads = feed_forward(
         False, True, (*ynorms, masked, masked_t), total, grad_total, *forward_full(11, 12),
         next_rounds(6),
     )
-    units_last = sums.add(parted(last_grads), forward_units(last_grads, sums.round))
+    units_last = sums.add(parted(last_grads), forward_units(last_grads, sums.round, SCATTER_LAST))
     grad_resid, mlp_gain_grad, dq, near_k, near_v, dsk, dsv, *early_grads = token_backward(
-        valid, resid, mlp_gain, masked, grad_total, normed_t, snormed_t,
+        valid, resid, gains, masked, grad_total, normed_t, snormed_t,
         q, k, v, sk, sv, wo, mixed, token_log, next_rounds(7),
     )
     units_early = sums.add(
-        parted(early_grads), square_units(sizes, early_grads, sums.round, 4, SCATTER_PIECES)
+        parted(early_grads), square_units(sizes, early_grads, sums.round, SCATTER_EARLY)
     )
     dk, dv, grad_state, state_gain_grad, bias_grad, *late_grads = state_backward(
-        valid, final_state_cotangent[0], state_gain, gate_bias, state_weights, wu,
+        valid, final_state_cotangent[0], gains, state_weights, wu,
         states, updates, sq, k, v, read, read_log, near_k, near_v, dsk, dsv, normed_t, snormed_t,
         next_rounds(8),
     )
     units_late = sums.add(
-        parted(late_grads), square_units(sizes, late_grads, sums.round, 4, SCATTER_PIECES)
-    )
-    small_unit = sums.add_small(
-        jnp.concatenate(
-            [jnp.zeros_like(mlp_gain_grad), state_gain_grad, mlp_gain_grad, bias_grad]
-            + [jnp.zeros((4, width), F32)]
-        )
-    )
+        parted(late_grads), square_units(sizes, late_grads, sums.round, SCATTER_LATE)
+    )
+    small_unit = sums.add_small(mlp_gain_grad)
     grad_tokens, _ = token_grad(
-        x, token_gain, grad_resid, [dq, dk, dv], token_weights, sums, sums.until(sums.all(), 9)
+        x, gains, grad_resid, [dq, dk, dv], token_weights,
+        [state_gain_grad, mlp_gain_grad, bias_grad], sums, sums.until(sums.all(), 9),
     )
     small_sum = small_unit.result[:4].reshape(4, seg_size, rows)
     small_sum = lax.dynamic_index_in_dim(small_sum, lax.axis_index("seg"), 1, keepdims=False)
@@ -1525,10 +1575,11 @@
         return [
             unit.result
             for units in (units_first, units_last)
-            for unit in units[i * FORWARD_PIECES : (i + 1) * FORWARD_PIECES]
+            for unit in units[i * len(units) // 2 : (i + 1) * len(units) // 2]
         ]
 
-    weight_sums = finish(
+    own_results, weight_sums = finish(
+        [last, out, grad_state, grad_tokens],
         [
             group(units_early, 1, 4),
             group(units_late, 0, 4),
@@ -1540,13 +1591,10 @@
             group(units_late, 3, 4),
             forward_group(0),
             forward_group(1),
-        ]
+        ],
     )
     return (
-        out[None],
-        last[None],
-        grad_tokens[None],
-        grad_state[None],
+        *[own_results[i][None] for i in (1, 0, 3, 2)],
         *weight_sums,
         *[small_sum[i] for i in range(4)],
     )

time: 503 us -> 498 us (0.990); the launches traced: 495 us -> 496 us
  local copies, waits for them, and re-layouts: 15.9 us -> 4.74 us
  Pallas kernels: 477 us -> 488 us
    unnamed x17 -> x3, local copies, waits for them, and re-layouts: 8.62 us -> 0.86 us
    pallas_call x1, Pallas kernels: 3.78 us -> 11.4 us  [finish(): pl.pallas_call(functools.partial(finish_kernel, len(arrays), [len(g) for...]
where the time goes in v5:
time: 498 us; the launch traced here: 496 us
  Pallas kernels  488 us (98%)
    pallas_call x9, Pallas kernels, run_kernel(): pl.pallas_call(kernel, grid=grid, in_specs=list(in_specs) + exchange.spec...  477 us
    pallas_call x1, Pallas kernels, finish(): pl.pallas_call(functools.partial(finish_kernel, len(arrays), [len(g) for...  11.4 us

profile of v5, /device:TPU:0, one launch (start us, length us, event | category | flops | bytes accessed | tf_op | source)
XLA Modules:
  0.0 495.6 jit_solution(13856930185317505678)
XLA Ops:
  0.7 0.8 maximum_bitcast_fusion
  1.4 0.6 pad.4.refs_0_
  2.0 71.3 %gather_first.1 = (bf16[4,2,2,16,128]{4,3,2,1,0:T(8,128)(2,1)}, bf16[4,2,2,64,1024]{4,3,2,1,0:T(8,128)(2,1)}, bf16[4,2,2,64,1024]{4,3,2,1,0:T(8,128)(2,1)}, bf16...) custom-call(bf16[16,128]{1,0:T(8,128)(2,1)} %pad.4.refs_0_, ...), custom_call_target="tpu_custom_call" | custom-call | tf_op jit(solution)/shard_map/gather_first/pallas_call | solution.py:642
  73.3 0.9 copy.51
  74.2 0.1 reshape.159
  74.3 0.7 reshape.158.refs_2_.refs_1_
  75.0 1.9 fusion.4
  77.5 45.8 %project_tokens.1 = (bf16[1024,1024]{1,0:T(8,128)(2,1)}, bf16[1024,1024]{1,0:T(8,128)(2,1)}, bf16[1024,1024]{1,0:T(8,128)(2,1)}, bf16[1024,1024]{1,0:T(8,128)(2,...) custom-call(s32[1]{0:T(128)S(6)} %copy.63.refs_0_, ...), custom_call_target="tpu_custom_call", output_to_operand_aliasing={{6}: (14, {}), {7}: (15, {}), {8}: (16, {}), {9}: (17, {})} | custom-call | tf_op jit(solution)/shard_map/project_tokens/pallas_call | solution.py:642
  123.3 32.3 %state_forward.1 = (bf16[1024,1024]{1,0:T(8,128)(2,1)}, bf16[1024,1024]{1,0:T(8,128)(2,1)}, bf16[1024,1024]{1,0:T(8,128)(2,1)}, bf16[1024,1024]{1,0:T(8,128)(2,1...) custom-call(s32[1]{0:T(128)S(6)} %copy.63.refs_0_, ...), custom_call_target="tpu_custom_call", output_to_operand_aliasing={{9}: (12, {}), {10}: (13, {}), {11}: (14, {})} | custom-call | tf_op jit(solution)/shard_map/state_forward/pallas_call | solution.py:642
  155.5 46.2 %token_forward.1 = (bf16[1024,1024]{1,0:T(8,128)(2,1)}, f32[4,2,1024]{2,1,0:T(2,128)}, f32[1024,1024]{1,0:T(8,128)}, bf16[1024,1024]{1,0:T(8,128)(2,1)}, bf16[10...) custom-call(s32[1]{0:T(128)S(6)} %copy.63.refs_0_, ...), custom_call_target="tpu_custom_call", output_to_operand_aliasing={{5}: (13, {}), {6}: (14, {})} | custom-call | tf_op jit(solution)/shard_map/token_forward/pallas_call | solution.py:642
  201.7 43.1 %feed_forward_first.1 = (f32[1024,1024]{1,0:T(8,128)}, f32[1024,1024]{1,0:T(8,128)}, bf16[2,1024,1024]{2,1,0:T(8,128)(2,1)}, bf16[2,1024,1024]{2,1,0:T(8,128)(2,...) custom-call(bf16[1024,1024]{1,0:T(8,128)(2,1)} %get-tuple-element.17, ...), custom_call_target="tpu_custom_call", output_to_operand_aliasing={{4}: (10, {}), {5}: (11, {})} | custom-call | tf_op jit(solution)/shard_map/feed_forward_first/pallas_call | solution.py:642
  244.8 46.4 %feed_forward_final.1 = (bf16[1024,1024]{1,0:T(8,128)(2,1)}, f32[1024,1024]{1,0:T(8,128)}, bf16[2,1024,1024]{2,1,0:T(8,128)(2,1)}, bf16[2,1024,1024]{2,1,0:T(8,1...) custom-call(bf16[1024,1024]{1,0:T(8,128)(2,1)} %get-tuple-element.17, ...), custom_call_target="tpu_custom_call" | custom-call | tf_op jit(solution)/shard_map/feed_forward_final/pallas_call | solution.py:642
  291.2 59.6 %token_backward.1 = (f32[1024,1024]{1,0:T(8,128)}, f32[1,1024]{1,0:T(1,128)}, bf16[1024,1024]{1,0:T(8,128)(2,1)}, f32[1024,1024]{1,0:T(8,128)}, f32[1024,1024]{1...) custom-call(s32[1]{0:T(128)S(6)} %copy.63.refs_0_, ...), custom_call_target="tpu_custom_call" | custom-call | tf_op jit(solution)/shard_map/token_backward/pallas_call | solution.py:642
  350.8 58.5 %state_backward.1 = (bf16[1024,1024]{1,0:T(8,128)(2,1)}, bf16[1024,1024]{1,0:T(8,128)(2,1)}, f32[512,1024]{1,0:T(8,128)}, f32[1,1024]{1,0:T(1,128)}, f32[1,1024]...) custom-call(s32[1]{0:T(128)S(6)} %copy.63.refs_0_, ...), custom_call_target="tpu_custom_call" | custom-call | tf_op jit(solution)/shard_map/state_backward/pallas_call | solution.py:642
  409.4 73.9 %token_grad.1 = (f32[1024,1024]{1,0:T(8,128)}, f32[1,1024]{1,0:T(1,128)}, f32[64,512]{1,0:T(8,128)}, f32[64,512]{1,0:T(8,128)}, f32[64,512]{1,0:T(8,128)}, /*ind...) custom-call(bf16[1024,1024]{1,0:T(8,128)(2,1)} %bitcast.62, ...), custom_call_target="tpu_custom_call" | custom-call | tf_op jit(solution)/shard_map/token_grad/pallas_call | solution.py:642
  483.3 0.0 copy-start
  483.3 11.4 %finish.1 = (bf16[512,1024]{1,0:T(8,128)(2,1)}, bf16[1024,1024]{1,0:T(8,128)(2,1)}, f32[512,1024]{1,0:T(8,128)}, f32[1024,1024]{1,0:T(8,128)}, f32[64,1024]{1,0:...) custom-call(bf16[512,1024]{1,0:T(8,128)(2,1)} %get-tuple-element.163, ...), custom_call_target="tpu_custom_call" | custom-call | tf_op jit(solution)/shard_map/finish/pallas_call | solution.py:1439
  494.7 0.0 copy-done
  494.8 0.1 reshape.157
  494.8 0.5 fusion
  (3 shorter events, 0.0 us)
Async XLA Ops:
  483.3 11.4 %copy-start = (f32[8,1024]{1,0:T(8,128)S(1)}, f32[8,1024]{1,0:T(8,128)}, u32[]{:S(2)}) copy-start(f32[8,1024]{1,0:T(8,128)} %get-tuple-element.273) | copy-start | bytes 98308

commit v6 on v5

--- a/solution.py
+++ b/solution.py
@@ -24,7 +24,7 @@
     (("mxz", 1, 1), ("mxz", 1, 1), ("xz", 1, 1), ("mxz", 1, 1)),
 )
 SCATTER_LATE = SCATTER_EARLY
-SCATTER_ROUNDS = (3, 3, 3)
+SCATTER_ROUNDS = (3, 3, 2)
 LINK_RATE = 85e3
 CORE_RATE = 560e3
 START_COST = 2.5
@@ -908,8 +908,8 @@
     count = valid[0]
     for head in range(2):
         lanes = pl.ds(head * HEAD, HEAD)
+        poll()
         for block in range(q.shape[0] // BLOCK):
-            poll()
             for half in range(BLOCK // TILE):
                 rows = pl.ds(block * BLOCK + half * TILE, TILE)
                 pieces = []
@@ -957,7 +957,7 @@
         name="token_forward",
         exchange=exchange,
         busy=28.4,
-        polls=2 * rows // BLOCK,
+        polls=2,
     )
 
 
@@ -1098,8 +1098,8 @@
 
             return add
 
+        poll()
         for block in range(q.shape[0] // BLOCK):
-            poll()
             for half in range(BLOCK // TILE):
                 rows = pl.ds(block * BLOCK + half * TILE, TILE)
                 pieces = []
@@ -1176,7 +1176,7 @@
         name="token_backward",
         exchange=exchange,
         busy=55.0,
-        polls=1 + 2 * rows // BLOCK,
+        polls=3,
     )
 
 

time: 498 us -> 496 us (level)
  no operation moved by 1% of the time
where the time goes in v6:
time: 496 us; the launch traced here: 494 us
  Pallas kernels  487 us (98%)
    pallas_call x9, Pallas kernels, run_kernel(): pl.pallas_call(kernel, grid=grid, in_specs=list(in_specs) + exchange.spec...  476 us
    pallas_call x1, Pallas kernels, finish(): pl.pallas_call(functools.partial(finish_kernel, len(arrays), [len(g) for...  11.4 us

profile of v6, /device:TPU:0, one launch (start us, length us, event | category | flops | bytes accessed | tf_op | source)
XLA Modules:
  0.0 494.4 jit_solution(13151439213923138524)
XLA Ops:
  0.7 0.8 maximum_bitcast_fusion
  1.4 0.6 pad.4.refs_0_
  2.0 71.3 %gather_first.1 = (bf16[4,2,2,16,128]{4,3,2,1,0:T(8,128)(2,1)}, bf16[4,2,2,64,1024]{4,3,2,1,0:T(8,128)(2,1)}, bf16[4,2,2,64,1024]{4,3,2,1,0:T(8,128)(2,1)}, bf16...) custom-call(bf16[16,128]{1,0:T(8,128)(2,1)} %pad.4.refs_0_, ...), custom_call_target="tpu_custom_call" | custom-call | tf_op jit(solution)/shard_map/gather_first/pallas_call | solution.py:642
  73.3 0.9 copy.51
  74.2 0.1 reshape.159
  74.3 0.7 reshape.158.refs_2_.refs_1_
  75.0 1.9 fusion.4
  77.5 45.8 %project_tokens.1 = (bf16[1024,1024]{1,0:T(8,128)(2,1)}, bf16[1024,1024]{1,0:T(8,128)(2,1)}, bf16[1024,1024]{1,0:T(8,128)(2,1)}, bf16[1024,1024]{1,0:T(8,128)(2,...) custom-call(s32[1]{0:T(128)S(6)} %copy.63.refs_0_, ...), custom_call_target="tpu_custom_call", output_to_operand_aliasing={{6}: (14, {}), {7}: (15, {}), {8}: (16, {}), {9}: (17, {})} | custom-call | tf_op jit(solution)/shard_map/project_tokens/pallas_call | solution.py:642
  123.3 32.3 %state_forward.1 = (bf16[1024,1024]{1,0:T(8,128)(2,1)}, bf16[1024,1024]{1,0:T(8,128)(2,1)}, bf16[1024,1024]{1,0:T(8,128)(2,1)}, bf16[1024,1024]{1,0:T(8,128)(2,1...) custom-call(s32[1]{0:T(128)S(6)} %copy.63.refs_0_, ...), custom_call_target="tpu_custom_call", output_to_operand_aliasing={{9}: (12, {}), {10}: (13, {}), {11}: (14, {})} | custom-call | tf_op jit(solution)/shard_map/state_forward/pallas_call | solution.py:642
  155.5 46.1 %token_forward.1 = (bf16[1024,1024]{1,0:T(8,128)(2,1)}, f32[4,2,1024]{2,1,0:T(2,128)}, f32[1024,1024]{1,0:T(8,128)}, bf16[1024,1024]{1,0:T(8,128)(2,1)}, bf16[10...) custom-call(s32[1]{0:T(128)S(6)} %copy.63.refs_0_, ...), custom_call_target="tpu_custom_call", output_to_operand_aliasing={{5}: (13, {}), {6}: (14, {})} | custom-call | tf_op jit(solution)/shard_map/token_forward/pallas_call | solution.py:642
  201.7 43.1 %feed_forward_first.1 = (f32[1024,1024]{1,0:T(8,128)}, f32[1024,1024]{1,0:T(8,128)}, bf16[2,1024,1024]{2,1,0:T(8,128)(2,1)}, bf16[2,1024,1024]{2,1,0:T(8,128)(2,...) custom-call(bf16[1024,1024]{1,0:T(8,128)(2,1)} %get-tuple-element.17, ...), custom_call_target="tpu_custom_call", output_to_operand_aliasing={{4}: (10, {}), {5}: (11, {})} | custom-call | tf_op jit(solution)/shard_map/feed_forward_first/pallas_call | solution.py:642
  244.7 46.4 %feed_forward_final.1 = (bf16[1024,1024]{1,0:T(8,128)(2,1)}, f32[1024,1024]{1,0:T(8,128)}, bf16[2,1024,1024]{2,1,0:T(8,128)(2,1)}, bf16[2,1024,1024]{2,1,0:T(8,1...) custom-call(bf16[1024,1024]{1,0:T(8,128)(2,1)} %get-tuple-element.17, ...), custom_call_target="tpu_custom_call" | custom-call | tf_op jit(solution)/shard_map/feed_forward_final/pallas_call | solution.py:642
  291.2 58.4 %token_backward.1 = (f32[1024,1024]{1,0:T(8,128)}, f32[1,1024]{1,0:T(1,128)}, bf16[1024,1024]{1,0:T(8,128)(2,1)}, f32[1024,1024]{1,0:T(8,128)}, f32[1024,1024]{1...) custom-call(s32[1]{0:T(128)S(6)} %copy.63.refs_0_, ...), custom_call_target="tpu_custom_call" | custom-call | tf_op jit(solution)/shard_map/token_backward/pallas_call | solution.py:642
  349.6 54.2 %state_backward.1 = (bf16[1024,1024]{1,0:T(8,128)(2,1)}, bf16[1024,1024]{1,0:T(8,128)(2,1)}, f32[512,1024]{1,0:T(8,128)}, f32[1,1024]{1,0:T(1,128)}, f32[1,1024]...) custom-call(s32[1]{0:T(128)S(6)} %copy.63.refs_0_, ...), custom_call_target="tpu_custom_call" | custom-call | tf_op jit(solution)/shard_map/state_backward/pallas_call | solution.py:642
  403.8 78.3 %token_grad.1 = (f32[1024,1024]{1,0:T(8,128)}, f32[1,1024]{1,0:T(1,128)}, f32[64,512]{1,0:T(8,128)}, f32[64,512]{1,0:T(8,128)}, f32[64,512]{1,0:T(8,128)}, /*ind...) custom-call(bf16[1024,1024]{1,0:T(8,128)(2,1)} %bitcast.52, ...), custom_call_target="tpu_custom_call" | custom-call | tf_op jit(solution)/shard_map/token_grad/pallas_call | solution.py:642
  482.1 0.0 copy-start
  482.1 11.4 %finish.1 = (bf16[512,1024]{1,0:T(8,128)(2,1)}, bf16[1024,1024]{1,0:T(8,128)(2,1)}, f32[512,1024]{1,0:T(8,128)}, f32[1024,1024]{1,0:T(8,128)}, f32[64,1024]{1,0:...) custom-call(bf16[512,1024]{1,0:T(8,128)(2,1)} %get-tuple-element.163, ...), custom_call_target="tpu_custom_call" | custom-call | tf_op jit(solution)/shard_map/finish/pallas_call | solution.py:1439
  493.5 0.0 copy-done
  493.5 0.1 reshape.157
  493.6 0.5 fusion
  (3 shorter events, 0.0 us)
Async XLA Ops:
  482.1 11.4 %copy-start = (f32[8,1024]{1,0:T(8,128)S(1)}, f32[8,1024]{1,0:T(8,128)}, u32[]{:S(2)}) copy-start(f32[8,1024]{1,0:T(8,128)} %get-tuple-element.273) | copy-start | bytes 98308

commit v7 on v6

--- a/solution.py
+++ b/solution.py
@@ -23,7 +23,10 @@
     (("xz", 0, 1), ("mxz", 0, 1), ("mxz", 0, 1), ("xz", 0, 1)),
     (("mxz", 1, 1), ("mxz", 1, 1), ("xz", 1, 1), ("mxz", 1, 1)),
 )
-SCATTER_LATE = SCATTER_EARLY
+SCATTER_LATE = (
+    (("xz", 0, 1), ("mxz", 0, 1), ("mxz", 0, 1), ("zx", 0, 1)),
+    (("mxz", 1, 1), ("mxz", 1, 1), ("xz", 1, 1), ("mxz", 1, 1)),
+)
 SCATTER_ROUNDS = (3, 3, 2)
 LINK_RATE = 85e3
 CORE_RATE = 560e3
@@ -1365,7 +1368,7 @@
 
 
 def plan_gather(sizes, small, square, forward):
-    width, half = square[0].shape[1], forward[0].shape[1]
+    width, half = square[0].shape[1], forward[0].shape[1] // 2
     units = [(0, "zx", False, (0, small.shape[1]), 0, 1)]
     for group, (starts, routes, stride) in zip(((1, 2, 3), (4, 5, 6), (7,), (8,)), GATHER_SQUARE):
         pieces = cut(width, len(starts))
@@ -1379,8 +1382,9 @@
         for n, columns in enumerate(cut(half, min(len(starts), half // 128))):
             order = ("zxm", "zmx")[n % 2]
             units.append((9 + i, order, False, columns, starts[n], stride))
-    arrays = [small] + square + forward
-    return Gather(sizes, arrays, [(0, array.shape[1]) for array in arrays], units)
+    spans = [(0, array.shape[1]) for array in [small] + square]
+    spans += [(first, half) for first in (0, half) for _ in forward]
+    return Gather(sizes, [small] + square + forward * 2, spans, units)
 
 
 def forward_units(arrays, start, table):
@@ -1490,11 +1494,7 @@
         state_update_weight,
         token_output_weight,
     ]
-    forward = [
-        weight[:, first : first + half]
-        for first in (0, half)
-        for weight in (up_projection_weight, down_projection_weight)
-    ]
+    forward = [up_projection_weight, down_projection_weight]
     plan = plan_gather(sizes, small, square, forward)
     x, s0, cot = tokens[0], initial_state[0], output_cotangent[0]
 

time: 496 us -> 494 us (level)
  no operation moved by 1% of the time
where the time goes in v7:
time: 494 us; the launch traced here: 493 us
  Pallas kernels  488 us (99%)
    pallas_call x9, Pallas kernels, run_kernel(): pl.pallas_call(kernel, grid=grid, in_specs=list(in_specs) + exchange.spec...  477 us
    pallas_call x1, Pallas kernels, finish(): pl.pallas_call(functools.partial(finish_kernel, len(arrays), [len(g) for...  11.4 us

profile of v7, /device:TPU:0, one launch (start us, length us, event | category | flops | bytes accessed | tf_op | source)
XLA Modules:
  0.0 493.2 jit_solution(18345022621820551154)
XLA Ops:
  0.7 0.8 maximum_bitcast_fusion
  1.4 0.6 pad.4.refs_0_
  2.0 71.3 %gather_first.1 = (bf16[4,2,2,16,128]{4,3,2,1,0:T(8,128)(2,1)}, bf16[4,2,2,64,1024]{4,3,2,1,0:T(8,128)(2,1)}, bf16[4,2,2,64,1024]{4,3,2,1,0:T(8,128)(2,1)}, bf16...) custom-call(bf16[16,128]{1,0:T(8,128)(2,1)} %pad.4.refs_0_, ...), custom_call_target="tpu_custom_call" | custom-call | tf_op jit(solution)/shard_map/gather_first/pallas_call | solution.py:645
  73.3 0.9 copy.51
  74.2 0.1 reshape.159
  74.3 0.7 reshape.158.refs_2_.refs_1_
  75.6 45.8 %project_tokens.1 = (bf16[1024,1024]{1,0:T(8,128)(2,1)}, bf16[1024,1024]{1,0:T(8,128)(2,1)}, bf16[1024,1024]{1,0:T(8,128)(2,1)}, bf16[1024,1024]{1,0:T(8,128)(2,...) custom-call(s32[1]{0:T(128)S(6)} %copy.63.refs_0_, ...), custom_call_target="tpu_custom_call", output_to_operand_aliasing={{6}: (14, {}), {7}: (15, {}), {8}: (16, {}), {9}: (17, {})} | custom-call | tf_op jit(solution)/shard_map/project_tokens/pallas_call | solution.py:645
  121.4 32.2 %state_forward.1 = (bf16[1024,1024]{1,0:T(8,128)(2,1)}, bf16[1024,1024]{1,0:T(8,128)(2,1)}, bf16[1024,1024]{1,0:T(8,128)(2,1)}, bf16[1024,1024]{1,0:T(8,128)(2,1...) custom-call(s32[1]{0:T(128)S(6)} %copy.63.refs_0_, ...), custom_call_target="tpu_custom_call", output_to_operand_aliasing={{9}: (12, {}), {10}: (13, {}), {11}: (14, {})} | custom-call | tf_op jit(solution)/shard_map/state_forward/pallas_call | solution.py:645
  153.6 46.2 %token_forward.1 = (bf16[1024,1024]{1,0:T(8,128)(2,1)}, f32[4,2,1024]{2,1,0:T(2,128)}, f32[1024,1024]{1,0:T(8,128)}, bf16[1024,1024]{1,0:T(8,128)(2,1)}, bf16[10...) custom-call(s32[1]{0:T(128)S(6)} %copy.63.refs_0_, ...), custom_call_target="tpu_custom_call", output_to_operand_aliasing={{5}: (13, {}), {6}: (14, {})} | custom-call | tf_op jit(solution)/shard_map/token_forward/pallas_call | solution.py:645
  199.7 43.0 %feed_forward_first.1 = (f32[1024,1024]{1,0:T(8,128)}, f32[1024,1024]{1,0:T(8,128)}, bf16[2,1024,1024]{2,1,0:T(8,128)(2,1)}, bf16[2,1024,1024]{2,1,0:T(8,128)(2,...) custom-call(bf16[1024,1024]{1,0:T(8,128)(2,1)} %get-tuple-element.17, ...), custom_call_target="tpu_custom_call", output_to_operand_aliasing={{4}: (10, {}), {5}: (11, {})} | custom-call | tf_op jit(solution)/shard_map/feed_forward_first/pallas_call | solution.py:645
  242.7 46.5 %feed_forward_final.1 = (bf16[1024,1024]{1,0:T(8,128)(2,1)}, f32[1024,1024]{1,0:T(8,128)}, bf16[2,1024,1024]{2,1,0:T(8,128)(2,1)}, bf16[2,1024,1024]{2,1,0:T(8,1...) custom-call(bf16[1024,1024]{1,0:T(8,128)(2,1)} %get-tuple-element.17, ...), custom_call_target="tpu_custom_call" | custom-call | tf_op jit(solution)/shard_map/feed_forward_final/pallas_call | solution.py:645
  289.3 58.4 %token_backward.1 = (f32[1024,1024]{1,0:T(8,128)}, f32[1,1024]{1,0:T(1,128)}, bf16[1024,1024]{1,0:T(8,128)(2,1)}, f32[1024,1024]{1,0:T(8,128)}, f32[1024,1024]{1...) custom-call(s32[1]{0:T(128)S(6)} %copy.63.refs_0_, ...), custom_call_target="tpu_custom_call" | custom-call | tf_op jit(solution)/shard_map/token_backward/pallas_call | solution.py:645
  347.7 54.2 %state_backward.1 = (bf16[1024,1024]{1,0:T(8,128)(2,1)}, bf16[1024,1024]{1,0:T(8,128)(2,1)}, f32[512,1024]{1,0:T(8,128)}, f32[1,1024]{1,0:T(1,128)}, f32[1,1024]...) custom-call(s32[1]{0:T(128)S(6)} %copy.63.refs_0_, ...), custom_call_target="tpu_custom_call" | custom-call | tf_op jit(solution)/shard_map/state_backward/pallas_call | solution.py:645
  401.9 79.1 %token_grad.1 = (f32[1024,1024]{1,0:T(8,128)}, f32[1,1024]{1,0:T(1,128)}, f32[64,512]{1,0:T(8,128)}, f32[64,512]{1,0:T(8,128)}, f32[64,512]{1,0:T(8,128)}, /*ind...) custom-call(bf16[1024,1024]{1,0:T(8,128)(2,1)} %bitcast.52, ...), custom_call_target="tpu_custom_call" | custom-call | tf_op jit(solution)/shard_map/token_grad/pallas_call | solution.py:645
  481.0 0.0 copy-start
  481.0 11.4 %finish.1 = (bf16[512,1024]{1,0:T(8,128)(2,1)}, bf16[1024,1024]{1,0:T(8,128)(2,1)}, f32[512,1024]{1,0:T(8,128)}, f32[1024,1024]{1,0:T(8,128)}, f32[64,1024]{1,0:...) custom-call(bf16[512,1024]{1,0:T(8,128)(2,1)} %get-tuple-element.163, ...), custom_call_target="tpu_custom_call" | custom-call | tf_op jit(solution)/shard_map/finish/pallas_call | solution.py:1443
  492.4 0.0 copy-done
  492.4 0.1 reshape.157
  492.5 0.5 fusion
  (3 shorter events, 0.0 us)
Async XLA Ops:
  481.0 11.4 %copy-start = (f32[8,1024]{1,0:T(8,128)S(1)}, f32[8,1024]{1,0:T(8,128)}, u32[]{:S(2)}) copy-start(f32[8,1024]{1,0:T(8,128)} %get-tuple-element.273) | copy-start | bytes 98308
